TPU v7x, 32 devices: a whole 2x2x4 slice. The times are simulated.
32 devices in a mesh: gx: 4 (over x, core), gy: 2 (over y), gz: 4 (over z).
Axes of the slice: x: 2, y: 2, z: 4, core: 2. Of those that a mesh axis runs over, the one named last changes fastest.
Arguments:
- density: float32 [32, 256, 512], P('gz', 'gx', 'gy'), may hold values from 0.2 to 2
- bins: int32 [32, 256, 512], P('gz', 'gx', 'gy'), may hold values from 0 to 255
- colour_table: bfloat16 [3, 256], replicated, may hold values from 0.049804688 to 1
- opacity_table: bfloat16 [256], replicated, may hold values from 0.19921875 to 2.5
- order: int32 [4, 2, 4], P('gx', 'gy'), may hold values from 0 to 3, each once within a row
Outputs:
- image: float32 [4, 256, 512], P(None, ('gx', 'gz'), 'gy')
Inputs may be any that keep to these rules, and one draw needn't show every extreme that they name: For each column block and row block, order holds each brick rank 0 to 3 once.
All inputs are finite; a program needn't handle non-finite values.
Results may differ from a plain program's by a relative error of at most 0.0003.
Values sent between devices are 32-bit elements; how exact they have to be, the bound alone decides.
No kernel may reach another device: no remote copies, remote signals or barrier semaphores. Data moves between devices by JAX's collectives and lax.ppermute only.
A program may use at most 64 MiB of HBM per device.

v0:
```python
import jax
import jax.numpy as jnp
from jax import lax
from jax.sharding import PartitionSpec as P


def padded_2(x, sides, width):
    for axis, dim in sides:
        devices, length = (lax.axis_size(axis), x.shape[dim])
        up = [(i, (i + 1) % devices) for i in range(devices - 1)]
        down = [(j, i) for i, j in up]
        last = lax.slice_in_dim(x, length - width, length, axis=dim)
        first = lax.slice_in_dim(x, 0, width, axis=dim)
        before = lax.ppermute(last, axis, up)
        after = lax.ppermute(first, axis, down)
        x = jnp.concatenate([before, x, after], axis=dim)
    return x


def local(density, bins, colour_table, opacity_table, order):
    ranks = order.reshape(-1)
    depth_cells, column_cells, row_cells = density.shape
    bricks = lax.axis_size("gz")
    total_depth = depth_cells * bricks
    table_size = colour_table.shape[1]
    padded = padded_2(density, (("gx", 1), ("gy", 2), ("gz", 0)), 1)
    slope_depth = (padded[2:, 1:-1, 1:-1] - padded[:-2, 1:-1, 1:-1]) * 0.5
    slope_column = (padded[1:-1, 2:, 1:-1] - padded[1:-1, :-2, 1:-1]) * 0.5
    slope_row = (padded[1:-1, 1:-1, 2:] - padded[1:-1, 1:-1, :-2]) * 0.5
    facing = 0.64 * slope_depth + 0.48 * slope_column + 0.6 * slope_row
    length = jnp.sqrt(
        slope_depth * slope_depth + slope_column * slope_column + slope_row * slope_row + 1.0
    )
    shade = 0.25 + 0.75 * jnp.abs(facing) / length
    table_four = jnp.concatenate([colour_table, opacity_table[None, :]], axis=0)
    plane_cells = column_cells * row_cells
    flat_bins = bins.reshape(2 * depth_cells, plane_cells // 2)
    entries = jnp.arange(table_size, dtype=jnp.int32)

    def lookup(block):
        onehot = (block[None, :] == entries[:, None]).astype(jnp.bfloat16)
        return jnp.dot(table_four, onehot, preferred_element_type=jnp.float32)

    looked = lax.map(lookup, flat_bins)
    looked = jnp.transpose(looked, (1, 0, 2)).reshape(4, depth_cells, column_cells, row_cells)
    sigma = looked[3] * density * (3.0 / total_depth)
    alpha = 1.0 - jnp.exp(-sigma)
    excl = jnp.cumsum(sigma, axis=0) - sigma
    weight = jnp.exp(-excl) * alpha * shade
    colour_local = jnp.sum(weight[None] * looked[:3], axis=1)
    depth_local = jnp.sum(sigma, axis=0)
    tile_rows = column_cells // bricks
    all_depth = lax.all_gather(depth_local[None], "gz", axis=0, tiled=True)
    mine = ranks[lax.axis_index("gz")]
    earlier = (ranks < mine).astype(jnp.float32)
    prefix = jnp.sum(earlier[:, None, None] * all_depth, axis=0)
    attenuated = jnp.exp(-prefix)[None] * colour_local
    colour_tile = lax.psum_scatter(attenuated, "gz", scatter_dimension=1, tiled=True)
    total = jnp.sum(all_depth, axis=0)
    total_tile = lax.dynamic_slice_in_dim(total, lax.axis_index("gz") * tile_rows, tile_rows, 0)
    opacity_tile = 1.0 - jnp.exp(-total_tile)
    return jnp.concatenate([colour_tile, opacity_tile[None]], axis=0)


def solution(mesh):
    return jax.shard_map(
        local,
        mesh=mesh,
        in_specs=(P("gz", "gx", "gy"), P("gz", "gx", "gy"), P(), P(), P("gx", "gy", None)),
        out_specs=P(None, ("gx", "gz"), "gy"),
        check_vma=False,
    )
```

profile of v0, /device:TPU:0, one launch (start us, length us, event | category | flops | bytes accessed | tf_op | source)
XLA Modules:
  0.0 119.8 jit_solution(12077710382541079909)
XLA Ops:
  7.4 1.3 %collective-permute-start.1 = (f32[8,1,256]{2,1,0:T(1,128)S(1)}, f32[8,1,256]{2,1,0:T(1,128)S(1)}, u32[]{:S(2)}, u32[]{:S(2)}) collective-permute-start(f32[8,1,256]{2,1,0:T(1,128)S(1)} %get-tuple-element.58), channel_id=1, source_target_pairs={{8,0},{16,8},{24,16},{9,1},{17,9},{25,17},{10,2},{18,10},{26,18},{... | collective-permute-start | bytes 24584 | tf_op jit(solution)/shard_map/ppermute | solution.py:15
  8.7 3.0 %collective-permute-start = (f32[8,1,256]{2,1,0:T(1,128)S(1)}, f32[8,1,256]{2,1,0:T(1,128)S(1)}, u32[]{:S(2)}, u32[]{:S(2)}) collective-permute-start(f32[8,1,256]{2,1,0:T(1,128)S(1)} %get-tuple-element.57), channel_id=1, source_target_pairs={{0,8},{8,16},{16,24},{1,9},{9,17},{17,25},{2,10},{10,18},{18,26},{... | collective-permute-start | bytes 24584 | tf_op jit(solution)/shard_map/ppermute | solution.py:14
  14.3 32.4 %while.11 = (s32[]{:T(128)}, f32[16,4,8192]{2,1,0:T(4,128)}, s32[16,8192]{1,0:T(8,128)S(1)}, bf16[4,256]{1,0:T(4,128)(2,1)S(1)}, s32[]{:T(128)}) while((s32[]{:T(128)}, f32[16,4,8192]{2,1,0:T(4,128)}, s32[16,8192]{1,0:T(8,128)S(1)}, bf16[4,256]{1,0:T(4,128)(2,1)S(1)}, s32[]{:T(128)}) %tuple.25), condition=%wide.region_1.2_spmd.clone, body=%wide.region_0.1_spmd.clone.sunk | while | flops 18874368 | bytes 231501 | solution.py:44
  14.3 2.0 %fusion.21 = f32[16,4,8192]{2,1,0:T(4,128)} fusion(f32[16,4,8192]{2,1,0:T(4,128)} %get-tuple-element.90, s32[]{:T(128)S(6)} %copy.11, bf16[4,256]{1,0:T(4,128)(2,1)S(1)} %get-tuple-element.97, s32[8192]{0:T(1024)S(1)} %bitcast.25), kind=kOutput, calls=%fused_computation.2.clone.1 | convolution fusion | flops 18874368 | bytes 165892 | tf_op jit(solution)/shard_map/while/body/eval_jaxpr/dot_general | solution.py:42
  16.3 2.0 %fusion.21 = f32[16,4,8192]{2,1,0:T(4,128)} fusion(f32[16,4,8192]{2,1,0:T(4,128)} %get-tuple-element.90, s32[]{:T(128)S(6)} %copy.11, bf16[4,256]{1,0:T(4,128)(2,1)S(1)} %get-tuple-element.97, s32[8192]{0:T(1024)S(1)} %bitcast.25), kind=kOutput, calls=%fused_computation.2.clone.1 | convolution fusion | flops 18874368 | bytes 165892 | tf_op jit(solution)/shard_map/while/body/eval_jaxpr/dot_general | solution.py:42
  18.3 2.0 %fusion.21 = f32[16,4,8192]{2,1,0:T(4,128)} fusion(f32[16,4,8192]{2,1,0:T(4,128)} %get-tuple-element.90, s32[]{:T(128)S(6)} %copy.11, bf16[4,256]{1,0:T(4,128)(2,1)S(1)} %get-tuple-element.97, s32[8192]{0:T(1024)S(1)} %bitcast.25), kind=kOutput, calls=%fused_computation.2.clone.1 | convolution fusion | flops 18874368 | bytes 165892 | tf_op jit(solution)/shard_map/while/body/eval_jaxpr/dot_general | solution.py:42
  20.4 2.0 %fusion.21 = f32[16,4,8192]{2,1,0:T(4,128)} fusion(f32[16,4,8192]{2,1,0:T(4,128)} %get-tuple-element.90, s32[]{:T(128)S(6)} %copy.11, bf16[4,256]{1,0:T(4,128)(2,1)S(1)} %get-tuple-element.97, s32[8192]{0:T(1024)S(1)} %bitcast.25), kind=kOutput, calls=%fused_computation.2.clone.1 | convolution fusion | flops 18874368 | bytes 165892 | tf_op jit(solution)/shard_map/while/body/eval_jaxpr/dot_general | solution.py:42
  22.4 2.0 %fusion.21 = f32[16,4,8192]{2,1,0:T(4,128)} fusion(f32[16,4,8192]{2,1,0:T(4,128)} %get-tuple-element.90, s32[]{:T(128)S(6)} %copy.11, bf16[4,256]{1,0:T(4,128)(2,1)S(1)} %get-tuple-element.97, s32[8192]{0:T(1024)S(1)} %bitcast.25), kind=kOutput, calls=%fused_computation.2.clone.1 | convolution fusion | flops 18874368 | bytes 165892 | tf_op jit(solution)/shard_map/while/body/eval_jaxpr/dot_general | solution.py:42
  24.4 2.0 %fusion.21 = f32[16,4,8192]{2,1,0:T(4,128)} fusion(f32[16,4,8192]{2,1,0:T(4,128)} %get-tuple-element.90, s32[]{:T(128)S(6)} %copy.11, bf16[4,256]{1,0:T(4,128)(2,1)S(1)} %get-tuple-element.97, s32[8192]{0:T(1024)S(1)} %bitcast.25), kind=kOutput, calls=%fused_computation.2.clone.1 | convolution fusion | flops 18874368 | bytes 165892 | tf_op jit(solution)/shard_map/while/body/eval_jaxpr/dot_general | solution.py:42
  26.4 2.0 %fusion.21 = f32[16,4,8192]{2,1,0:T(4,128)} fusion(f32[16,4,8192]{2,1,0:T(4,128)} %get-tuple-element.90, s32[]{:T(128)S(6)} %copy.11, bf16[4,256]{1,0:T(4,128)(2,1)S(1)} %get-tuple-element.97, s32[8192]{0:T(1024)S(1)} %bitcast.25), kind=kOutput, calls=%fused_computation.2.clone.1 | convolution fusion | flops 18874368 | bytes 165892 | tf_op jit(solution)/shard_map/while/body/eval_jaxpr/dot_general | solution.py:42
  28.5 2.0 %fusion.21 = f32[16,4,8192]{2,1,0:T(4,128)} fusion(f32[16,4,8192]{2,1,0:T(4,128)} %get-tuple-element.90, s32[]{:T(128)S(6)} %copy.11, bf16[4,256]{1,0:T(4,128)(2,1)S(1)} %get-tuple-element.97, s32[8192]{0:T(1024)S(1)} %bitcast.25), kind=kOutput, calls=%fused_computation.2.clone.1 | convolution fusion | flops 18874368 | bytes 165892 | tf_op jit(solution)/shard_map/while/body/eval_jaxpr/dot_general | solution.py:42
  30.5 2.0 %fusion.21 = f32[16,4,8192]{2,1,0:T(4,128)} fusion(f32[16,4,8192]{2,1,0:T(4,128)} %get-tuple-element.90, s32[]{:T(128)S(6)} %copy.11, bf16[4,256]{1,0:T(4,128)(2,1)S(1)} %get-tuple-element.97, s32[8192]{0:T(1024)S(1)} %bitcast.25), kind=kOutput, calls=%fused_computation.2.clone.1 | convolution fusion | flops 18874368 | bytes 165892 | tf_op jit(solution)/shard_map/while/body/eval_jaxpr/dot_general | solution.py:42
  32.5 2.0 %fusion.21 = f32[16,4,8192]{2,1,0:T(4,128)} fusion(f32[16,4,8192]{2,1,0:T(4,128)} %get-tuple-element.90, s32[]{:T(128)S(6)} %copy.11, bf16[4,256]{1,0:T(4,128)(2,1)S(1)} %get-tuple-element.97, s32[8192]{0:T(1024)S(1)} %bitcast.25), kind=kOutput, calls=%fused_computation.2.clone.1 | convolution fusion | flops 18874368 | bytes 165892 | tf_op jit(solution)/shard_map/while/body/eval_jaxpr/dot_general | solution.py:42
  34.5 2.0 %fusion.21 = f32[16,4,8192]{2,1,0:T(4,128)} fusion(f32[16,4,8192]{2,1,0:T(4,128)} %get-tuple-element.90, s32[]{:T(128)S(6)} %copy.11, bf16[4,256]{1,0:T(4,128)(2,1)S(1)} %get-tuple-element.97, s32[8192]{0:T(1024)S(1)} %bitcast.25), kind=kOutput, calls=%fused_computation.2.clone.1 | convolution fusion | flops 18874368 | bytes 165892 | tf_op jit(solution)/shard_map/while/body/eval_jaxpr/dot_general | solution.py:42
  36.5 2.0 %fusion.21 = f32[16,4,8192]{2,1,0:T(4,128)} fusion(f32[16,4,8192]{2,1,0:T(4,128)} %get-tuple-element.90, s32[]{:T(128)S(6)} %copy.11, bf16[4,256]{1,0:T(4,128)(2,1)S(1)} %get-tuple-element.97, s32[8192]{0:T(1024)S(1)} %bitcast.25), kind=kOutput, calls=%fused_computation.2.clone.1 | convolution fusion | flops 18874368 | bytes 165892 | tf_op jit(solution)/shard_map/while/body/eval_jaxpr/dot_general | solution.py:42
  38.6 2.0 %fusion.21 = f32[16,4,8192]{2,1,0:T(4,128)} fusion(f32[16,4,8192]{2,1,0:T(4,128)} %get-tuple-element.90, s32[]{:T(128)S(6)} %copy.11, bf16[4,256]{1,0:T(4,128)(2,1)S(1)} %get-tuple-element.97, s32[8192]{0:T(1024)S(1)} %bitcast.25), kind=kOutput, calls=%fused_computation.2.clone.1 | convolution fusion | flops 18874368 | bytes 165892 | tf_op jit(solution)/shard_map/while/body/eval_jaxpr/dot_general | solution.py:42
  40.6 2.0 %fusion.21 = f32[16,4,8192]{2,1,0:T(4,128)} fusion(f32[16,4,8192]{2,1,0:T(4,128)} %get-tuple-element.90, s32[]{:T(128)S(6)} %copy.11, bf16[4,256]{1,0:T(4,128)(2,1)S(1)} %get-tuple-element.97, s32[8192]{0:T(1024)S(1)} %bitcast.25), kind=kOutput, calls=%fused_computation.2.clone.1 | convolution fusion | flops 18874368 | bytes 165892 | tf_op jit(solution)/shard_map/while/body/eval_jaxpr/dot_general | solution.py:42
  42.6 2.0 %fusion.21 = f32[16,4,8192]{2,1,0:T(4,128)} fusion(f32[16,4,8192]{2,1,0:T(4,128)} %get-tuple-element.90, s32[]{:T(128)S(6)} %copy.11, bf16[4,256]{1,0:T(4,128)(2,1)S(1)} %get-tuple-element.97, s32[8192]{0:T(1024)S(1)} %bitcast.25), kind=kOutput, calls=%fused_computation.2.clone.1 | convolution fusion | flops 18874368 | bytes 165892 | tf_op jit(solution)/shard_map/while/body/eval_jaxpr/dot_general | solution.py:42
  44.6 2.0 %fusion.21 = f32[16,4,8192]{2,1,0:T(4,128)} fusion(f32[16,4,8192]{2,1,0:T(4,128)} %get-tuple-element.90, s32[]{:T(128)S(6)} %copy.11, bf16[4,256]{1,0:T(4,128)(2,1)S(1)} %get-tuple-element.97, s32[8192]{0:T(1024)S(1)} %bitcast.25), kind=kOutput, calls=%fused_computation.2.clone.1 | convolution fusion | flops 18874368 | bytes 165892 | tf_op jit(solution)/shard_map/while/body/eval_jaxpr/dot_general | solution.py:42
  46.6 3.2 %slice_reduce_fusion = f32[16,8192]{1,0:T(8,128)S(1)} fusion(f32[4,16,8192]{2,0,1:T(4,128)} %bitcast.22), kind=kLoop, calls=%fused_computation.34 | loop fusion | bytes 1048576 | tf_op jit(solution)/shard_map/slice | solution.py:46
  51.2 16.0 %all-gather = f32[256,256]{1,0:T(8,128)S(1)} all-gather(f32[64,256]{1,0:T(8,128)S(1)} %fusion.11), channel_id=2, replica_groups=mesh['gx'=4,'gy'=2,'gz'=4] {'gz'}, dimensions={0}, use_global_device_ids=true | all-gather | bytes 327680 | tf_op jit(solution)/shard_map/all_gather | solution.py:53
  67.5 3.6 %collective-permute-start.2 = (f32[8,66,1]{2,1,0:T(8,128)S(1)}, f32[8,66,1]{2,1,0:T(8,128)S(1)}, u32[]{:S(2)}, u32[]{:S(2)}) collective-permute-start(f32[8,66,1]{2,1,0:T(8,128)S(1)} %get-tuple-element.56), channel_id=1, source_target_pairs={{0,4},{1,5},{2,6},{3,7},{8,12},{9,13},{10,14},{11,15},{16,20},{17,... | collective-permute-start | bytes 6344 | tf_op jit(solution)/shard_map/ppermute | solution.py:14
  71.0 1.3 %collective-permute-start.3 = (f32[8,66,1]{2,1,0:T(8,128)S(1)}, f32[8,66,1]{2,1,0:T(8,128)S(1)}, u32[]{:S(2)}, u32[]{:S(2)}) collective-permute-start(f32[8,66,1]{2,1,0:T(8,128)S(1)} %get-tuple-element.55), channel_id=1, source_target_pairs={{4,0},{5,1},{6,2},{7,3},{12,8},{13,9},{14,10},{15,11},{20,16},{21,... | collective-permute-start | bytes 6344 | tf_op jit(solution)/shard_map/ppermute | solution.py:15
  73.0 3.7 %collective-permute-done.2 = f32[8,66,1]{2,1,0:T(8,128)S(1)} collective-permute-done((f32[8,66,1]{2,1,0:T(8,128)S(1)}, f32[8,66,1]{2,1,0:T(8,128)S(1)}, u32[]{:S(2)}, u32[]{:S(2)}) %collective-permute-start.2) | collective-permute-done | bytes 2144 | tf_op jit(solution)/shard_map/ppermute | solution.py:14
  76.7 4.1 %collective-permute-done.3 = f32[8,66,1]{2,1,0:T(8,128)S(1)} collective-permute-done((f32[8,66,1]{2,1,0:T(8,128)S(1)}, f32[8,66,1]{2,1,0:T(8,128)S(1)}, u32[]{:S(2)}, u32[]{:S(2)}) %collective-permute-start.3) | collective-permute-done | bytes 2144 | tf_op jit(solution)/shard_map/ppermute | solution.py:15
  81.6 3.4 %collective-permute-start.5 = (f32[1,66,258]{2,1,0:T(8,128)}, f32[1,66,258]{2,1,0:T(8,128)S(1)}, u32[]{:S(2)}, u32[]{:S(2)}) collective-permute-start(f32[1,66,258]{2,1,0:T(8,128)} %get-tuple-element.54), channel_id=1, source_target_pairs={{0,1},{1,2},{2,3},{4,5},{5,6},{6,7},{8,9},{9,10},{10,11},{12,13},{... | collective-permute-start | bytes 204344 | tf_op jit(solution)/shard_map/ppermute | solution.py:14
  85.1 1.3 %collective-permute-start.4 = (f32[1,66,258]{2,1,0:T(8,128)}, f32[1,66,258]{2,1,0:T(8,128)S(1)}, u32[]{:S(2)}, u32[]{:S(2)}) collective-permute-start(f32[1,66,258]{2,1,0:T(8,128)} %get-tuple-element.53), channel_id=1, source_target_pairs={{1,0},{2,1},{3,2},{5,4},{6,5},{7,6},{9,8},{10,9},{11,10},{13,12},{... | collective-permute-start | bytes 204344 | tf_op jit(solution)/shard_map/ppermute | solution.py:15
  86.4 2.1 %copy.7 = f32[3,16,8192]{2,1,0:T(8,128)} copy(f32[3,16,8192]{2,0,1:T(4,128)S(1)} %bitcast.23) | data formatting | bytes 3145728 | tf_op jit(solution)/shard_map/slice | solution.py:50
  88.5 1.5 %slice.66 = f32[3,8,64,256]{3,2,1,0:T(8,128)S(1)} reshape(f32[3,16,8192]{2,1,0:T(8,128)} %copy.7) | data formatting | bytes 3145728 | tf_op jit(solution)/shard_map/slice | solution.py:50
  90.0 1.9 %collective-permute-done.4 = f32[1,66,258]{2,1,0:T(8,128)S(1)} collective-permute-done((f32[1,66,258]{2,1,0:T(8,128)}, f32[1,66,258]{2,1,0:T(8,128)S(1)}, u32[]{:S(2)}, u32[]{:S(2)}) %collective-permute-start.4) | collective-permute-done | bytes 68144 | tf_op jit(solution)/shard_map/ppermute | solution.py:15
  94.4 17.1 %reduce-scatter.2.cloned.1.call-done = f32[3,16,256]{2,1,0:T(8,128)} async-done(((f32[3,64,256]{2,1,0:T(8,128)}), f32[3,16,256]{2,1,0:T(8,128)}) %reduce-scatter.2.cloned.1.call-update) | async-done | bytes 49168 | tf_op jit(solution)/shard_map/reduce_scatter | solution.py:58
  111.5 1.4 %pad_maximum_fusion.24 = f32[4,16,256]{2,1,0:T(8,128)} fusion(f32[1,16,256]{2,1,0:T(8,128)S(1)} %subtract_bitcast_fusion, f32[3,16,256]{2,1,0:T(8,128)} %reduce-scatter.2.cloned.1.call-done), kind=kLoop, calls=%fused_computation.45 | loop fusion | flops 16384 | bytes 131072 | tf_op jit(solution)/shard_map/concatenate | solution.py:62
  (45 shorter events, 9.4 us)
Async XLA Ops:
  6.5 105.0 %reduce-scatter.2.cloned.1.call-start = ((), (), s32[]{:S(2)}) async-start(), calls=%async_computation.1 | async-start | bytes 245760 | tf_op jit(solution)/shard_map/reduce_scatter | solution.py:58
  7.4 59.8 %collective-permute-start.1 = (f32[8,1,256]{2,1,0:T(1,128)S(1)}, f32[8,1,256]{2,1,0:T(1,128)S(1)}, u32[]{:S(2)}, u32[]{:S(2)}) collective-permute-start(f32[8,1,256]{2,1,0:T(1,128)S(1)} %get-tuple-element.58), channel_id=1, source_target_pairs={{8,0},{16,8},{24,16},{9,1},{17,9},{25,17},{10,2},{18,10},{26,18},{... | collective-permute-start | bytes 24584 | tf_op jit(solution)/shard_map/ppermute | solution.py:15
  8.7 58.5 %collective-permute-start = (f32[8,1,256]{2,1,0:T(1,128)S(1)}, f32[8,1,256]{2,1,0:T(1,128)S(1)}, u32[]{:S(2)}, u32[]{:S(2)}) collective-permute-start(f32[8,1,256]{2,1,0:T(1,128)S(1)} %get-tuple-element.57), channel_id=1, source_target_pairs={{0,8},{8,16},{16,24},{1,9},{9,17},{17,25},{2,10},{10,18},{18,26},{... | collective-permute-start | bytes 24584 | tf_op jit(solution)/shard_map/ppermute | solution.py:14
  46.6 3.3 %copy-start = (f32[8,64,256]{2,1,0:T(8,128)S(1)}, f32[8,64,256]{2,1,0:T(8,128)}, u32[]{:S(2)}) copy-start(f32[8,64,256]{2,1,0:T(8,128)} %param.7) | copy-start | bytes 1572868
  46.6 3.3 %copy-start.2 = (s32[1,1,4]{2,1,0:T(1,128)S(1)}, s32[1,1,4]{2,1,0:T(1,128)}, u32[]{:S(2)}) copy-start(s32[1,1,4]{2,1,0:T(1,128)} %param.11) | copy-start | bytes 52
  67.2 19.2 %copy-start.1 = (f32[16,4,8192]{2,1,0:T(4,128)S(1)}, f32[16,4,8192]{2,1,0:T(4,128)}, u32[]{:S(2)}) copy-start(f32[16,4,8192]{2,1,0:T(4,128)} %get-tuple-element.32) | copy-start | bytes 6291460
  67.5 9.2 %collective-permute-start.2 = (f32[8,66,1]{2,1,0:T(8,128)S(1)}, f32[8,66,1]{2,1,0:T(8,128)S(1)}, u32[]{:S(2)}, u32[]{:S(2)}) collective-permute-start(f32[8,66,1]{2,1,0:T(8,128)S(1)} %get-tuple-element.56), channel_id=1, source_target_pairs={{0,4},{1,5},{2,6},{3,7},{8,12},{9,13},{10,14},{11,15},{16,20},{17,... | collective-permute-start | bytes 6344 | tf_op jit(solution)/shard_map/ppermute | solution.py:14
  71.0 9.8 %collective-permute-start.3 = (f32[8,66,1]{2,1,0:T(8,128)S(1)}, f32[8,66,1]{2,1,0:T(8,128)S(1)}, u32[]{:S(2)}, u32[]{:S(2)}) collective-permute-start(f32[8,66,1]{2,1,0:T(8,128)S(1)} %get-tuple-element.55), channel_id=1, source_target_pairs={{4,0},{5,1},{6,2},{7,3},{12,8},{13,9},{14,10},{15,11},{20,16},{21,... | collective-permute-start | bytes 6344 | tf_op jit(solution)/shard_map/ppermute | solution.py:15
  81.6 8.4 %collective-permute-start.5 = (f32[1,66,258]{2,1,0:T(8,128)}, f32[1,66,258]{2,1,0:T(8,128)S(1)}, u32[]{:S(2)}, u32[]{:S(2)}) collective-permute-start(f32[1,66,258]{2,1,0:T(8,128)} %get-tuple-element.54), channel_id=1, source_target_pairs={{0,1},{1,2},{2,3},{4,5},{5,6},{6,7},{8,9},{9,10},{10,11},{12,13},{... | collective-permute-start | bytes 204344 | tf_op jit(solution)/shard_map/ppermute | solution.py:14
  85.1 6.9 %collective-permute-start.4 = (f32[1,66,258]{2,1,0:T(8,128)}, f32[1,66,258]{2,1,0:T(8,128)S(1)}, u32[]{:S(2)}, u32[]{:S(2)}) collective-permute-start(f32[1,66,258]{2,1,0:T(8,128)} %get-tuple-element.53), channel_id=1, source_target_pairs={{1,0},{2,1},{3,2},{5,4},{6,5},{7,6},{9,8},{10,9},{11,10},{13,12},{... | collective-permute-start | bytes 204344 | tf_op jit(solution)/shard_map/ppermute | solution.py:15
Sparse Core Ops, SparseCore 0:
  93.8 17.6 reduce-scatter.1
where the time goes:
time: 120 us
  matrix products  31.9 us (27%)
  waiting for transfers between devices  26.9 us (22%)
  blocking collectives  16 us (13%)
  starting transfers between devices  13.9 us (12%)
  between operations  13.6 us (11%)
  local copies, waits for them, and re-layouts  10.7 us (9%)
  other arithmetic  6.88 us (6%)
    dot_general x16, matrix products, lookup(): return jnp.dot(table_four, onehot, preferred_element_type=jnp.float32)  31.9 us
    reduce_scatter x1, waiting for transfers between devices, local(): lax.psum_scatter(attenuated, 'gz', scatter_dimension=1, tiled=True)  17.1 us
    all_gather x1, blocking collectives, local(): all_depth = lax.all_gather(depth_local[None], 'gz', axis=0, tiled=True)  16 us
    ppermute x3, starting transfers between devices, padded_2(): before = lax.ppermute(last, axis, up)  10 us
    ppermute x3, waiting for transfers between devices, padded_2(): after = lax.ppermute(first, axis, down)  6.05 us
    ppermute x3, starting transfers between devices, padded_2(): after = lax.ppermute(first, axis, down)  3.88 us
    ppermute x3, waiting for transfers between devices, padded_2(): before = lax.ppermute(last, axis, up)  3.68 us
    slice x2, local copies, waits for them, and re-layouts, local(): colour_local = jnp.sum(weight[None] * looked[:3], axis=1)  3.58 us
  transfers between devices with their start and end apart: 7, of which 4 were waited for; matrix products, arithmetic and copies ran while one was open for 37% of the time, Pallas kernels for 0%

commit v1 on v0

v1 whole, which is shorter than its diff:
```python
import functools
import math

import jax
import jax.numpy as jnp
from jax import lax
from jax.experimental import pallas as pl
from jax.experimental.pallas import tpu as pltpu
from jax.sharding import PartitionSpec as P

LANES = 128
SUBLANES = 8
VMEM = pl.BlockSpec(memory_space=pltpu.VMEM)
SMEM = pl.BlockSpec(memory_space=pltpu.SMEM)


def faces_kernel(even_ref, density_ref, z_a, z_b, x_a, x_b, y_a, y_b):
    depth, columns, rows = density_ref.shape
    even_x, even_y, even_z = (even_ref[i] == 1 for i in range(3))
    first, last = density_ref[0], density_ref[depth - 1]
    z_a[...] = jnp.where(even_z, last, first)
    z_b[...] = jnp.where(even_z, first, last)
    for z in range(depth):
        first, last = density_ref[z, 0:1, :], density_ref[z, columns - 1 : columns, :]
        x_a[z : z + 1, :] = jnp.where(even_x, last, first)
        x_b[z : z + 1, :] = jnp.where(even_x, first, last)
    lane = lax.broadcasted_iota(jnp.int32, (columns, LANES), 1)
    first = last = jnp.zeros((columns, LANES), jnp.float32)
    for z in range(depth):
        first = jnp.where(lane == z, pltpu.roll(density_ref[z, :, :LANES], z, 1), first)
        last = jnp.where(lane == z, pltpu.roll(density_ref[z, :, rows - LANES :], z + 1, 1), last)
    y_a[...] = jnp.where(even_y, last, first)
    y_b[...] = jnp.where(even_y, first, last)


def look(words, index, upper):
    low, high = (
        jnp.take_along_axis(half, index, axis=1, mode="promise_in_bounds") for half in words
    )
    return jnp.where(upper, high, low)


def brick_kernel(
    step, parts, scalar_ref, density_ref, bins_ref, colour_ref, opacity_ref, *refs
):
    (z_a, z_b, x_a, x_b, y_a, y_b), outs = refs[:6], refs[6:]
    depth, columns, rows = density_ref.shape
    even_x, even_y, even_z = (scalar_ref[i] == 1 for i in range(3))
    tiles = columns // SUBLANES
    per_part = tiles // parts

    colours = (colour_ref[...].astype(jnp.float32) * 4096.0).astype(jnp.int32)
    opacity = (opacity_ref[...].astype(jnp.float32) * 1024.0).astype(jnp.int32)
    red_green = colours[0:1] * 8192 + colours[1:2]
    blue_opacity = colours[2:3] * 8192 + opacity

    def halves(word):
        return [
            jnp.broadcast_to(word[:, i : i + LANES], (SUBLANES, LANES)) for i in (0, LANES)
        ]

    red_green, blue_opacity = halves(red_green), halves(blue_opacity)
    sub = lax.broadcasted_iota(jnp.int32, (SUBLANES, rows), 0)
    lane = lax.broadcasted_iota(jnp.int32, (SUBLANES, rows), 1)

    def one_tile(i, carry):
        part, within = i // per_part, i % per_part
        tile = scalar_ref[3 + part] * per_part + within
        x0 = pl.multiple_of(tile * SUBLANES, SUBLANES)
        here = pl.ds(x0, SUBLANES)
        above = pl.ds(pl.multiple_of(jnp.maximum(x0 - SUBLANES, 0), SUBLANES), SUBLANES)
        below = pl.ds(
            pl.multiple_of(jnp.minimum(x0 + SUBLANES, columns - SUBLANES), SUBLANES), SUBLANES
        )
        top, bottom = tile == 0, tile == tiles - 1
        plane = jnp.where(even_z, z_b[here, :], z_a[here, :])
        after = jnp.where(even_z, z_a[here, :], z_b[here, :])
        y_before = jnp.where(even_y, y_b[here, :], y_a[here, :])
        y_after = jnp.where(even_y, y_a[here, :], y_b[here, :])
        current = density_ref[0, here, :]
        total = jnp.zeros((SUBLANES, rows), jnp.float32)
        seen = jnp.ones((SUBLANES, rows), jnp.float32)
        sums = [jnp.zeros((SUBLANES, rows), jnp.float32) for _ in range(3)]
        for z in range(depth):
            following = density_ref[z + 1, here, :] if z + 1 < depth else after
            slope_depth = following - plane
            x_before = jnp.where(even_x, x_b[z : z + 1, :], x_a[z : z + 1, :])
            x_after = jnp.where(even_x, x_a[z : z + 1, :], x_b[z : z + 1, :])
            before = jnp.where(top, x_before, density_ref[z, above, :])
            beyond = jnp.where(bottom, x_after, density_ref[z, below, :])
            slope_column = pltpu.roll(
                jnp.where(sub == 0, beyond, current), SUBLANES - 1, 0
            ) - pltpu.roll(jnp.where(sub == SUBLANES - 1, before, current), 1, 0)
            slope_row = jnp.where(
                lane == rows - 1, y_after[:, z : z + 1], pltpu.roll(current, rows - 1, 1)
            ) - jnp.where(lane == 0, y_before[:, z : z + 1], pltpu.roll(current, 1, 1))
            facing = 0.32 * slope_depth + 0.24 * slope_column + 0.3 * slope_row
            square = (
                slope_depth * slope_depth + slope_column * slope_column + slope_row * slope_row
            )
            shade = 0.25 + 0.75 * jnp.abs(facing) * lax.rsqrt(0.25 * square + 1.0)
            bins = bins_ref[z, here, :]
            looked = []
            for c in range(0, rows, LANES):
                b = bins[:, c : c + LANES]
                index, upper = b & (LANES - 1), b >= LANES
                looked.append((look(red_green, index, upper), look(blue_opacity, index, upper)))
            rg, bo = (jnp.concatenate([v[i] for v in looked], axis=1) for i in range(2))
            opacity = (bo & 8191).astype(jnp.float32)
            total = total + opacity * current * step
            left = jnp.exp2(-total)
            weight = (seen - left) * shade
            seen = left
            entries = (rg >> 13, rg & 8191, bo >> 13)
            sums = [s + weight * e.astype(jnp.float32) for s, e in zip(sums, entries)]
            plane, current = current, following
        values = [s * (1.0 / 4096.0) for s in sums] + [total]
        for p in range(parts):

            @pl.when(part == p)
            def _():
                at = pl.ds(pl.multiple_of(within * SUBLANES, SUBLANES), SUBLANES)
                for c, v in enumerate(values):
                    outs[p][c, at, :] = v

        return carry

    lax.fori_loop(0, tiles, one_tile, 0)


def compose_kernel(count, scalar_ref, *refs):
    if len(refs) == 2:
        bricks, out = [refs[0].at[i] for i in range(count)], refs[1]
    else:
        bricks, out = refs[:count], refs[count]
    depths = [b[3] for b in bricks]
    sums = [jnp.zeros_like(depths[0]) for _ in range(3)]
    total = jnp.zeros_like(depths[0])
    for i, brick in enumerate(bricks):
        prefix = jnp.zeros_like(total)
        for j in range(count):
            if j != i:
                prefix = prefix + jnp.where(scalar_ref[j] < scalar_ref[i], depths[j], 0.0)
        left = jnp.exp2(-prefix)
        sums = [s + left * brick[c] for c, s in enumerate(sums)]
        total = total + depths[i]
    for c in range(3):
        out[c] = sums[c]
    out[3] = 1.0 - jnp.exp2(-total)


def swap(to_first, to_second, axis):
    n = lax.axis_size(axis)
    got = []
    for value, start in ((to_first, 0), (to_second, 1)):
        pairs = [(i, i + 1) for i in range(start, n - 1, 2)]
        if pairs:
            got.append(lax.ppermute(value, axis, pairs + [(j, i) for i, j in pairs]))
        else:
            got.append(jnp.zeros_like(value))
    return got


def local(density, bins, colour_table, opacity_table, order):
    depth, columns, rows = density.shape
    bricks = lax.axis_size("gz")
    me = lax.axis_index("gz")
    f32 = lambda *shape: jax.ShapeDtypeStruct(shape, jnp.float32)
    even = jnp.stack([1 - lax.axis_index(a) % 2 for a in ("gx", "gy", "gz")])
    faces = pl.pallas_call(
        faces_kernel,
        out_shape=[f32(columns, rows)] * 2 + [f32(depth, rows)] * 2 + [f32(columns, LANES)] * 2,
        in_specs=[SMEM, VMEM],
        out_specs=[VMEM] * 6,
        name="faces",
    )(even, density)
    z_a, z_b = swap(faces[0], faces[1], "gz")
    x_a, x_b = swap(faces[2], faces[3], "gx")
    y_a, y_b = swap(faces[4], faces[5], "gy")

    tile_rows = columns // bricks
    direct = tile_rows % SUBLANES == 0 and bricks & (bricks - 1) == 0
    parts = bricks if direct else 1
    owners = jnp.arange(parts, dtype=jnp.int32)
    if direct:
        owners = owners ^ me
    step = 3.0 / (depth * bricks) * math.log2(math.e) / 1024.0
    sent = pl.pallas_call(
        functools.partial(brick_kernel, step, parts),
        out_shape=[f32(4, columns // parts, rows)] * parts,
        in_specs=[SMEM] + [VMEM] * 10,
        out_specs=[VMEM] * parts,
        name="brick",
    )(
        jnp.concatenate([even, owners]), density, bins, colour_table, opacity_table[None, :],
        z_a, z_b, x_a, x_b, y_a, y_b,
    )
    ranks = order.reshape(-1)
    if direct:
        received = [sent[0]] + [
            lax.ppermute(sent[k], "gz", [(i, i ^ k) for i in range(bricks)])
            for k in range(1, bricks)
        ]
        ranks = ranks[owners]
    else:
        cut = jnp.moveaxis(sent[0].reshape(4, bricks, tile_rows, rows), 1, 0)
        received = [lax.all_to_all(cut, "gz", 0, 0)]
    return pl.pallas_call(
        functools.partial(compose_kernel, bricks),
        out_shape=f32(4, tile_rows, rows),
        in_specs=[SMEM] + [VMEM] * len(received),
        out_specs=VMEM,
        name="compose",
    )(ranks, *received)


def solution(mesh):
    return jax.shard_map(
        local,
        mesh=mesh,
        in_specs=(P("gz", "gx", "gy"), P("gz", "gx", "gy"), P(), P(), P("gx", "gy", None)),
        out_specs=P(None, ("gx", "gz"), "gy"),
        check_vma=False,
    )
```

time: 120 us -> 31.5 us (0.26)
  matrix products: 31.9 us -> 0 us
  waiting for transfers between devices: 26.9 us -> 5.68 us
  blocking collectives: 16 us -> 0 us
  between operations: 13.6 us -> 0.1 us
  Pallas kernels: 0 us -> 7.83 us
  local copies, waits for them, and re-layouts: 10.7 us -> 3.09 us
  other arithmetic: 6.88 us -> 1.16 us
    dot_general x16 -> x0, matrix products: 31.9 us -> none  [lookup(): return jnp.dot(table_four, onehot, preferred_element_type=jnp.float32)]
    reduce_scatter x1 -> x0, waiting for transfers between devices: 17.1 us -> none  [local(): lax.psum_scatter(attenuated, 'gz', scatter_dimension=1, tiled=True)]
    all_gather x1 -> x0, blocking collectives: 16 us -> none  [local(): all_depth = lax.all_gather(depth_local[None], 'gz', axis=0, tiled=True)]
    pallas_call x0 -> x3, Pallas kernels: none -> 7.83 us  [the longest x1 4.36 us: local(): pl.pallas_call(functools.partial(brick_kernel, step, parts), out_shape=[f...]
    slice x5 -> x0, local copies, waits for them, and re-layouts: 7.76 us -> none  [the longest x2 3.58 us: local(): colour_local = jnp.sum(weight[None] * looked[:3], axis=1)]
    ppermute x6 -> x8, waiting for transfers between devices: 9.73 us -> 5.68 us  [the longest x3 4.73 us: local(): lax.ppermute(sent[k], 'gz', [(i, i ^ k) for i in range(bricks)])]
    concatenate x3 -> x1, other arithmetic: 2.18 us -> 0.56 us  [local(): jnp.concatenate([even, owners])]
    ppermute x6 -> x8, starting transfers between devices: 13.9 us -> 13.4 us  [the longest x3 7.49 us: local(): lax.ppermute(sent[k], 'gz', [(i, i ^ k) for i in range(bricks)])]
  transfers between devices with their start and end apart: 7 -> 8, of which waited for: 4 -> 3; matrix products, arithmetic and copies ran while one was open for 37% -> 7% of each run, Pallas kernels for 0% -> 0%
where the time goes in v1:
time: 31.5 us; the launch traced here: 31.3 us
  starting transfers between devices  13.4 us (43%)
  Pallas kernels  7.83 us (25%)
  waiting for transfers between devices  5.68 us (18%)
  local copies, waits for them, and re-layouts  3.09 us (10%)
  other arithmetic  1.16 us (4%)
    ppermute x3, starting transfers between devices, local(): lax.ppermute(sent[k], 'gz', [(i, i ^ k) for i in range(bricks)])  7.49 us
    ppermute x5, starting transfers between devices, swap(): got.append(lax.ppermute(value, axis, pairs + [(j, i) for i, j in pairs]))  5.91 us
    ppermute x3, waiting for transfers between devices, local(): lax.ppermute(sent[k], 'gz', [(i, i ^ k) for i in range(bricks)])  4.73 us
    pallas_call x1, Pallas kernels, local(): pl.pallas_call(functools.partial(brick_kernel, step, parts), out_shape=[f...  4.36 us
    pallas_call x1, Pallas kernels, local(): pl.pallas_call(faces_kernel, out_shape=[f32(columns, rows)] * 2 + [f32(de...  1.86 us
    pallas_call x1, Pallas kernels, local(): pl.pallas_call(functools.partial(compose_kernel, bricks), out_shape=f32(4...  1.62 us
    gather x1, local copies, waits for them, and re-layouts, local(): ranks = ranks[owners]  1.14 us
    ppermute x5, waiting for transfers between devices, swap(): got.append(lax.ppermute(value, axis, pairs + [(j, i) for i, j in pairs]))  0.95 us
  transfers between devices with their start and end apart: 8, of which 3 were waited for; matrix products, arithmetic and copies ran while one was open for 7% of the time, Pallas kernels for 0%

profile of v1, /device:TPU:0, one launch (start us, length us, event | category | flops | bytes accessed | tf_op | source)
XLA Modules:
  0.0 31.3 jit_solution(3963317868289181033)
XLA Ops:
  0.0 0.0 copy-start
  0.0 0.6 %pad_add_fusion.1.even_ref = s32[3]{0:T(128)} fusion(s32[1]{0:T(128)} %bitcast.4, s32[1]{0:T(128)} %bitcast.3, s32[1]{0:T(128)} %bitcast.2), kind=kLoop, calls=%fused_computation.5 | loop fusion | flops 6 | bytes 24 | tf_op jit(solution)/shard_map/stack | solution.py:169
  0.6 1.9 %faces.1 = (f32[64,256]{1,0:T(8,128)}, f32[64,256]{1,0:T(8,128)}, f32[8,256]{1,0:T(8,128)}, f32[8,256]{1,0:T(8,128)}, f32[64,128]{1,0:T(8,128)}, /*index=5*/f32[64,128]{1,0:T(8,128)}) custom-call(s32[3]{0:T(128)} %pad_add_fusion.1.even_ref, f32[8,64,256]{2,1,0:T(8,128)} %density_ref.3), custom_call_target="tpu_custom_call" | custom-call | tf_op jit(solution)/shard_map/faces/pallas_call | solution.py:170
  2.4 0.5 %collective-permute-start.2 = (f32[8,256]{1,0:T(8,128)}, f32[8,256]{1,0:T(8,128)S(1)}, u32[]{:S(2)}, u32[]{:S(2)}) collective-permute-start(f32[8,256]{1,0:T(8,128)} %get-tuple-element.16), channel_id=1, source_target_pairs={{0,8},{16,24},{8,0},{24,16},{1,9},{17,25},{9,1},{25,17},{2,10},{18... | collective-permute-start | bytes 24584 | tf_op jit(solution)/shard_map/ppermute | solution.py:158
  2.9 0.6 %collective-permute-start.3 = (f32[8,256]{1,0:T(8,128)}, f32[8,256]{1,0:T(8,128)S(1)}, u32[]{:S(2)}, u32[]{:S(2)}) collective-permute-start(f32[8,256]{1,0:T(8,128)} %get-tuple-element.17), channel_id=1, source_target_pairs={{8,16},{16,8},{9,17},{17,9},{10,18},{18,10},{11,19},{19,11},{12,20... | collective-permute-start | bytes 24584 | tf_op jit(solution)/shard_map/ppermute | solution.py:158
  3.6 2.6 %collective-permute-start.4 = (f32[64,128]{1,0:T(8,128)}, f32[64,128]{1,0:T(8,128)S(1)}, u32[]{:S(2)}, u32[]{:S(2)}) collective-permute-start(f32[64,128]{1,0:T(8,128)} %get-tuple-element.18), channel_id=1, source_target_pairs={{0,4},{4,0},{1,5},{5,1},{2,6},{6,2},{3,7},{7,3},{8,12},{12,8},{9,1... | collective-permute-start | bytes 98312 | tf_op jit(solution)/shard_map/ppermute | solution.py:158
  6.1 1.6 %collective-permute-start = (f32[64,256]{1,0:T(8,128)}, f32[64,256]{1,0:T(8,128)S(1)}, u32[]{:S(2)}, u32[]{:S(2)}) collective-permute-start(f32[64,256]{1,0:T(8,128)} %get-tuple-element.14), channel_id=1, source_target_pairs={{0,1},{2,3},{1,0},{3,2},{4,5},{6,7},{5,4},{7,6},{8,9},{10,11},{9,8... | collective-permute-start | bytes 196616 | tf_op jit(solution)/shard_map/ppermute | solution.py:158
  7.7 0.7 %collective-permute-start.1 = (f32[64,256]{1,0:T(8,128)}, f32[64,256]{1,0:T(8,128)S(1)}, u32[]{:S(2)}, u32[]{:S(2)}) collective-permute-start(f32[64,256]{1,0:T(8,128)} %get-tuple-element.15), channel_id=1, source_target_pairs={{1,2},{2,1},{5,6},{6,5},{9,10},{10,9},{13,14},{14,13},{17,18},{18,... | collective-permute-start | bytes 196616 | tf_op jit(solution)/shard_map/ppermute | solution.py:158
  8.4 0.0 copy-start.9
  8.4 0.6 %pad_add_fusion.scalar_ref = s32[7]{0:T(128)} fusion(s32[4]{0:T(128)S(1)} %iota_xor_fusion, s32[1]{0:T(128)} %bitcast.4, s32[1]{0:T(128)} %bitcast.3, s32[1]{0:T(128)} %bitcast.2), kind=kLoop, calls=%fused_computation.4 | loop fusion | flops 21 | bytes 56 | tf_op jit(solution)/shard_map/concatenate | solution.py:195
  9.0 0.1 copy-done.9
  9.1 0.6 %broadcast_in_dim.7.opacity_ref = bf16[1,256]{1,0:T(2,128)(2,1)} reshape(bf16[256]{0:T(256)(128)(2,1)S(1)} %copy-done.9) | data formatting | bytes 1024 | tf_op jit(solution)/shard_map/broadcast_in_dim | solution.py:195
  9.6 0.0 collective-permute-done.2.refs_2_
  9.6 0.0 collective-permute-done.3.refs_3_
  9.7 0.0 collective-permute-done.4.refs_4_
  9.7 0.0 copy-start.6
  9.7 0.9 %collective-permute-done.refs_0_ = f32[64,256]{1,0:T(8,128)S(1)} collective-permute-done((f32[64,256]{1,0:T(8,128)}, f32[64,256]{1,0:T(8,128)S(1)}, u32[]{:S(2)}, u32[]{:S(2)}) %collective-permute-start) | collective-permute-done | bytes 65568 | tf_op jit(solution)/shard_map/ppermute | solution.py:158
  10.6 0.0 collective-permute-done.1.refs_1_
  10.6 0.6 %broadcast_in_dim.8.refs_5_ = f32[64,128]{1,0:T(8,128)} broadcast(f32[]{:T(128)} %constant.38.clone.1), dimensions={} | broadcast | bytes 32772 | tf_op jit(solution)/shard_map/broadcast_in_dim | solution.py:160
  11.3 0.0 copy-done.7
  11.3 0.0 copy-done.5
  11.3 4.4 %brick.1 = (f32[4,16,256]{2,1,0:T(8,128)}, f32[4,16,256]{2,1,0:T(8,128)}, f32[4,16,256]{2,1,0:T(8,128)}, f32[4,16,256]{2,1,0:T(8,128)}) custom-call(s32[7]{0:T(128)} %pad_add_fusion.scalar_ref, f32[8,64,256]{2,1,0:T(8,128)} %density_ref.3, s32[8,64,256]{2,1,0:T(8,128)} %bins_ref.1, bf16[3,256]{1,0:T(4,128)(2,1)} %colour_ref.1, ...), custom_call_target="tpu_custom_call" | custom-call | tf_op jit(solution)/shard_map/brick/pallas_call | solution.py:188
  15.6 4.6 %collective-permute-start.5 = (f32[4,16,256]{2,1,0:T(8,128)}, f32[4,16,256]{2,1,0:T(8,128)S(1)}, u32[]{:S(2)}, u32[]{:S(2)}) collective-permute-start(f32[4,16,256]{2,1,0:T(8,128)} %get-tuple-element.20), channel_id=1, source_target_pairs={{0,1},{1,0},{2,3},{3,2},{4,5},{5,4},{6,7},{7,6},{8,9},{9,8},{10,11... | collective-permute-start | bytes 196616 | tf_op jit(solution)/shard_map/ppermute | solution.py:201
  20.2 1.5 %collective-permute-start.6 = (f32[4,16,256]{2,1,0:T(8,128)}, f32[4,16,256]{2,1,0:T(8,128)S(1)}, u32[]{:S(2)}, u32[]{:S(2)}) collective-permute-start(f32[4,16,256]{2,1,0:T(8,128)} %get-tuple-element.21), channel_id=1, source_target_pairs={{0,2},{1,3},{2,0},{3,1},{4,6},{5,7},{6,4},{7,5},{8,10},{9,11},{10,... | collective-permute-start | bytes 196616 | tf_op jit(solution)/shard_map/ppermute | solution.py:201
  21.7 1.4 %collective-permute-start.7 = (f32[4,16,256]{2,1,0:T(8,128)}, f32[4,16,256]{2,1,0:T(8,128)S(1)}, u32[]{:S(2)}, u32[]{:S(2)}) collective-permute-start(f32[4,16,256]{2,1,0:T(8,128)} %get-tuple-element.22), channel_id=1, source_target_pairs={{0,3},{1,2},{2,1},{3,0},{4,7},{5,6},{6,5},{7,4},{8,11},{9,10},{10,... | collective-permute-start | bytes 196616 | tf_op jit(solution)/shard_map/ppermute | solution.py:201
  23.1 0.0 copy-done
  23.1 1.1 %gather_fusion = s32[4]{0:T(128)} fusion(s32[4]{0:T(128)S(1)} %bitcast.6, s32[1024]{0:T(1024)S(1)} %pad_clamp_fusion), kind=kCustom, calls=%fused_computation | custom fusion | bytes 48 | tf_op jit(solution)/shard_map/gather | solution.py:204
  24.3 0.0 collective-permute-done.5.refs_1_
  24.3 1.8 %collective-permute-done.6.refs_2_ = f32[4,16,256]{2,1,0:T(8,128)S(1)} collective-permute-done((f32[4,16,256]{2,1,0:T(8,128)}, f32[4,16,256]{2,1,0:T(8,128)S(1)}, u32[]{:S(2)}, u32[]{:S(2)}) %collective-permute-start.6) | collective-permute-done | bytes 65568 | tf_op jit(solution)/shard_map/ppermute | solution.py:201
  26.1 2.9 %collective-permute-done.7.refs_3_ = f32[4,16,256]{2,1,0:T(8,128)S(1)} collective-permute-done((f32[4,16,256]{2,1,0:T(8,128)}, f32[4,16,256]{2,1,0:T(8,128)S(1)}, u32[]{:S(2)}, u32[]{:S(2)}) %collective-permute-start.7) | collective-permute-done | bytes 65568 | tf_op jit(solution)/shard_map/ppermute | solution.py:201
  29.0 0.6 %copy-done.3 = f32[4,16,256]{2,1,0:T(8,128)} copy-done((f32[4,16,256]{2,1,0:T(8,128)}, f32[4,16,256]{2,1,0:T(8,128)S(1)}, u32[]{:S(2)}) %copy-start.3) | copy-done | bytes 65560
  29.6 1.6 %compose.1 = f32[4,16,256]{2,1,0:T(8,128)} custom-call(s32[4]{0:T(128)} %gather_fusion, f32[4,16,256]{2,1,0:T(8,128)} %get-tuple-element.19.refs_0_, f32[4,16,256]{2,1,0:T(8,128)} %copy-done.1, f32[4,16,256]{2,1,0:T(8,128)} %copy-done.2, f32[4,16,256]{2,1,0:T(8,128)} %copy-done.3), custom_call_target="tpu_custom_call" | custom-call | tf_op jit(solution)/shard_map/compose/pallas_call | solution.py:208
  (15 shorter events, 0.0 us)
Async XLA Ops:
  0.0 23.1 %copy-start = (s32[1,1,4]{2,1,0:T(1,128)S(1)}, s32[1,1,4]{2,1,0:T(1,128)}, u32[]{:S(2)}) copy-start(s32[1,1,4]{2,1,0:T(1,128)} %param.9) | copy-start | bytes 52
  2.4 7.2 %collective-permute-start.2 = (f32[8,256]{1,0:T(8,128)}, f32[8,256]{1,0:T(8,128)S(1)}, u32[]{:S(2)}, u32[]{:S(2)}) collective-permute-start(f32[8,256]{1,0:T(8,128)} %get-tuple-element.16), channel_id=1, source_target_pairs={{0,8},{16,24},{8,0},{24,16},{1,9},{17,25},{9,1},{25,17},{2,10},{18... | collective-permute-start | bytes 24584 | tf_op jit(solution)/shard_map/ppermute | solution.py:158
  2.9 6.7 %collective-permute-start.3 = (f32[8,256]{1,0:T(8,128)}, f32[8,256]{1,0:T(8,128)S(1)}, u32[]{:S(2)}, u32[]{:S(2)}) collective-permute-start(f32[8,256]{1,0:T(8,128)} %get-tuple-element.17), channel_id=1, source_target_pairs={{8,16},{16,8},{9,17},{17,9},{10,18},{18,10},{11,19},{19,11},{12,20... | collective-permute-start | bytes 24584 | tf_op jit(solution)/shard_map/ppermute | solution.py:158
  3.6 6.1 %collective-permute-start.4 = (f32[64,128]{1,0:T(8,128)}, f32[64,128]{1,0:T(8,128)S(1)}, u32[]{:S(2)}, u32[]{:S(2)}) collective-permute-start(f32[64,128]{1,0:T(8,128)} %get-tuple-element.18), channel_id=1, source_target_pairs={{0,4},{4,0},{1,5},{5,1},{2,6},{6,2},{3,7},{7,3},{8,12},{12,8},{9,1... | collective-permute-start | bytes 98312 | tf_op jit(solution)/shard_map/ppermute | solution.py:158
  6.1 4.5 %collective-permute-start = (f32[64,256]{1,0:T(8,128)}, f32[64,256]{1,0:T(8,128)S(1)}, u32[]{:S(2)}, u32[]{:S(2)}) collective-permute-start(f32[64,256]{1,0:T(8,128)} %get-tuple-element.14), channel_id=1, source_target_pairs={{0,1},{2,3},{1,0},{3,2},{4,5},{6,7},{5,4},{7,6},{8,9},{10,11},{9,8... | collective-permute-start | bytes 196616 | tf_op jit(solution)/shard_map/ppermute | solution.py:158
  7.7 2.9 %collective-permute-start.1 = (f32[64,256]{1,0:T(8,128)}, f32[64,256]{1,0:T(8,128)S(1)}, u32[]{:S(2)}, u32[]{:S(2)}) collective-permute-start(f32[64,256]{1,0:T(8,128)} %get-tuple-element.15), channel_id=1, source_target_pairs={{1,2},{2,1},{5,6},{6,5},{9,10},{10,9},{13,14},{14,13},{17,18},{18,... | collective-permute-start | bytes 196616 | tf_op jit(solution)/shard_map/ppermute | solution.py:158
  8.4 0.7 %copy-start.9 = (bf16[256]{0:T(256)(128)(2,1)S(1)}, bf16[256]{0:T(256)(128)(2,1)}, u32[]{:S(2)}) copy-start(bf16[256]{0:T(256)(128)(2,1)} %param.8) | copy-start | bytes 1540
  9.6 1.6 %copy-start.7 = (f32[8,256]{1,0:T(8,128)}, f32[8,256]{1,0:T(8,128)S(1)}, u32[]{:S(2)}) copy-start(f32[8,256]{1,0:T(8,128)S(1)} %collective-permute-done.2.refs_2_) | copy-start | bytes 24580
  9.6 1.6 %copy-start.8 = (f32[8,256]{1,0:T(8,128)}, f32[8,256]{1,0:T(8,128)S(1)}, u32[]{:S(2)}) copy-start(f32[8,256]{1,0:T(8,128)S(1)} %collective-permute-done.3.refs_3_) | copy-start | bytes 24580
  9.7 1.6 %copy-start.6 = (f32[64,128]{1,0:T(8,128)}, f32[64,128]{1,0:T(8,128)S(1)}, u32[]{:S(2)}) copy-start(f32[64,128]{1,0:T(8,128)S(1)} %collective-permute-done.4.refs_4_) | copy-start | bytes 98308
  10.6 0.7 %copy-start.4 = (f32[64,256]{1,0:T(8,128)}, f32[64,256]{1,0:T(8,128)S(1)}, u32[]{:S(2)}) copy-start(f32[64,256]{1,0:T(8,128)S(1)} %collective-permute-done.refs_0_) | copy-start | bytes 196612
  10.6 0.7 %copy-start.5 = (f32[64,256]{1,0:T(8,128)}, f32[64,256]{1,0:T(8,128)S(1)}, u32[]{:S(2)}) copy-start(f32[64,256]{1,0:T(8,128)S(1)} %collective-permute-done.1.refs_1_) | copy-start | bytes 196612
  15.6 8.6 %collective-permute-start.5 = (f32[4,16,256]{2,1,0:T(8,128)}, f32[4,16,256]{2,1,0:T(8,128)S(1)}, u32[]{:S(2)}, u32[]{:S(2)}) collective-permute-start(f32[4,16,256]{2,1,0:T(8,128)} %get-tuple-element.20), channel_id=1, source_target_pairs={{0,1},{1,0},{2,3},{3,2},{4,5},{5,4},{6,7},{7,6},{8,9},{9,8},{10,11... | collective-permute-start | bytes 196616 | tf_op jit(solution)/shard_map/ppermute | solution.py:201
  20.2 5.9 %collective-permute-start.6 = (f32[4,16,256]{2,1,0:T(8,128)}, f32[4,16,256]{2,1,0:T(8,128)S(1)}, u32[]{:S(2)}, u32[]{:S(2)}) collective-permute-start(f32[4,16,256]{2,1,0:T(8,128)} %get-tuple-element.21), channel_id=1, source_target_pairs={{0,2},{1,3},{2,0},{3,1},{4,6},{5,7},{6,4},{7,5},{8,10},{9,11},{10,... | collective-permute-start | bytes 196616 | tf_op jit(solution)/shard_map/ppermute | solution.py:201
  21.7 7.3 %collective-permute-start.7 = (f32[4,16,256]{2,1,0:T(8,128)}, f32[4,16,256]{2,1,0:T(8,128)S(1)}, u32[]{:S(2)}, u32[]{:S(2)}) collective-permute-start(f32[4,16,256]{2,1,0:T(8,128)} %get-tuple-element.22), channel_id=1, source_target_pairs={{0,3},{1,2},{2,1},{3,0},{4,7},{5,6},{6,5},{7,4},{8,11},{9,10},{10,... | collective-permute-start | bytes 196616 | tf_op jit(solution)/shard_map/ppermute | solution.py:201
  24.3 4.7 %copy-start.1 = (f32[4,16,256]{2,1,0:T(8,128)}, f32[4,16,256]{2,1,0:T(8,128)S(1)}, u32[]{:S(2)}) copy-start(f32[4,16,256]{2,1,0:T(8,128)S(1)} %collective-permute-done.5.refs_1_) | copy-start | bytes 196612
  26.1 2.9 %copy-start.2 = (f32[4,16,256]{2,1,0:T(8,128)}, f32[4,16,256]{2,1,0:T(8,128)S(1)}, u32[]{:S(2)}) copy-start(f32[4,16,256]{2,1,0:T(8,128)S(1)} %collective-permute-done.6.refs_2_) | copy-start | bytes 196612
  29.0 0.6 %copy-start.3 = (f32[4,16,256]{2,1,0:T(8,128)}, f32[4,16,256]{2,1,0:T(8,128)S(1)}, u32[]{:S(2)}) copy-start(f32[4,16,256]{2,1,0:T(8,128)S(1)} %collective-permute-done.7.refs_3_) | copy-start | bytes 196612

commit v2 on v1

--- a/solution.py
+++ b/solution.py
@@ -14,9 +14,13 @@
 SMEM = pl.BlockSpec(memory_space=pltpu.SMEM)
 
 
-def faces_kernel(even_ref, density_ref, z_a, z_b, x_a, x_b, y_a, y_b):
+def evens():
+    return [lax.axis_index(axis) % 2 == 0 for axis in ("gx", "gy", "gz")]
+
+
+def faces_kernel(density_ref, z_a, z_b, x_a, x_b, y_a, *y_b):
     depth, columns, rows = density_ref.shape
-    even_x, even_y, even_z = (even_ref[i] == 1 for i in range(3))
+    even_x, even_y, even_z = evens()
     first, last = density_ref[0], density_ref[depth - 1]
     z_a[...] = jnp.where(even_z, last, first)
     z_b[...] = jnp.where(even_z, first, last)
@@ -30,7 +34,8 @@
         first = jnp.where(lane == z, pltpu.roll(density_ref[z, :, :LANES], z, 1), first)
         last = jnp.where(lane == z, pltpu.roll(density_ref[z, :, rows - LANES :], z + 1, 1), last)
     y_a[...] = jnp.where(even_y, last, first)
-    y_b[...] = jnp.where(even_y, first, last)
+    for y in y_b:
+        y[...] = jnp.where(even_y, first, last)
 
 
 def look(words, index, upper):
@@ -41,16 +46,22 @@
 
 
 def brick_kernel(
-    step, parts, scalar_ref, density_ref, bins_ref, colour_ref, opacity_ref, *refs
+    step, parts, density_ref, bins_ref, colour_ref, opacity_ref, *refs
 ):
-    (z_a, z_b, x_a, x_b, y_a, y_b), outs = refs[:6], refs[6:]
+    halos, outs = refs[:-parts], refs[-parts:]
+    z_a, z_b, x_a, x_b, y_a = halos[:5]
     depth, columns, rows = density_ref.shape
-    even_x, even_y, even_z = (scalar_ref[i] == 1 for i in range(3))
+    even_x, even_y, even_z = evens()
+    first_x, first_y, first_z = (lax.axis_index(a) == 0 for a in ("gx", "gy", "gz"))
+    last_x, last_y, last_z = (
+        lax.axis_index(a) == lax.axis_size(a) - 1 for a in ("gx", "gy", "gz")
+    )
+    me = lax.axis_index("gz")
     tiles = columns // SUBLANES
     per_part = tiles // parts
 
     colours = (colour_ref[...].astype(jnp.float32) * 4096.0).astype(jnp.int32)
-    opacity = (opacity_ref[...].astype(jnp.float32) * 1024.0).astype(jnp.int32)
+    opacity = (opacity_ref[...].reshape(1, -1).astype(jnp.float32) * 1024.0).astype(jnp.int32)
     red_green = colours[0:1] * 8192 + colours[1:2]
     blue_opacity = colours[2:3] * 8192 + opacity
 
@@ -65,7 +76,7 @@
 
     def one_tile(i, carry):
         part, within = i // per_part, i % per_part
-        tile = scalar_ref[3 + part] * per_part + within
+        tile = (part ^ me) * per_part + within if parts > 1 else i
         x0 = pl.multiple_of(tile * SUBLANES, SUBLANES)
         here = pl.ds(x0, SUBLANES)
         above = pl.ds(pl.multiple_of(jnp.maximum(x0 - SUBLANES, 0), SUBLANES), SUBLANES)
@@ -73,10 +84,13 @@
             pl.multiple_of(jnp.minimum(x0 + SUBLANES, columns - SUBLANES), SUBLANES), SUBLANES
         )
         top, bottom = tile == 0, tile == tiles - 1
-        plane = jnp.where(even_z, z_b[here, :], z_a[here, :])
-        after = jnp.where(even_z, z_a[here, :], z_b[here, :])
-        y_before = jnp.where(even_y, y_b[here, :], y_a[here, :])
-        y_after = jnp.where(even_y, y_a[here, :], y_b[here, :])
+        plane = jnp.where(first_z, 0.0, jnp.where(even_z, z_b[here, :], z_a[here, :]))
+        after = jnp.where(last_z, 0.0, jnp.where(even_z, z_a[here, :], z_b[here, :]))
+        y_before = y_after = y_a[here, :]
+        if len(halos) == 6:
+            y_before = jnp.where(even_y, halos[5][here, :], y_before)
+            y_after = jnp.where(even_y, y_after, halos[5][here, :])
+        y_before, y_after = jnp.where(first_y, 0.0, y_before), jnp.where(last_y, 0.0, y_after)
         current = density_ref[0, here, :]
         total = jnp.zeros((SUBLANES, rows), jnp.float32)
         seen = jnp.ones((SUBLANES, rows), jnp.float32)
@@ -85,7 +99,9 @@
             following = density_ref[z + 1, here, :] if z + 1 < depth else after
             slope_depth = following - plane
             x_before = jnp.where(even_x, x_b[z : z + 1, :], x_a[z : z + 1, :])
+            x_before = jnp.where(first_x, 0.0, x_before)
             x_after = jnp.where(even_x, x_a[z : z + 1, :], x_b[z : z + 1, :])
+            x_after = jnp.where(last_x, 0.0, x_after)
             before = jnp.where(top, x_before, density_ref[z, above, :])
             beyond = jnp.where(bottom, x_after, density_ref[z, below, :])
             slope_column = pltpu.roll(
@@ -128,11 +144,13 @@
     lax.fori_loop(0, tiles, one_tile, 0)
 
 
-def compose_kernel(count, scalar_ref, *refs):
+def compose_kernel(count, order_ref, *refs):
     if len(refs) == 2:
         bricks, out = [refs[0].at[i] for i in range(count)], refs[1]
+        ranks = [order_ref[0, 0, i] for i in range(count)]
     else:
         bricks, out = refs[:count], refs[count]
+        ranks = [order_ref[0, 0, lax.axis_index("gz") ^ i] for i in range(count)]
     depths = [b[3] for b in bricks]
     sums = [jnp.zeros_like(depths[0]) for _ in range(3)]
     total = jnp.zeros_like(depths[0])
@@ -140,7 +158,7 @@
         prefix = jnp.zeros_like(total)
         for j in range(count):
             if j != i:
-                prefix = prefix + jnp.where(scalar_ref[j] < scalar_ref[i], depths[j], 0.0)
+                prefix = prefix + jnp.where(ranks[j] < ranks[i], depths[j], 0.0)
         left = jnp.exp2(-prefix)
         sums = [s + left * brick[c] for c, s in enumerate(sums)]
         total = total + depths[i]
@@ -149,69 +167,72 @@
     out[3] = 1.0 - jnp.exp2(-total)
 
 
-def swap(to_first, to_second, axis):
-    n = lax.axis_size(axis)
+AXES = ("gx", "gy", "gz")
+
+
+def swap(values, axis):
+    sizes = [lax.axis_size(a) for a in AXES]
+    at, other = AXES.index(axis), 0 if axis != "gx" else 1
+    strides = [sizes[1] * sizes[2], sizes[2], 1]
     got = []
-    for value, start in ((to_first, 0), (to_second, 1)):
-        pairs = [(i, i + 1) for i in range(start, n - 1, 2)]
-        if pairs:
-            got.append(lax.ppermute(value, axis, pairs + [(j, i) for i, j in pairs]))
-        else:
-            got.append(jnp.zeros_like(value))
+    for start, value in enumerate(values):
+        pairs = []
+        for device in range(sizes[0] * sizes[1] * sizes[2]):
+            where = [device // s % n for s, n in zip(strides, sizes)]
+            partner = where[at] + 1 if where[at] % 2 == start else where[at] - 1
+            if 0 <= partner < sizes[at]:
+                where[at] = partner
+            else:
+                where[other] ^= 1
+            pairs.append((device, sum(w * s for w, s in zip(where, strides))))
+        got.append(lax.ppermute(value, AXES, pairs))
     return got
 
 
 def local(density, bins, colour_table, opacity_table, order):
     depth, columns, rows = density.shape
     bricks = lax.axis_size("gz")
-    me = lax.axis_index("gz")
-    f32 = lambda *shape: jax.ShapeDtypeStruct(shape, jnp.float32)
-    even = jnp.stack([1 - lax.axis_index(a) % 2 for a in ("gx", "gy", "gz")])
+    near = lambda *shape: pltpu.VMEM(shape, jnp.float32)
+    here = lambda *arrays: [pltpu.with_memory_space_constraint(a, pltpu.VMEM) for a in arrays]
+    density, bins = here(density, bins)
+    y_sides = 1 if lax.axis_size("gy") == 2 else 2
     faces = pl.pallas_call(
         faces_kernel,
-        out_shape=[f32(columns, rows)] * 2 + [f32(depth, rows)] * 2 + [f32(columns, LANES)] * 2,
-        in_specs=[SMEM, VMEM],
-        out_specs=[VMEM] * 6,
+        out_shape=[near(columns, rows)] * 2
+        + [near(depth, rows)] * 2
+        + [near(columns, LANES)] * y_sides,
+        in_specs=[VMEM],
+        out_specs=[VMEM] * (4 + y_sides),
         name="faces",
-    )(even, density)
-    z_a, z_b = swap(faces[0], faces[1], "gz")
-    x_a, x_b = swap(faces[2], faces[3], "gx")
-    y_a, y_b = swap(faces[4], faces[5], "gy")
+    )(density)
+    halos = swap(faces[0:2], "gz") + swap(faces[2:4], "gx") + swap(faces[4:], "gy")
 
     tile_rows = columns // bricks
     direct = tile_rows % SUBLANES == 0 and bricks & (bricks - 1) == 0
     parts = bricks if direct else 1
-    owners = jnp.arange(parts, dtype=jnp.int32)
-    if direct:
-        owners = owners ^ me
     step = 3.0 / (depth * bricks) * math.log2(math.e) / 1024.0
     sent = pl.pallas_call(
         functools.partial(brick_kernel, step, parts),
-        out_shape=[f32(4, columns // parts, rows)] * parts,
-        in_specs=[SMEM] + [VMEM] * 10,
+        out_shape=[near(4, columns // parts, rows)] * parts,
+        in_specs=[VMEM] * (4 + len(halos)),
         out_specs=[VMEM] * parts,
         name="brick",
-    )(
-        jnp.concatenate([even, owners]), density, bins, colour_table, opacity_table[None, :],
-        z_a, z_b, x_a, x_b, y_a, y_b,
-    )
-    ranks = order.reshape(-1)
+    )(density, bins, colour_table, opacity_table, *here(*halos))
     if direct:
         received = [sent[0]] + [
             lax.ppermute(sent[k], "gz", [(i, i ^ k) for i in range(bricks)])
             for k in range(1, bricks)
         ]
-        ranks = ranks[owners]
     else:
         cut = jnp.moveaxis(sent[0].reshape(4, bricks, tile_rows, rows), 1, 0)
         received = [lax.all_to_all(cut, "gz", 0, 0)]
     return pl.pallas_call(
         functools.partial(compose_kernel, bricks),
-        out_shape=f32(4, tile_rows, rows),
+        out_shape=jax.ShapeDtypeStruct((4, tile_rows, rows), jnp.float32),
         in_specs=[SMEM] + [VMEM] * len(received),
         out_specs=VMEM,
         name="compose",
-    )(ranks, *received)
+    )(order, *here(*received))
 
 
 def solution(mesh):

time: 31.5 us -> 24.9 us (0.79)
  Pallas kernels: 7.83 us -> 4.65 us
  starting transfers between devices: 13.4 us -> 10.8 us
  waiting for transfers between devices: 5.68 us -> 8.2 us
  local copies, waits for them, and re-layouts: 3.09 us -> 1.04 us
  other arithmetic: 1.16 us -> 0 us
    pallas_call x3, Pallas kernels: 7.83 us -> 4.65 us  [the longest x1 3.13 us: local(): pl.pallas_call(functools.partial(brick_kernel, step, parts), out_shape=[n...]
    ppermute x5, waiting for transfers between devices: 0.95 us -> 3.15 us  [swap(): got.append(lax.ppermute(value, AXES, pairs))]
    ppermute x3, starting transfers between devices: 7.49 us -> 5.43 us  [local(): lax.ppermute(sent[k], 'gz', [(i, i ^ k) for i in range(bricks)])]
    broadcast_in_dim x2 -> x0, local copies, waits for them, and re-layouts: 1.22 us -> none  [the longest x1 0.64 us: swap(): got.append(jnp.zeros_like(value))]
    gather x1 -> x0, local copies, waits for them, and re-layouts: 1.14 us -> none  [local(): ranks = ranks[owners]]
    another operation x1 -> x0, other arithmetic: 0.58 us -> none  [local(): even = jnp.stack([1 - lax.axis_index(a) % 2 for a in ('gx', 'gy', 'gz')])]
    ppermute x5, starting transfers between devices: 5.91 us -> 5.34 us  [swap(): got.append(lax.ppermute(value, AXES, pairs))]
    concatenate x1 -> x0, other arithmetic: 0.56 us -> none  [local(): jnp.concatenate([even, owners])]
  transfers between devices with their start and end apart: 8 -> 8, of which waited for: 3 -> 3; matrix products, arithmetic and copies ran while one was open for 7% -> 0% of each run, Pallas kernels for 0% -> 0%
where the time goes in v2:
time: 24.9 us; the launch traced here: 24.7 us
  starting transfers between devices  10.8 us (43%)
  waiting for transfers between devices  8.2 us (33%)
  Pallas kernels  4.65 us (19%)
  local copies, waits for them, and re-layouts  1.04 us (4%)
    ppermute x3, starting transfers between devices, local(): lax.ppermute(sent[k], 'gz', [(i, i ^ k) for i in range(bricks)])  5.43 us
    ppermute x5, starting transfers between devices, swap(): got.append(lax.ppermute(value, AXES, pairs))  5.34 us
    ppermute x3, waiting for transfers between devices, local(): lax.ppermute(sent[k], 'gz', [(i, i ^ k) for i in range(bricks)])  5.05 us
    ppermute x5, waiting for transfers between devices, swap(): got.append(lax.ppermute(value, AXES, pairs))  3.15 us
    pallas_call x1, Pallas kernels, local(): pl.pallas_call(functools.partial(brick_kernel, step, parts), out_shape=[n...  3.13 us
    pallas_call x1, Pallas kernels, local(): pl.pallas_call(functools.partial(compose_kernel, bricks), out_shape=jax.S...  1.34 us
    unnamed x4, local copies, waits for them, and re-layouts  1.04 us
  transfers between devices with their start and end apart: 8, of which 3 were waited for; matrix products, arithmetic and copies ran while one was open for 0% of the time, Pallas kernels for 0%

profile of v2, /device:TPU:0, one launch (start us, length us, event | category | flops | bytes accessed | tf_op | source)
XLA Modules:
  0.0 24.7 jit_solution(18295419150997288784)
XLA Ops:
  0.0 0.0 copy-start
  0.0 1.0 %copy-done = f32[8,64,256]{2,1,0:T(8,128)S(1)} copy-done((f32[8,64,256]{2,1,0:T(8,128)S(1)}, f32[8,64,256]{2,1,0:T(8,128)}, u32[]{:S(2)}) %copy-start) | copy-done | bytes 524312
  1.0 0.0 copy-start.1
  1.0 0.2 faces.1
  1.2 3.1 %collective-permute-start = (f32[64,256]{1,0:T(8,128)S(1)}, f32[64,256]{1,0:T(8,128)S(1)}, u32[]{:S(2)}, u32[]{:S(2)}) collective-permute-start(f32[64,256]{1,0:T(8,128)S(1)} %get-tuple-element.14), channel_id=1, source_target_pairs={{0,1},{1,0},{2,3},{3,2},{4,5},{5,4},{6,7},{7,6},{8,9},{9,8},{10,11... | collective-permute-start | bytes 196616 | tf_op jit(solution)/shard_map/ppermute | solution.py:188
  4.3 0.0 collective-permute-start.1
  4.3 1.5 %collective-permute-start.4 = (f32[64,128]{1,0:T(8,128)S(1)}, f32[64,128]{1,0:T(8,128)S(1)}, u32[]{:S(2)}, u32[]{:S(2)}) collective-permute-start(f32[64,128]{1,0:T(8,128)S(1)} %get-tuple-element.18), channel_id=1, source_target_pairs={{0,4},{1,5},{2,6},{3,7},{4,0},{5,1},{6,2},{7,3},{8,12},{9,13},{10,... | collective-permute-start | bytes 98312 | tf_op jit(solution)/shard_map/ppermute | solution.py:188
  5.9 0.2 collective-permute-start.2
  6.1 0.5 %collective-permute-start.3 = (f32[8,256]{1,0:T(8,128)S(1)}, f32[8,256]{1,0:T(8,128)S(1)}, u32[]{:S(2)}, u32[]{:S(2)}) collective-permute-start(f32[8,256]{1,0:T(8,128)S(1)} %get-tuple-element.17), channel_id=1, source_target_pairs={{0,4},{1,5},{2,6},{3,7},{4,0},{5,1},{6,2},{7,3},{8,16},{9,17},{10,... | collective-permute-start | bytes 24584 | tf_op jit(solution)/shard_map/ppermute | solution.py:188
  6.6 0.4 %collective-permute-done.2.refs_2_ = f32[8,256]{1,0:T(8,128)S(1)} collective-permute-done((f32[8,256]{1,0:T(8,128)S(1)}, f32[8,256]{1,0:T(8,128)S(1)}, u32[]{:S(2)}, u32[]{:S(2)}) %collective-permute-start.2) | collective-permute-done | bytes 8224 | tf_op jit(solution)/shard_map/ppermute | solution.py:188
  7.0 2.7 %collective-permute-done.3.refs_3_ = f32[8,256]{1,0:T(8,128)S(1)} collective-permute-done((f32[8,256]{1,0:T(8,128)S(1)}, f32[8,256]{1,0:T(8,128)S(1)}, u32[]{:S(2)}, u32[]{:S(2)}) %collective-permute-start.3) | collective-permute-done | bytes 8224 | tf_op jit(solution)/shard_map/ppermute | solution.py:188
  9.7 0.0 collective-permute-done.4.refs_4_
  9.7 0.0 collective-permute-done.refs_0_
  9.7 0.0 collective-permute-done.1.refs_1_
  9.7 0.0 copy-done.1
  9.8 3.1 %brick.1 = (f32[4,16,256]{2,1,0:T(8,128)S(1)}, f32[4,16,256]{2,1,0:T(8,128)S(1)}, f32[4,16,256]{2,1,0:T(8,128)S(1)}, f32[4,16,256]{2,1,0:T(8,128)S(1)}) custom-call(f32[8,64,256]{2,1,0:T(8,128)S(1)} %copy-done, s32[8,64,256]{2,1,0:T(8,128)S(1)} %copy-done.1, bf16[3,256]{1,0:T(4,128)(2,1)} %colour_ref.1, bf16[256]{0:T(256)(128)(2,1)} %opacity_ref.1, ...), custom_call_target="tpu_custom_call" | custom-call | tf_op jit(solution)/shard_map/brick/pallas_call | solution.py:214
  12.9 3.0 %collective-permute-start.5 = (f32[4,16,256]{2,1,0:T(8,128)S(1)}, f32[4,16,256]{2,1,0:T(8,128)S(1)}, u32[]{:S(2)}, u32[]{:S(2)}) collective-permute-start(f32[4,16,256]{2,1,0:T(8,128)S(1)} %get-tuple-element.20), channel_id=1, source_target_pairs={{0,1},{1,0},{2,3},{3,2},{4,5},{5,4},{6,7},{7,6},{8,9},{9,8},{10,11... | collective-permute-start | bytes 196616 | tf_op jit(solution)/shard_map/ppermute | solution.py:223
  15.9 0.1 collective-permute-start.6
  16.0 2.3 %collective-permute-start.7 = (f32[4,16,256]{2,1,0:T(8,128)S(1)}, f32[4,16,256]{2,1,0:T(8,128)S(1)}, u32[]{:S(2)}, u32[]{:S(2)}) collective-permute-start(f32[4,16,256]{2,1,0:T(8,128)S(1)} %get-tuple-element.22), channel_id=1, source_target_pairs={{0,3},{1,2},{2,1},{3,0},{4,7},{5,6},{6,5},{7,4},{8,11},{9,10},{10,... | collective-permute-start | bytes 196616 | tf_op jit(solution)/shard_map/ppermute | solution.py:223
  18.3 0.0 collective-permute-done.5.refs_1_
  18.3 5.0 %collective-permute-done.6.refs_2_ = f32[4,16,256]{2,1,0:T(8,128)S(1)} collective-permute-done((f32[4,16,256]{2,1,0:T(8,128)S(1)}, f32[4,16,256]{2,1,0:T(8,128)S(1)}, u32[]{:S(2)}, u32[]{:S(2)}) %collective-permute-start.6) | collective-permute-done | bytes 65568 | tf_op jit(solution)/shard_map/ppermute | solution.py:223
  23.4 0.0 collective-permute-done.7.refs_3_
  23.4 1.3 %compose.1 = f32[4,16,256]{2,1,0:T(8,128)} custom-call(s32[1,1,4]{2,1,0:T(1,128)} %order_ref.1, f32[4,16,256]{2,1,0:T(8,128)S(1)} %get-tuple-element.19.refs_0_, f32[4,16,256]{2,1,0:T(8,128)S(1)} %collective-permute-done.5.refs_1_, f32[4,16,256]{2,1,0:T(8,128)S(1)} %collective-permute-done.6.refs_2_, f32[4,16,256]{2,1,0:T(8,128)S(1)} %collective-permute-done.7.refs_3_), custom_call_target="tpu_custom_call" | custom-call | tf_op jit(solution)/shard_map/compose/pallas_call | solution.py:229
Async XLA Ops:
  0.0 1.0 %copy-start = (f32[8,64,256]{2,1,0:T(8,128)S(1)}, f32[8,64,256]{2,1,0:T(8,128)}, u32[]{:S(2)}) copy-start(f32[8,64,256]{2,1,0:T(8,128)} %density_ref.3) | copy-start | bytes 1572868
  1.0 8.7 %copy-start.1 = (s32[8,64,256]{2,1,0:T(8,128)S(1)}, s32[8,64,256]{2,1,0:T(8,128)}, u32[]{:S(2)}) copy-start(s32[8,64,256]{2,1,0:T(8,128)} %bins_ref.1) | copy-start | bytes 1572868
  1.2 8.5 %collective-permute-start = (f32[64,256]{1,0:T(8,128)S(1)}, f32[64,256]{1,0:T(8,128)S(1)}, u32[]{:S(2)}, u32[]{:S(2)}) collective-permute-start(f32[64,256]{1,0:T(8,128)S(1)} %get-tuple-element.14), channel_id=1, source_target_pairs={{0,1},{1,0},{2,3},{3,2},{4,5},{5,4},{6,7},{7,6},{8,9},{9,8},{10,11... | collective-permute-start | bytes 196616 | tf_op jit(solution)/shard_map/ppermute | solution.py:188
  4.3 5.4 %collective-permute-start.1 = (f32[64,256]{1,0:T(8,128)S(1)}, f32[64,256]{1,0:T(8,128)S(1)}, u32[]{:S(2)}, u32[]{:S(2)}) collective-permute-start(f32[64,256]{1,0:T(8,128)S(1)} %get-tuple-element.15), channel_id=1, source_target_pairs={{0,8},{1,2},{2,1},{3,11},{4,12},{5,6},{6,5},{7,15},{8,0},{9,10},{1... | collective-permute-start | bytes 196616 | tf_op jit(solution)/shard_map/ppermute | solution.py:188
  4.3 5.4 %collective-permute-start.4 = (f32[64,128]{1,0:T(8,128)S(1)}, f32[64,128]{1,0:T(8,128)S(1)}, u32[]{:S(2)}, u32[]{:S(2)}) collective-permute-start(f32[64,128]{1,0:T(8,128)S(1)} %get-tuple-element.18), channel_id=1, source_target_pairs={{0,4},{1,5},{2,6},{3,7},{4,0},{5,1},{6,2},{7,3},{8,12},{9,13},{10,... | collective-permute-start | bytes 98312 | tf_op jit(solution)/shard_map/ppermute | solution.py:188
  5.9 1.2 %collective-permute-start.2 = (f32[8,256]{1,0:T(8,128)S(1)}, f32[8,256]{1,0:T(8,128)S(1)}, u32[]{:S(2)}, u32[]{:S(2)}) collective-permute-start(f32[8,256]{1,0:T(8,128)S(1)} %get-tuple-element.16), channel_id=1, source_target_pairs={{0,8},{1,9},{2,10},{3,11},{4,12},{5,13},{6,14},{7,15},{8,0},{9,1},... | collective-permute-start | bytes 24584 | tf_op jit(solution)/shard_map/ppermute | solution.py:188
  6.1 3.7 %collective-permute-start.3 = (f32[8,256]{1,0:T(8,128)S(1)}, f32[8,256]{1,0:T(8,128)S(1)}, u32[]{:S(2)}, u32[]{:S(2)}) collective-permute-start(f32[8,256]{1,0:T(8,128)S(1)} %get-tuple-element.17), channel_id=1, source_target_pairs={{0,4},{1,5},{2,6},{3,7},{4,0},{5,1},{6,2},{7,3},{8,16},{9,17},{10,... | collective-permute-start | bytes 24584 | tf_op jit(solution)/shard_map/ppermute | solution.py:188
  12.9 5.4 %collective-permute-start.5 = (f32[4,16,256]{2,1,0:T(8,128)S(1)}, f32[4,16,256]{2,1,0:T(8,128)S(1)}, u32[]{:S(2)}, u32[]{:S(2)}) collective-permute-start(f32[4,16,256]{2,1,0:T(8,128)S(1)} %get-tuple-element.20), channel_id=1, source_target_pairs={{0,1},{1,0},{2,3},{3,2},{4,5},{5,4},{6,7},{7,6},{8,9},{9,8},{10,11... | collective-permute-start | bytes 196616 | tf_op jit(solution)/shard_map/ppermute | solution.py:223
  15.9 7.5 %collective-permute-start.6 = (f32[4,16,256]{2,1,0:T(8,128)S(1)}, f32[4,16,256]{2,1,0:T(8,128)S(1)}, u32[]{:S(2)}, u32[]{:S(2)}) collective-permute-start(f32[4,16,256]{2,1,0:T(8,128)S(1)} %get-tuple-element.21), channel_id=1, source_target_pairs={{0,2},{1,3},{2,0},{3,1},{4,6},{5,7},{6,4},{7,5},{8,10},{9,11},{10,... | collective-permute-start | bytes 196616 | tf_op jit(solution)/shard_map/ppermute | solution.py:223
  16.0 7.4 %collective-permute-start.7 = (f32[4,16,256]{2,1,0:T(8,128)S(1)}, f32[4,16,256]{2,1,0:T(8,128)S(1)}, u32[]{:S(2)}, u32[]{:S(2)}) collective-permute-start(f32[4,16,256]{2,1,0:T(8,128)S(1)} %get-tuple-element.22), channel_id=1, source_target_pairs={{0,3},{1,2},{2,1},{3,0},{4,7},{5,6},{6,5},{7,4},{8,11},{9,10},{10,... | collective-permute-start | bytes 196616 | tf_op jit(solution)/shard_map/ppermute | solution.py:223

commit v3 on v2

v3 whole, which is shorter than its diff:
```python
import functools
import math

import jax
import jax.numpy as jnp
from jax import lax
from jax.experimental import pallas as pl
from jax.experimental.pallas import tpu as pltpu
from jax.sharding import PartitionSpec as P

LANES = 128
SUBLANES = 8
AXES = ("gx", "gy", "gz")
SCOPED = 8 * 1024 * 1024
VMEM = pl.BlockSpec(memory_space=pltpu.VMEM)
HBM = pl.BlockSpec(memory_space=pltpu.HBM)


def evens():
    return [lax.axis_index(axis) % 2 == 0 for axis in AXES]


def ends():
    return [(lax.axis_index(a) == 0, lax.axis_index(a) == lax.axis_size(a) - 1) for a in AXES]


def load_kernel(density_hbm, order_hbm, colour_hbm, opacity_hbm, *refs):
    density_ref, order_ref, colour_ref, opacity_ref, z_a, z_b, x_a, x_b, y_a, *y_b, sems = refs
    depth, columns, rows = density_ref.shape
    even_x, even_y, even_z = evens()
    copies = [
        pltpu.make_async_copy(source, target, sems.at[i])
        for i, (source, target) in enumerate(
            (
                (density_hbm, density_ref),
                (order_hbm, order_ref),
                (colour_hbm, colour_ref),
                (opacity_hbm, opacity_ref),
            )
        )
    ]
    for copy in copies:
        copy.start()
    for copy in copies:
        copy.wait()
    first, last = density_ref[0], density_ref[depth - 1]
    z_a[...] = jnp.where(even_z, last, first)
    z_b[...] = jnp.where(even_z, first, last)
    for z in range(depth):
        first, last = density_ref[z, 0:1, :], density_ref[z, columns - 1 : columns, :]
        x_a[z : z + 1, :] = jnp.where(even_x, last, first)
        x_b[z : z + 1, :] = jnp.where(even_x, first, last)
    lane = lax.broadcasted_iota(jnp.int32, (columns, LANES), 1)
    first = last = jnp.zeros((columns, LANES), jnp.float32)
    for z in range(depth):
        first = jnp.where(lane == z, pltpu.roll(density_ref[z, :, :LANES], z, 1), first)
        last = jnp.where(lane == z, pltpu.roll(density_ref[z, :, rows - LANES :], z + 1, 1), last)
    y_a[...] = jnp.where(even_y, last, first)
    for y in y_b:
        y[...] = jnp.where(even_y, first, last)


def look(words, index, upper):
    low, high = (
        jnp.take_along_axis(half, index, axis=1, mode="promise_in_bounds") for half in words
    )
    return jnp.where(upper, high, low)


def pieces(rows):
    return [slice(c, c + LANES) for c in range(0, rows, LANES)]


def weights_kernel(
    step, relative, order_ref, density_ref, bins_hbm, colour_ref, opacity_ref,
    weighted, depth_out, earlier, bins_ref, sems,
):
    depth, columns, rows = density_ref.shape
    bricks = order_ref.shape[2]
    me = lax.axis_index("gz")

    def fetch(tile):
        at = pl.ds(pl.multiple_of(tile * SUBLANES, SUBLANES), SUBLANES)
        return pltpu.make_async_copy(
            bins_hbm.at[:, at, :], bins_ref.at[:, at, :], sems.at[tile]
        )

    lax.fori_loop(0, columns // SUBLANES, lambda i, c: fetch(i).start(), None)
    order = order_ref[0]
    brick = lax.broadcasted_iota(jnp.int32, order.shape, 1)
    ranks = [
        jnp.sum(jnp.where(brick == (i ^ me if relative else i), order, 0), axis=1, keepdims=True)
        for i in range(bricks)
    ]
    for i in range(bricks):
        for j in range(bricks):
            before = jnp.where(ranks[j] < ranks[i], 1.0, 0.0)
            earlier[i * bricks + j : i * bricks + j + 1, :] = jnp.broadcast_to(before, (1, rows))

    colours = (colour_ref[...].astype(jnp.float32) * 4096.0).astype(jnp.int32)
    opacity = (opacity_ref[...].reshape(1, -1).astype(jnp.float32) * 1024.0).astype(jnp.int32)
    red_green = colours[0:1] * 8192 + colours[1:2]
    blue_opacity = colours[2:3] * 8192 + opacity

    def halves(word):
        return [
            jnp.broadcast_to(word[:, i : i + LANES], (SUBLANES, LANES)) for i in (0, LANES)
        ]

    red_green, blue_opacity = halves(red_green), halves(blue_opacity)

    def one_tile(tile, carry):
        here = pl.ds(pl.multiple_of(tile * SUBLANES, SUBLANES), SUBLANES)
        fetch(tile).wait()
        for at in pieces(rows):
            total = jnp.zeros((SUBLANES, LANES), jnp.float32)
            seen = jnp.full((SUBLANES, LANES), 1.0 / 4096.0, jnp.float32)
            for z in range(depth):
                b = bins_ref[z, here, at]
                index, upper = b & (LANES - 1), b >= LANES
                rg, bo = look(red_green, index, upper), look(blue_opacity, index, upper)
                opacity = (bo & 8191).astype(jnp.float32)
                total = total + opacity * (density_ref[z, here, at] * step)
                left = jnp.exp2(-total) * (1.0 / 4096.0)
                weight = seen - left
                seen = left
                for c, entry in enumerate((rg >> 13, rg & 8191, bo >> 13)):
                    weighted[c, z, here, at] = weight * entry.astype(jnp.float32)
            depth_out[here, at] = total
        return carry

    lax.fori_loop(0, columns // SUBLANES, one_tile, 0)


def shade_kernel(part, density_ref, weighted, depth_in, *refs):
    halos, out, x_before, x_after = refs[:-3], refs[-3], refs[-2], refs[-1]
    z_a, z_b, x_a, x_b, y_a = halos[:5]
    depth, columns, rows = density_ref.shape
    even_x, even_y, even_z = evens()
    (first_x, last_x), (first_y, last_y), (first_z, last_z) = ends()
    tiles = out.shape[1] // SUBLANES
    start = 0 if part is None else (lax.axis_index("gz") ^ part) * tiles
    end = columns // SUBLANES - 1
    x_before[...] = jnp.where(first_x, 0.0, jnp.where(even_x, x_b[...], x_a[...]))
    x_after[...] = jnp.where(last_x, 0.0, jnp.where(even_x, x_a[...], x_b[...]))
    sub = lax.broadcasted_iota(jnp.int32, (SUBLANES, LANES), 0)
    lane = lax.broadcasted_iota(jnp.int32, (SUBLANES, LANES), 1)
    cuts = pieces(rows)

    def one_tile(i, carry):
        tile = start + i
        x0 = tile * SUBLANES
        here = pl.ds(pl.multiple_of(x0, SUBLANES), SUBLANES)
        above = pl.ds(pl.multiple_of(jnp.maximum(x0 - SUBLANES, 0), SUBLANES), SUBLANES)
        below = pl.ds(
            pl.multiple_of(jnp.minimum(x0 + SUBLANES, columns - SUBLANES), SUBLANES), SUBLANES
        )
        top, bottom = tile == 0, tile == end
        y_before = y_after = y_a[here, :]
        if len(halos) == 6:
            y_before = jnp.where(even_y, halos[5][here, :], y_before)
            y_after = jnp.where(even_y, y_after, halos[5][here, :])
        y_before, y_after = jnp.where(first_y, 0.0, y_before), jnp.where(last_y, 0.0, y_after)
        plane = [
            jnp.where(first_z, 0.0, jnp.where(even_z, z_b[here, at], z_a[here, at])) for at in cuts
        ]
        after = [
            jnp.where(last_z, 0.0, jnp.where(even_z, z_a[here, at], z_b[here, at])) for at in cuts
        ]
        current = [density_ref[0, here, at] for at in cuts]
        sums = [[jnp.zeros((SUBLANES, LANES), jnp.float32) for _ in range(3)] for _ in cuts]
        for z in range(depth):
            following = [density_ref[z + 1, here, at] for at in cuts] if z + 1 < depth else after
            right = [pltpu.roll(v, 1, 1) for v in current]
            left = [pltpu.roll(v, LANES - 1, 1) for v in current]
            for p, at in enumerate(cuts):
                low = right[p - 1] if p > 0 else y_before[:, z : z + 1]
                high = left[p + 1] if p + 1 < len(cuts) else y_after[:, z : z + 1]
                slope_row = jnp.where(lane == LANES - 1, high, left[p]) - jnp.where(
                    lane == 0, low, right[p]
                )
                before = jnp.where(top, x_before[z : z + 1, at], density_ref[z, above, at])
                beyond = jnp.where(bottom, x_after[z : z + 1, at], density_ref[z, below, at])
                slope_column = pltpu.roll(
                    jnp.where(sub == 0, beyond, current[p]), SUBLANES - 1, 0
                ) - pltpu.roll(jnp.where(sub == SUBLANES - 1, before, current[p]), 1, 0)
                slope_depth = following[p] - plane[p]
                facing = 0.48 * slope_depth + 0.36 * slope_column + 0.45 * slope_row
                square = (
                    slope_depth * slope_depth
                    + slope_column * slope_column
                    + (slope_row * slope_row + 4.0)
                )
                shade = 0.25 + jnp.abs(facing) * lax.rsqrt(square)
                for c in range(3):
                    sums[p][c] = sums[p][c] + shade * weighted[c, z, here, at]
            plane, current = current, following
        to = pl.ds(pl.multiple_of(i * SUBLANES, SUBLANES), SUBLANES)
        for p, at in enumerate(cuts):
            for c in range(3):
                out[c, to, at] = sums[p][c]
            out[3, to, at] = depth_in[here, at]
        return carry

    lax.fori_loop(0, tiles, one_tile, 0)


def compose_kernel(count, earlier, *refs):
    out = refs[-1]
    bricks = refs[count - 1 :: -1] if len(refs) > 2 else [refs[0].at[i] for i in range(count)]
    depths = [b[3] for b in bricks]
    sums = [jnp.zeros_like(depths[0]) for _ in range(3)]
    total = jnp.zeros_like(depths[0])
    for i, brick in enumerate(bricks):
        prefix = jnp.zeros_like(total)
        for j in range(count):
            if j != i:
                k = i * count + j
                prefix = prefix + earlier[k : k + 1, :] * depths[j]
        left = jnp.exp2(-prefix)
        sums = [s + left * brick[c] for c, s in enumerate(sums)]
        total = total + depths[i]
    for c in range(3):
        out[c] = sums[c]
    out[3] = 1.0 - jnp.exp2(-total)


def swap(values, axis):
    sizes = [lax.axis_size(a) for a in AXES]
    at, other = AXES.index(axis), 0 if axis != "gx" else 1
    strides = [sizes[1] * sizes[2], sizes[2], 1]
    got = []
    for start, value in enumerate(values):
        pairs = []
        for device in range(sizes[0] * sizes[1] * sizes[2]):
            where = [device // s % n for s, n in zip(strides, sizes)]
            partner = where[at] + 1 if where[at] % 2 == start else where[at] - 1
            if 0 <= partner < sizes[at]:
                where[at] = partner
            else:
                where[other] ^= 1
            pairs.append((device, sum(w * s for w, s in zip(where, strides))))
        got.append(lax.ppermute(value, AXES, pairs))
    return got


def local(density, bins, colour_table, opacity_table, order):
    depth, columns, rows = density.shape
    bricks = lax.axis_size("gz")
    near = lambda *shape: pltpu.VMEM(shape, jnp.float32)
    here = lambda *arrays: [pltpu.with_memory_space_constraint(a, pltpu.VMEM) for a in arrays]
    far = lambda *arrays: [pltpu.with_memory_space_constraint(a, pltpu.HBM) for a in arrays]
    call = lambda kernel, name, out_shape, in_specs, **more: pl.pallas_call(
        kernel, name=name, out_shape=out_shape, in_specs=in_specs,
        out_specs=jax.tree.map(lambda _: VMEM, out_shape),
        compiler_params=pltpu.CompilerParams(vmem_limit_bytes=SCOPED), **more,
    )
    y_sides = 1 if lax.axis_size("gy") == 2 else 2
    density, order, colour_table, opacity_table, *faces = call(
        load_kernel, "load",
        [pltpu.VMEM(a.shape, a.dtype) for a in (density, order, colour_table, opacity_table)]
        + [near(columns, rows)] * 2 + [near(depth, rows)] * 2 + [near(columns, LANES)] * y_sides,
        [HBM] * 4, scratch_shapes=[pltpu.SemaphoreType.DMA((4,))],
    )(*far(density, order, colour_table, opacity_table))
    density, order, colour_table, opacity_table, *faces = here(
        density, order, colour_table, opacity_table, *faces
    )
    halos = swap(faces[:2], "gz") + swap(faces[2:4], "gx") + swap(faces[4:], "gy")

    tile_rows = columns // bricks
    direct = tile_rows % SUBLANES == 0 and bricks & (bricks - 1) == 0
    step = 3.0 / (depth * bricks) * math.log2(math.e) / 1024.0
    weighted, depths, earlier = call(
        functools.partial(weights_kernel, step, direct), "weights",
        [near(3, depth, columns, rows), near(columns, rows), near(bricks * bricks, rows)],
        [VMEM] * 2 + [HBM] + [VMEM] * 2,
        scratch_shapes=[
            pltpu.VMEM(bins.shape, bins.dtype),
            pltpu.SemaphoreType.DMA((columns // SUBLANES,)),
        ],
    )(order, density, *far(bins), colour_table, opacity_table)
    weighted, depths, earlier = here(weighted, depths, earlier)
    shade = lambda part, tile: call(
        functools.partial(shade_kernel, part), "shade",
        near(4, tile, rows), [VMEM] * (3 + len(halos)),
        scratch_shapes=[pltpu.VMEM((depth, rows), jnp.float32)] * 2,
    )(density, weighted, depths, *here(*halos))
    if direct:
        received = []
        for k in range(bricks - 1, 0, -1):
            pairs = [(i, i ^ k) for i in range(bricks)]
            received.append(lax.ppermute(shade(k, tile_rows), "gz", pairs))
        received.append(shade(0, tile_rows))
    else:
        whole = shade(None, columns)
        cut = jnp.moveaxis(whole.reshape(4, bricks, tile_rows, rows), 1, 0)
        received = [lax.all_to_all(cut, "gz", 0, 0)]
    return call(
        functools.partial(compose_kernel, bricks), "compose",
        jax.ShapeDtypeStruct((4, tile_rows, rows), jnp.float32), [VMEM] * (1 + len(received)),
    )(earlier, *here(*received))


def solution(mesh):
    return jax.shard_map(
        local,
        mesh=mesh,
        in_specs=(P("gz", "gx", "gy"), P("gz", "gx", "gy"), P(), P(), P("gx", "gy", None)),
        out_specs=P(None, ("gx", "gz"), "gy"),
        check_vma=False,
    )
```

time: 24.9 us -> 21.9 us (0.88)
  waiting for transfers between devices: 8.2 us -> 5.89 us
  Pallas kernels: 4.65 us -> 5.86 us
  local copies, waits for them, and re-layouts: 1.04 us -> 0 us
  starting transfers between devices: 10.8 us -> 9.93 us
    ppermute x5, waiting for transfers between devices: 3.15 us -> 0.59 us  [swap(): got.append(lax.ppermute(value, AXES, pairs))]
    pallas_call x3 -> x7, Pallas kernels: 4.65 us -> 5.86 us  [the longest x1 2.55 us: local(): call(functools.partial(weights_kernel, step, direct), 'weights', [near(3,...]
    unnamed x4 -> x0, local copies, waits for them, and re-layouts: 1.04 us -> none
    ppermute x3, starting transfers between devices: 5.43 us -> 4.59 us  [local(): received.append(lax.ppermute(shade(k, tile_rows), 'gz', pairs))]
    ppermute x3, waiting for transfers between devices: 5.05 us -> 5.3 us  [local(): received.append(lax.ppermute(shade(k, tile_rows), 'gz', pairs))]
  transfers between devices with their start and end apart: 8 -> 8, of which waited for: 3 -> 4; matrix products, arithmetic and copies ran while one was open for 0% -> 0% of each run, Pallas kernels for 0% -> 16%
where the time goes in v3:
time: 21.9 us; the launch traced here: 21.7 us
  starting transfers between devices  9.93 us (45%)
  waiting for transfers between devices  5.89 us (27%)
  Pallas kernels  5.86 us (27%)
    ppermute x5, starting transfers between devices, swap(): got.append(lax.ppermute(value, AXES, pairs))  5.34 us
    ppermute x3, waiting for transfers between devices, local(): received.append(lax.ppermute(shade(k, tile_rows), 'gz', pairs))  5.3 us
    ppermute x3, starting transfers between devices, local(): received.append(lax.ppermute(shade(k, tile_rows), 'gz', pairs))  4.59 us
    pallas_call x1, Pallas kernels, local(): call(functools.partial(weights_kernel, step, direct), 'weights', [near(3,...  2.55 us
    pallas_call x4, Pallas kernels, local(): call(functools.partial(shade_kernel, part), 'shade', near(4, tile, rows),...  1.37 us
    pallas_call x1, Pallas kernels, local(): call(load_kernel, 'load', [pltpu.VMEM(a.shape, a.dtype) for a in (density...  1.28 us
    pallas_call x1, Pallas kernels, local(): call(functools.partial(compose_kernel, bricks), 'compose', jax.ShapeDtype...  0.67 us
    ppermute x5, waiting for transfers between devices, swap(): got.append(lax.ppermute(value, AXES, pairs))  0.59 us
  transfers between devices with their start and end apart: 8, of which 4 were waited for; matrix products, arithmetic and copies ran while one was open for 0% of the time, Pallas kernels for 16%

profile of v3, /device:TPU:0, one launch (start us, length us, event | category | flops | bytes accessed | tf_op | source)
XLA Modules:
  0.0 21.7 jit_solution(13539298614044230644)
XLA Ops:
  0.0 1.3 %load.1 = (f32[8,64,256]{2,1,0:T(8,128)S(1)}, s32[1,1,4]{2,1,0:T(1,128)S(1)}, bf16[3,256]{1,0:T(4,128)(2,1)S(1)}, bf16[256]{0:T(256)(128)(2,1)S(1)}, f32[64,256]...) custom-call(f32[8,64,256]{2,1,0:T(8,128)} %density_hbm.1, ...), custom_call_target="tpu_custom_call" | custom-call | tf_op jit(solution)/shard_map/load/pallas_call | solution.py:259
  1.3 3.1 %collective-permute-start = (f32[64,256]{1,0:T(8,128)S(1)}, f32[64,256]{1,0:T(8,128)S(1)}, u32[]{:S(2)}, u32[]{:S(2)}) collective-permute-start(f32[64,256]{1,0:T(8,128)S(1)} %get-tuple-element.24), channel_id=1, source_target_pairs={{0,1},{1,0},{2,3},{3,2},{4,5},{5,4},{6,7},{7,6},{8,9},{9,8},{10,11... | collective-permute-start | bytes 196616 | tf_op jit(solution)/shard_map/ppermute | solution.py:243
  4.4 0.0 collective-permute-start.1
  4.4 1.5 %collective-permute-start.4 = (f32[64,128]{1,0:T(8,128)S(1)}, f32[64,128]{1,0:T(8,128)S(1)}, u32[]{:S(2)}, u32[]{:S(2)}) collective-permute-start(f32[64,128]{1,0:T(8,128)S(1)} %get-tuple-element.28), channel_id=1, source_target_pairs={{0,4},{1,5},{2,6},{3,7},{4,0},{5,1},{6,2},{7,3},{8,12},{9,13},{10,... | collective-permute-start | bytes 98312 | tf_op jit(solution)/shard_map/ppermute | solution.py:243
  5.9 0.2 %collective-permute-start.2 = (f32[8,256]{1,0:T(8,128)S(1)}, f32[8,256]{1,0:T(8,128)S(1)}, u32[]{:S(2)}, u32[]{:S(2)}) collective-permute-start(f32[8,256]{1,0:T(8,128)S(1)} %get-tuple-element.26), channel_id=1, source_target_pairs={{0,8},{1,9},{2,10},{3,11},{4,12},{5,13},{6,14},{7,15},{8,0},{9,1},... | collective-permute-start | bytes 24584 | tf_op jit(solution)/shard_map/ppermute | solution.py:243
  6.1 0.5 %collective-permute-start.3 = (f32[8,256]{1,0:T(8,128)S(1)}, f32[8,256]{1,0:T(8,128)S(1)}, u32[]{:S(2)}, u32[]{:S(2)}) collective-permute-start(f32[8,256]{1,0:T(8,128)S(1)} %get-tuple-element.27), channel_id=1, source_target_pairs={{0,4},{1,5},{2,6},{3,7},{4,0},{5,1},{6,2},{7,3},{8,16},{9,17},{10,... | collective-permute-start | bytes 24584 | tf_op jit(solution)/shard_map/ppermute | solution.py:243
  6.6 2.5 %weights.1 = (f32[3,8,64,256]{3,2,1,0:T(8,128)S(1)}, f32[64,256]{1,0:T(8,128)S(1)}, f32[16,256]{1,0:T(8,128)S(1)}) custom-call(s32[1,1,4]{2,1,0:T(1,128)S(1)} %get-tuple-element.17.order_ref, f32[8,64,256]{2,1,0:T(8,128)S(1)} %get-tuple-element.18.density_ref, s32[8,64,256]{2,1,0:T(8,128)} %bins_hbm.1, bf16[3,256]{1,0:T(4,128)(2,1)S(1)} %get-tuple-element.19.colour_ref, ...), custom_call_target="tpu_custom_call" | custom-call | tf_op jit(solution)/shard_map/weights/pallas_call | solution.py:273
  9.2 0.0 collective-permute-done.2.refs_2_
  9.2 0.6 %collective-permute-done.3.refs_3_ = f32[8,256]{1,0:T(8,128)S(1)} collective-permute-done((f32[8,256]{1,0:T(8,128)S(1)}, f32[8,256]{1,0:T(8,128)S(1)}, u32[]{:S(2)}, u32[]{:S(2)}) %collective-permute-start.3) | collective-permute-done | bytes 8224 | tf_op jit(solution)/shard_map/ppermute | solution.py:243
  9.8 0.0 collective-permute-done.4.refs_4_
  9.8 0.0 collective-permute-done.refs_0_
  9.8 0.0 collective-permute-done.1.refs_1_
  9.8 0.4 %shade.4 = f32[4,16,256]{2,1,0:T(8,128)S(1)} custom-call(f32[8,64,256]{2,1,0:T(8,128)S(1)} %get-tuple-element.18.density_ref, f32[3,8,64,256]{3,2,1,0:T(8,128)S(1)} %get-tuple-element.22.weighted, f32[64,256]{1,0:T(8,128)S(1)} %get-tuple-element.23.depth_in, f32[64,256]{1,0:T(8,128)S(1)} %collective-permute-done.refs_0_, ...), custom_call_target="tpu_custom_call" | custom-call | tf_op jit(solution)/shard_map/shade/pallas_call | solution.py:283
  10.1 2.5 %collective-permute-start.5 = (f32[4,16,256]{2,1,0:T(8,128)S(1)}, f32[4,16,256]{2,1,0:T(8,128)S(1)}, u32[]{:S(2)}, u32[]{:S(2)}) collective-permute-start(f32[4,16,256]{2,1,0:T(8,128)S(1)} %shade.4), channel_id=1, source_target_pairs={{0,3},{1,2},{2,1},{3,0},{4,7},{5,6},{6,5},{7,4},{8,11},{9,10},{10,... | collective-permute-start | bytes 196616 | tf_op jit(solution)/shard_map/ppermute | solution.py:292
  12.7 0.3 %shade.5 = f32[4,16,256]{2,1,0:T(8,128)S(1)} custom-call(f32[8,64,256]{2,1,0:T(8,128)S(1)} %get-tuple-element.18.density_ref, f32[3,8,64,256]{3,2,1,0:T(8,128)S(1)} %get-tuple-element.22.weighted, f32[64,256]{1,0:T(8,128)S(1)} %get-tuple-element.23.depth_in, f32[64,256]{1,0:T(8,128)S(1)} %collective-permute-done.refs_0_, ...), custom_call_target="tpu_custom_call" | custom-call | tf_op jit(solution)/shard_map/shade/pallas_call | solution.py:283
  13.0 2.0 %collective-permute-start.6 = (f32[4,16,256]{2,1,0:T(8,128)S(1)}, f32[4,16,256]{2,1,0:T(8,128)S(1)}, u32[]{:S(2)}, u32[]{:S(2)}) collective-permute-start(f32[4,16,256]{2,1,0:T(8,128)S(1)} %shade.5), channel_id=1, source_target_pairs={{0,2},{1,3},{2,0},{3,1},{4,6},{5,7},{6,4},{7,5},{8,10},{9,11},{10,... | collective-permute-start | bytes 196616 | tf_op jit(solution)/shard_map/ppermute | solution.py:292
  15.0 0.3 %shade.6 = f32[4,16,256]{2,1,0:T(8,128)S(1)} custom-call(f32[8,64,256]{2,1,0:T(8,128)S(1)} %get-tuple-element.18.density_ref, f32[3,8,64,256]{3,2,1,0:T(8,128)S(1)} %get-tuple-element.22.weighted, f32[64,256]{1,0:T(8,128)S(1)} %get-tuple-element.23.depth_in, f32[64,256]{1,0:T(8,128)S(1)} %collective-permute-done.refs_0_, ...), custom_call_target="tpu_custom_call" | custom-call | tf_op jit(solution)/shard_map/shade/pallas_call | solution.py:283
  15.3 0.1 collective-permute-start.7
  15.4 0.4 %shade.7.refs_3_ = f32[4,16,256]{2,1,0:T(8,128)S(1)} custom-call(f32[8,64,256]{2,1,0:T(8,128)S(1)} %get-tuple-element.18.density_ref, f32[3,8,64,256]{3,2,1,0:T(8,128)S(1)} %get-tuple-element.22.weighted, f32[64,256]{1,0:T(8,128)S(1)} %get-tuple-element.23.depth_in, f32[64,256]{1,0:T(8,128)S(1)} %collective-permute-done.refs_0_, ...), custom_call_target="tpu_custom_call" | custom-call | tf_op jit(solution)/shard_map/shade/pallas_call | solution.py:283
  15.8 0.9 %collective-permute-done.5.refs_0_ = f32[4,16,256]{2,1,0:T(8,128)S(1)} collective-permute-done((f32[4,16,256]{2,1,0:T(8,128)S(1)}, f32[4,16,256]{2,1,0:T(8,128)S(1)}, u32[]{:S(2)}, u32[]{:S(2)}) %collective-permute-start.5) | collective-permute-done | bytes 65568 | tf_op jit(solution)/shard_map/ppermute | solution.py:292
  16.6 4.2 %collective-permute-done.6.refs_1_ = f32[4,16,256]{2,1,0:T(8,128)S(1)} collective-permute-done((f32[4,16,256]{2,1,0:T(8,128)S(1)}, f32[4,16,256]{2,1,0:T(8,128)S(1)}, u32[]{:S(2)}, u32[]{:S(2)}) %collective-permute-start.6) | collective-permute-done | bytes 65568 | tf_op jit(solution)/shard_map/ppermute | solution.py:292
  20.9 0.2 collective-permute-done.7.refs_2_
  21.1 0.7 %compose.1 = f32[4,16,256]{2,1,0:T(8,128)} custom-call(f32[16,256]{1,0:T(8,128)S(1)} %get-tuple-element.21.earlier, f32[4,16,256]{2,1,0:T(8,128)S(1)} %collective-permute-done.5.refs_0_, f32[4,16,256]{2,1,0:T(8,128)S(1)} %collective-permute-done.6.refs_1_, f32[4,16,256]{2,1,0:T(8,128)S(1)} %collective-permute-done.7.refs_2_, f32[4,16,256]{2,1,0:T(8,128)S(1)} %shade.7.refs_3_), custom_call_target="tpu_custom_call" | custom-call | tf_op jit(solution)/shard_map/compose/pallas_call | solution.py:298
Async XLA Ops:
  1.3 8.5 %collective-permute-start = (f32[64,256]{1,0:T(8,128)S(1)}, f32[64,256]{1,0:T(8,128)S(1)}, u32[]{:S(2)}, u32[]{:S(2)}) collective-permute-start(f32[64,256]{1,0:T(8,128)S(1)} %get-tuple-element.24), channel_id=1, source_target_pairs={{0,1},{1,0},{2,3},{3,2},{4,5},{5,4},{6,7},{7,6},{8,9},{9,8},{10,11... | collective-permute-start | bytes 196616 | tf_op jit(solution)/shard_map/ppermute | solution.py:243
  4.4 5.4 %collective-permute-start.1 = (f32[64,256]{1,0:T(8,128)S(1)}, f32[64,256]{1,0:T(8,128)S(1)}, u32[]{:S(2)}, u32[]{:S(2)}) collective-permute-start(f32[64,256]{1,0:T(8,128)S(1)} %get-tuple-element.25), channel_id=1, source_target_pairs={{0,8},{1,2},{2,1},{3,11},{4,12},{5,6},{6,5},{7,15},{8,0},{9,10},{1... | collective-permute-start | bytes 196616 | tf_op jit(solution)/shard_map/ppermute | solution.py:243
  4.4 5.4 %collective-permute-start.4 = (f32[64,128]{1,0:T(8,128)S(1)}, f32[64,128]{1,0:T(8,128)S(1)}, u32[]{:S(2)}, u32[]{:S(2)}) collective-permute-start(f32[64,128]{1,0:T(8,128)S(1)} %get-tuple-element.28), channel_id=1, source_target_pairs={{0,4},{1,5},{2,6},{3,7},{4,0},{5,1},{6,2},{7,3},{8,12},{9,13},{10,... | collective-permute-start | bytes 98312 | tf_op jit(solution)/shard_map/ppermute | solution.py:243
  5.9 3.3 %collective-permute-start.2 = (f32[8,256]{1,0:T(8,128)S(1)}, f32[8,256]{1,0:T(8,128)S(1)}, u32[]{:S(2)}, u32[]{:S(2)}) collective-permute-start(f32[8,256]{1,0:T(8,128)S(1)} %get-tuple-element.26), channel_id=1, source_target_pairs={{0,8},{1,9},{2,10},{3,11},{4,12},{5,13},{6,14},{7,15},{8,0},{9,1},... | collective-permute-start | bytes 24584 | tf_op jit(solution)/shard_map/ppermute | solution.py:243
  6.1 3.7 %collective-permute-start.3 = (f32[8,256]{1,0:T(8,128)S(1)}, f32[8,256]{1,0:T(8,128)S(1)}, u32[]{:S(2)}, u32[]{:S(2)}) collective-permute-start(f32[8,256]{1,0:T(8,128)S(1)} %get-tuple-element.27), channel_id=1, source_target_pairs={{0,4},{1,5},{2,6},{3,7},{4,0},{5,1},{6,2},{7,3},{8,16},{9,17},{10,... | collective-permute-start | bytes 24584 | tf_op jit(solution)/shard_map/ppermute | solution.py:243
  10.1 6.5 %collective-permute-start.5 = (f32[4,16,256]{2,1,0:T(8,128)S(1)}, f32[4,16,256]{2,1,0:T(8,128)S(1)}, u32[]{:S(2)}, u32[]{:S(2)}) collective-permute-start(f32[4,16,256]{2,1,0:T(8,128)S(1)} %shade.4), channel_id=1, source_target_pairs={{0,3},{1,2},{2,1},{3,0},{4,7},{5,6},{6,5},{7,4},{8,11},{9,10},{10,... | collective-permute-start | bytes 196616 | tf_op jit(solution)/shard_map/ppermute | solution.py:292
  13.0 7.9 %collective-permute-start.6 = (f32[4,16,256]{2,1,0:T(8,128)S(1)}, f32[4,16,256]{2,1,0:T(8,128)S(1)}, u32[]{:S(2)}, u32[]{:S(2)}) collective-permute-start(f32[4,16,256]{2,1,0:T(8,128)S(1)} %shade.5), channel_id=1, source_target_pairs={{0,2},{1,3},{2,0},{3,1},{4,6},{5,7},{6,4},{7,5},{8,10},{9,11},{10,... | collective-permute-start | bytes 196616 | tf_op jit(solution)/shard_map/ppermute | solution.py:292
  15.3 5.7 %collective-permute-start.7 = (f32[4,16,256]{2,1,0:T(8,128)S(1)}, f32[4,16,256]{2,1,0:T(8,128)S(1)}, u32[]{:S(2)}, u32[]{:S(2)}) collective-permute-start(f32[4,16,256]{2,1,0:T(8,128)S(1)} %shade.6), channel_id=1, source_target_pairs={{0,1},{1,0},{2,3},{3,2},{4,5},{5,4},{6,7},{7,6},{8,9},{9,8},{10,11... | collective-permute-start | bytes 196616 | tf_op jit(solution)/shard_map/ppermute | solution.py:292

commit v4 on v3

--- a/solution.py
+++ b/solution.py
@@ -24,40 +24,54 @@
     return [(lax.axis_index(a) == 0, lax.axis_index(a) == lax.axis_size(a) - 1) for a in AXES]
 
 
-def load_kernel(density_hbm, order_hbm, colour_hbm, opacity_hbm, *refs):
-    density_ref, order_ref, colour_ref, opacity_ref, z_a, z_b, x_a, x_b, y_a, *y_b, sems = refs
-    depth, columns, rows = density_ref.shape
-    even_x, even_y, even_z = evens()
+def y_place(depth, tile):
+    tiles = (LANES - 1) // depth
+    return tile // tiles * SUBLANES, tile % tiles * depth
+
+
+def y_shape(depth, columns):
+    return y_place(depth, columns // SUBLANES - 1)[0] + SUBLANES, LANES
+
+
+def depth_faces_kernel(density_ref, z_a, z_b, sems):
+    last = density_ref.shape[0] - 1
+    even = lax.axis_index("gz") % 2 == 0
     copies = [
-        pltpu.make_async_copy(source, target, sems.at[i])
-        for i, (source, target) in enumerate(
-            (
-                (density_hbm, density_ref),
-                (order_hbm, order_ref),
-                (colour_hbm, colour_ref),
-                (opacity_hbm, opacity_ref),
-            )
-        )
+        pltpu.make_async_copy(density_ref.at[jnp.where(even, last, 0)], z_a, sems.at[0]),
+        pltpu.make_async_copy(density_ref.at[jnp.where(even, 0, last)], z_b.at[: z_a.shape[0]], sems.at[1]),
     ]
     for copy in copies:
         copy.start()
     for copy in copies:
         copy.wait()
-    first, last = density_ref[0], density_ref[depth - 1]
-    z_a[...] = jnp.where(even_z, last, first)
-    z_b[...] = jnp.where(even_z, first, last)
+
+
+def side_faces_kernel(density_ref, x_a, x_b, y_a, *y_b):
+    depth, columns, rows = density_ref.shape
+    even_x, even_y, _ = evens()
+    odd_y = lax.axis_index("gy") % 2
+    for out in (x_a, x_b, y_a, *y_b):
+        out[...] = jnp.zeros_like(out)
+    lane = lax.broadcasted_iota(jnp.int32, (SUBLANES, LANES), 1) - odd_y
+    faces = {}
     for z in range(depth):
         first, last = density_ref[z, 0:1, :], density_ref[z, columns - 1 : columns, :]
         x_a[z : z + 1, :] = jnp.where(even_x, last, first)
         x_b[z : z + 1, :] = jnp.where(even_x, first, last)
-    lane = lax.broadcasted_iota(jnp.int32, (columns, LANES), 1)
-    first = last = jnp.zeros((columns, LANES), jnp.float32)
-    for z in range(depth):
-        first = jnp.where(lane == z, pltpu.roll(density_ref[z, :, :LANES], z, 1), first)
-        last = jnp.where(lane == z, pltpu.roll(density_ref[z, :, rows - LANES :], z + 1, 1), last)
-    y_a[...] = jnp.where(even_y, last, first)
-    for y in y_b:
-        y[...] = jnp.where(even_y, first, last)
+        for tile in range(columns // SUBLANES):
+            here = slice(tile * SUBLANES, (tile + 1) * SUBLANES)
+            first, last = density_ref[z, here, :LANES], density_ref[z, here, rows - LANES :]
+            to, at = y_place(depth, tile)
+            for out, near_, far_ in ((y_a, last, first), *((y, first, last) for y in y_b)):
+                edge = jnp.where(even_y, near_, far_)
+                if out is not y_a:
+                    edge = pltpu.roll(edge, jnp.where(even_y, LANES - 1, 1), 1)
+                key = (to, out is y_a)
+                faces[key] = jnp.where(
+                    lane == at + z, pltpu.roll(edge, at + z + 1, 1), faces.get(key, 0.0)
+                )
+    for (to, is_a), value in faces.items():
+        (y_a if is_a else y_b[0])[to : to + SUBLANES, :] = value
 
 
 def look(words, index, upper):
@@ -72,20 +86,13 @@
 
 
 def weights_kernel(
-    step, relative, order_ref, density_ref, bins_hbm, colour_ref, opacity_ref,
-    weighted, depth_out, earlier, bins_ref, sems,
+    step, relative, order_ref, density_ref, bins_ref, colour_ref, opacity_ref,
+    weighted, depth_out, earlier,
 ):
     depth, columns, rows = density_ref.shape
     bricks = order_ref.shape[2]
     me = lax.axis_index("gz")
 
-    def fetch(tile):
-        at = pl.ds(pl.multiple_of(tile * SUBLANES, SUBLANES), SUBLANES)
-        return pltpu.make_async_copy(
-            bins_hbm.at[:, at, :], bins_ref.at[:, at, :], sems.at[tile]
-        )
-
-    lax.fori_loop(0, columns // SUBLANES, lambda i, c: fetch(i).start(), None)
     order = order_ref[0]
     brick = lax.broadcasted_iota(jnp.int32, order.shape, 1)
     ranks = [
@@ -111,7 +118,6 @@
 
     def one_tile(tile, carry):
         here = pl.ds(pl.multiple_of(tile * SUBLANES, SUBLANES), SUBLANES)
-        fetch(tile).wait()
         for at in pieces(rows):
             total = jnp.zeros((SUBLANES, LANES), jnp.float32)
             seen = jnp.full((SUBLANES, LANES), 1.0 / 4096.0, jnp.float32)
@@ -129,7 +135,7 @@
             depth_out[here, at] = total
         return carry
 
-    lax.fori_loop(0, columns // SUBLANES, one_tile, 0)
+    lax.fori_loop(0, columns // SUBLANES, one_tile, 0, unroll=True)
 
 
 def shade_kernel(part, density_ref, weighted, depth_in, *refs):
@@ -141,8 +147,9 @@
     tiles = out.shape[1] // SUBLANES
     start = 0 if part is None else (lax.axis_index("gz") ^ part) * tiles
     end = columns // SUBLANES - 1
-    x_before[...] = jnp.where(first_x, 0.0, jnp.where(even_x, x_b[...], x_a[...]))
-    x_after[...] = jnp.where(last_x, 0.0, jnp.where(even_x, x_a[...], x_b[...]))
+    x_a, x_b = x_a[:depth, :], x_b[:depth, :]
+    x_before[...] = jnp.where(first_x, 0.0, jnp.where(even_x, x_b, x_a))
+    x_after[...] = jnp.where(last_x, 0.0, jnp.where(even_x, x_a, x_b))
     sub = lax.broadcasted_iota(jnp.int32, (SUBLANES, LANES), 0)
     lane = lax.broadcasted_iota(jnp.int32, (SUBLANES, LANES), 1)
     cuts = pieces(rows)
@@ -156,10 +163,14 @@
             pl.multiple_of(jnp.minimum(x0 + SUBLANES, columns - SUBLANES), SUBLANES), SUBLANES
         )
         top, bottom = tile == 0, tile == end
-        y_before = y_after = y_a[here, :]
+        to, lane0 = y_place(depth, tile)
+        turn = (LANES - lane0 - jnp.where(even_y, 1, 0)) % LANES
+        y_rows = pl.ds(pl.multiple_of(to, SUBLANES), SUBLANES)
+        y_before = y_after = pltpu.roll(y_a[y_rows, :], turn, 1)
         if len(halos) == 6:
-            y_before = jnp.where(even_y, halos[5][here, :], y_before)
-            y_after = jnp.where(even_y, y_after, halos[5][here, :])
+            second = pltpu.roll(halos[5][y_rows, :], turn, 1)
+            y_before = jnp.where(even_y, second, y_before)
+            y_after = jnp.where(even_y, y_after, second)
         y_before, y_after = jnp.where(first_y, 0.0, y_before), jnp.where(last_y, 0.0, y_after)
         plane = [
             jnp.where(first_z, 0.0, jnp.where(even_z, z_b[here, at], z_a[here, at])) for at in cuts
@@ -202,7 +213,7 @@
             out[3, to, at] = depth_in[here, at]
         return carry
 
-    lax.fori_loop(0, tiles, one_tile, 0)
+    lax.fori_loop(0, tiles, one_tile, 0, unroll=tiles <= 2)
 
 
 def compose_kernel(count, earlier, *refs):
@@ -227,7 +238,7 @@
 
 def swap(values, axis):
     sizes = [lax.axis_size(a) for a in AXES]
-    at, other = AXES.index(axis), 0 if axis != "gx" else 1
+    at, other = AXES.index(axis), 0
     strides = [sizes[1] * sizes[2], sizes[2], 1]
     got = []
     for start, value in enumerate(values):
@@ -237,6 +248,8 @@
             partner = where[at] + 1 if where[at] % 2 == start else where[at] - 1
             if 0 <= partner < sizes[at]:
                 where[at] = partner
+            elif axis == "gx":
+                where[at] = sizes[at] - 1 - where[at]
             else:
                 where[other] ^= 1
             pairs.append((device, sum(w * s for w, s in zip(where, strides))))
@@ -255,16 +268,22 @@
         out_specs=jax.tree.map(lambda _: VMEM, out_shape),
         compiler_params=pltpu.CompilerParams(vmem_limit_bytes=SCOPED), **more,
     )
+    y_height, _ = y_shape(depth, columns)
     y_sides = 1 if lax.axis_size("gy") == 2 else 2
-    density, order, colour_table, opacity_table, *faces = call(
-        load_kernel, "load",
-        [pltpu.VMEM(a.shape, a.dtype) for a in (density, order, colour_table, opacity_table)]
-        + [near(columns, rows)] * 2 + [near(depth, rows)] * 2 + [near(columns, LANES)] * y_sides,
-        [HBM] * 4, scratch_shapes=[pltpu.SemaphoreType.DMA((4,))],
-    )(*far(density, order, colour_table, opacity_table))
-    density, order, colour_table, opacity_table, *faces = here(
-        density, order, colour_table, opacity_table, *faces
+    z_faces = call(
+        depth_faces_kernel, "depth_faces", [near(columns, rows), near(columns + SUBLANES, rows)], [HBM],
+        scratch_shapes=[pltpu.SemaphoreType.DMA((2,))],
+        cost_estimate=pl.CostEstimate(flops=2 * 10**9, bytes_accessed=2 * 10**6, transcendentals=0),
+    )(*far(density))
+    density, bins, order, colour_table, opacity_table = here(
+        density, bins, order, colour_table, opacity_table
     )
+    side_faces = call(
+        side_faces_kernel, "side_faces",
+        [near(depth, rows), near(2 * depth, rows)]
+        + [near(y_height + 2 * SUBLANES, LANES)] * y_sides, [VMEM],
+    )(density)
+    faces = here(*z_faces, *side_faces)
     halos = swap(faces[:2], "gz") + swap(faces[2:4], "gx") + swap(faces[4:], "gy")
 
     tile_rows = columns // bricks
@@ -273,12 +292,8 @@
     weighted, depths, earlier = call(
         functools.partial(weights_kernel, step, direct), "weights",
         [near(3, depth, columns, rows), near(columns, rows), near(bricks * bricks, rows)],
-        [VMEM] * 2 + [HBM] + [VMEM] * 2,
-        scratch_shapes=[
-            pltpu.VMEM(bins.shape, bins.dtype),
-            pltpu.SemaphoreType.DMA((columns // SUBLANES,)),
-        ],
-    )(order, density, *far(bins), colour_table, opacity_table)
+        [VMEM] * 5,
+    )(order, density, bins, colour_table, opacity_table)
     weighted, depths, earlier = here(weighted, depths, earlier)
     shade = lambda part, tile: call(
         functools.partial(shade_kernel, part), "shade",

time: 21.9 us -> 20.1 us (0.918)
  starting transfers between devices: 9.93 us -> 12.2 us
  waiting for transfers between devices: 5.89 us -> 3.71 us
  Pallas kernels: 5.86 us -> 3.96 us
    ppermute x5, starting transfers between devices: 5.34 us -> 7.59 us  [swap(): got.append(lax.ppermute(value, AXES, pairs))]
    ppermute x3, waiting for transfers between devices: 5.3 us -> 3.57 us  [local(): received.append(lax.ppermute(shade(k, tile_rows), 'gz', pairs))]
    pallas_call x1, Pallas kernels: 2.55 us -> 1.07 us  [local(): call(functools.partial(weights_kernel, step, direct), 'weights', [near(3,...]
    ppermute x5, waiting for transfers between devices: 0.59 us -> 0.14 us  [swap(): got.append(lax.ppermute(value, AXES, pairs))]
    pallas_call x4, Pallas kernels: 1.37 us -> 1.09 us  [local(): call(functools.partial(shade_kernel, part), 'shade', near(4, tile, rows),...]
    pallas_call x1 -> x2, Pallas kernels: 1.28 us -> 1.13 us  [the longest x1 0.99 us: local(): call(depth_faces_kernel, 'depth_faces', [near(columns, rows), near(column...]
  transfers between devices with their start and end apart: 8 -> 8, of which waited for: 4 -> 4; matrix products, arithmetic and copies ran while one was open for 0% -> 0% of each run, Pallas kernels for 16% -> 10%
where the time goes in v4:
time: 20.1 us; the launch traced here: 19.9 us
  starting transfers between devices  12.2 us (61%)
  Pallas kernels  3.96 us (20%)
  waiting for transfers between devices  3.71 us (18%)
    ppermute x5, starting transfers between devices, swap(): got.append(lax.ppermute(value, AXES, pairs))  7.59 us
    ppermute x3, starting transfers between devices, local(): received.append(lax.ppermute(shade(k, tile_rows), 'gz', pairs))  4.58 us
    ppermute x3, waiting for transfers between devices, local(): received.append(lax.ppermute(shade(k, tile_rows), 'gz', pairs))  3.57 us
    pallas_call x4, Pallas kernels, local(): call(functools.partial(shade_kernel, part), 'shade', near(4, tile, rows),...  1.09 us
    pallas_call x1, Pallas kernels, local(): call(functools.partial(weights_kernel, step, direct), 'weights', [near(3,...  1.07 us
    pallas_call x1, Pallas kernels, local(): call(depth_faces_kernel, 'depth_faces', [near(columns, rows), near(column...  0.99 us
    pallas_call x1, Pallas kernels, local(): call(functools.partial(compose_kernel, bricks), 'compose', jax.ShapeDtype...  0.68 us
  transfers between devices with their start and end apart: 8, of which 4 were waited for; matrix products, arithmetic and copies ran while one was open for 0% of the time, Pallas kernels for 10%

profile of v4, /device:TPU:0, one launch (start us, length us, event | category | flops | bytes accessed | tf_op | source)
XLA Modules:
  0.0 19.9 jit_solution(17183556898100373443)
XLA Ops:
  0.0 0.0 copy-start
  0.0 0.0 copy-start.3
  0.0 0.0 copy-start.4
  0.0 1.0 %depth_faces.1 = (f32[64,256]{1,0:T(8,128)S(1)}, f32[72,256]{1,0:T(8,128)S(1)}) custom-call(f32[8,64,256]{2,1,0:T(8,128)} %density_ref.13), custom_call_target="tpu_custom_call" | custom-call | flops 2000000000 | bytes 2000000 | tf_op jit(solution)/shard_map/depth_faces/pallas_call | solution.py:273
  1.0 0.5 %collective-permute-start.1 = (f32[72,256]{1,0:T(8,128)S(1)}, f32[72,256]{1,0:T(8,128)S(1)}, u32[]{:S(2)}, u32[]{:S(2)}) collective-permute-start(f32[72,256]{1,0:T(8,128)S(1)} %get-tuple-element.17), channel_id=1, source_target_pairs={{0,8},{1,2},{2,1},{3,11},{4,12},{5,6},{6,5},{7,15},{8,0},{9,10},{1... | collective-permute-start | bytes 221192 | tf_op jit(solution)/shard_map/ppermute | solution.py:256
  1.5 4.1 %collective-permute-start = (f32[64,256]{1,0:T(8,128)S(1)}, f32[64,256]{1,0:T(8,128)S(1)}, u32[]{:S(2)}, u32[]{:S(2)}) collective-permute-start(f32[64,256]{1,0:T(8,128)S(1)} %get-tuple-element.16), channel_id=1, source_target_pairs={{0,1},{1,0},{2,3},{3,2},{4,5},{5,4},{6,7},{7,6},{8,9},{9,8},{10,11... | collective-permute-start | bytes 196616 | tf_op jit(solution)/shard_map/ppermute | solution.py:256
  5.7 0.0 copy-done
  5.7 0.1 side_faces.1
  5.8 0.4 %collective-permute-start.3 = (f32[16,256]{1,0:T(8,128)S(1)}, f32[16,256]{1,0:T(8,128)S(1)}, u32[]{:S(2)}, u32[]{:S(2)}) collective-permute-start(f32[16,256]{1,0:T(8,128)S(1)} %get-tuple-element.19), channel_id=1, source_target_pairs={{0,24},{1,25},{2,26},{3,27},{4,28},{5,29},{6,30},{7,31},{8,16},{9,... | collective-permute-start | bytes 49160 | tf_op jit(solution)/shard_map/ppermute | solution.py:256
  6.3 1.5 %collective-permute-start.4 = (f32[24,128]{1,0:T(8,128)S(1)}, f32[24,128]{1,0:T(8,128)S(1)}, u32[]{:S(2)}, u32[]{:S(2)}) collective-permute-start(f32[24,128]{1,0:T(8,128)S(1)} %get-tuple-element.20), channel_id=1, source_target_pairs={{0,4},{1,5},{2,6},{3,7},{4,0},{5,1},{6,2},{7,3},{8,12},{9,13},{10,... | collective-permute-start | bytes 36872 | tf_op jit(solution)/shard_map/ppermute | solution.py:256
  7.8 1.0 %collective-permute-start.2 = (f32[8,256]{1,0:T(8,128)S(1)}, f32[8,256]{1,0:T(8,128)S(1)}, u32[]{:S(2)}, u32[]{:S(2)}) collective-permute-start(f32[8,256]{1,0:T(8,128)S(1)} %get-tuple-element.18), channel_id=1, source_target_pairs={{0,8},{1,9},{2,10},{3,11},{4,12},{5,13},{6,14},{7,15},{8,0},{9,1},... | collective-permute-start | bytes 24584 | tf_op jit(solution)/shard_map/ppermute | solution.py:256
  8.8 0.0 copy-done.3
  8.8 0.0 copy-done.4
  8.8 0.0 copy-done.2
  8.8 0.0 copy-done.1
  8.8 1.1 %weights.1 = (f32[3,8,64,256]{3,2,1,0:T(8,128)S(1)}, f32[64,256]{1,0:T(8,128)S(1)}, f32[16,256]{1,0:T(8,128)S(1)}) custom-call(s32[1,1,4]{2,1,0:T(1,128)S(1)} %copy-done.3, f32[8,64,256]{2,1,0:T(8,128)S(1)} %copy-done, s32[8,64,256]{2,1,0:T(8,128)S(1)} %copy-done.1, bf16[3,256]{1,0:T(4,128)(2,1)S(1)} %copy-done.2, bf16[256]{0:T(256)(128)(2,1)S(1)} %copy-done.4), custom_call_target="tpu_custom_call" | custom-call | tf_op jit(solution)/shard_map/weights/pallas_call | solution.py:292
  9.8 0.0 collective-permute-done.2.refs_2_
  9.8 0.1 collective-permute-done.4.refs_4_
  10.0 0.0 collective-permute-done.3.refs_3_
  10.0 0.0 collective-permute-done.refs_0_
  10.0 0.0 collective-permute-done.1.refs_1_
  10.0 0.3 %shade.4 = f32[4,16,256]{2,1,0:T(8,128)S(1)} custom-call(f32[8,64,256]{2,1,0:T(8,128)S(1)} %copy-done, f32[3,8,64,256]{3,2,1,0:T(8,128)S(1)} %get-tuple-element.14.weighted, f32[64,256]{1,0:T(8,128)S(1)} %get-tuple-element.15.depth_in, f32[64,256]{1,0:T(8,128)S(1)} %collective-permute-done.refs_0_, f32[72,256]{1,0:T(8,128)S(1)} %collective-permute-done.1.refs_1_, ...), custom_call_target="tpu_custom_call" | custom-call | tf_op jit(solution)/shard_map/shade/pallas_call | solution.py:298
  10.3 1.8 %collective-permute-start.5 = (f32[4,16,256]{2,1,0:T(8,128)S(1)}, f32[4,16,256]{2,1,0:T(8,128)S(1)}, u32[]{:S(2)}, u32[]{:S(2)}) collective-permute-start(f32[4,16,256]{2,1,0:T(8,128)S(1)} %shade.4), channel_id=1, source_target_pairs={{0,3},{1,2},{2,1},{3,0},{4,7},{5,6},{6,5},{7,4},{8,11},{9,10},{10,... | collective-permute-start | bytes 196616 | tf_op jit(solution)/shard_map/ppermute | solution.py:307
  12.1 0.3 %shade.5 = f32[4,16,256]{2,1,0:T(8,128)S(1)} custom-call(f32[8,64,256]{2,1,0:T(8,128)S(1)} %copy-done, f32[3,8,64,256]{3,2,1,0:T(8,128)S(1)} %get-tuple-element.14.weighted, f32[64,256]{1,0:T(8,128)S(1)} %get-tuple-element.15.depth_in, f32[64,256]{1,0:T(8,128)S(1)} %collective-permute-done.refs_0_, f32[72,256]{1,0:T(8,128)S(1)} %collective-permute-done.1.refs_1_, ...), custom_call_target="tpu_custom_call" | custom-call | tf_op jit(solution)/shard_map/shade/pallas_call | solution.py:298
  12.4 0.3 %collective-permute-start.6 = (f32[4,16,256]{2,1,0:T(8,128)S(1)}, f32[4,16,256]{2,1,0:T(8,128)S(1)}, u32[]{:S(2)}, u32[]{:S(2)}) collective-permute-start(f32[4,16,256]{2,1,0:T(8,128)S(1)} %shade.5), channel_id=1, source_target_pairs={{0,2},{1,3},{2,0},{3,1},{4,6},{5,7},{6,4},{7,5},{8,10},{9,11},{10,... | collective-permute-start | bytes 196616 | tf_op jit(solution)/shard_map/ppermute | solution.py:307
  12.7 0.3 %shade.6 = f32[4,16,256]{2,1,0:T(8,128)S(1)} custom-call(f32[8,64,256]{2,1,0:T(8,128)S(1)} %copy-done, f32[3,8,64,256]{3,2,1,0:T(8,128)S(1)} %get-tuple-element.14.weighted, f32[64,256]{1,0:T(8,128)S(1)} %get-tuple-element.15.depth_in, f32[64,256]{1,0:T(8,128)S(1)} %collective-permute-done.refs_0_, f32[72,256]{1,0:T(8,128)S(1)} %collective-permute-done.1.refs_1_, ...), custom_call_target="tpu_custom_call" | custom-call | tf_op jit(solution)/shard_map/shade/pallas_call | solution.py:298
  13.0 2.4 %collective-permute-start.7 = (f32[4,16,256]{2,1,0:T(8,128)S(1)}, f32[4,16,256]{2,1,0:T(8,128)S(1)}, u32[]{:S(2)}, u32[]{:S(2)}) collective-permute-start(f32[4,16,256]{2,1,0:T(8,128)S(1)} %shade.6), channel_id=1, source_target_pairs={{0,1},{1,0},{2,3},{3,2},{4,5},{5,4},{6,7},{7,6},{8,9},{9,8},{10,11... | collective-permute-start | bytes 196616 | tf_op jit(solution)/shard_map/ppermute | solution.py:307
  15.4 0.3 %shade.7.refs_3_ = f32[4,16,256]{2,1,0:T(8,128)S(1)} custom-call(f32[8,64,256]{2,1,0:T(8,128)S(1)} %copy-done, f32[3,8,64,256]{3,2,1,0:T(8,128)S(1)} %get-tuple-element.14.weighted, f32[64,256]{1,0:T(8,128)S(1)} %get-tuple-element.15.depth_in, f32[64,256]{1,0:T(8,128)S(1)} %collective-permute-done.refs_0_, f32[72,256]{1,0:T(8,128)S(1)} %collective-permute-done.1.refs_1_, ...), custom_call_target="tpu_custom_call" | custom-call | tf_op jit(solution)/shard_map/shade/pallas_call | solution.py:298
  15.7 1.4 %collective-permute-done.5.refs_0_ = f32[4,16,256]{2,1,0:T(8,128)S(1)} collective-permute-done((f32[4,16,256]{2,1,0:T(8,128)S(1)}, f32[4,16,256]{2,1,0:T(8,128)S(1)}, u32[]{:S(2)}, u32[]{:S(2)}) %collective-permute-start.5) | collective-permute-done | bytes 65568 | tf_op jit(solution)/shard_map/ppermute | solution.py:307
  17.1 2.1 %collective-permute-done.6.refs_1_ = f32[4,16,256]{2,1,0:T(8,128)S(1)} collective-permute-done((f32[4,16,256]{2,1,0:T(8,128)S(1)}, f32[4,16,256]{2,1,0:T(8,128)S(1)}, u32[]{:S(2)}, u32[]{:S(2)}) %collective-permute-start.6) | collective-permute-done | bytes 65568 | tf_op jit(solution)/shard_map/ppermute | solution.py:307
  19.1 0.1 collective-permute-done.7.refs_2_
  19.3 0.7 %compose.1 = f32[4,16,256]{2,1,0:T(8,128)} custom-call(f32[16,256]{1,0:T(8,128)S(1)} %get-tuple-element.13.earlier, f32[4,16,256]{2,1,0:T(8,128)S(1)} %collective-permute-done.5.refs_0_, f32[4,16,256]{2,1,0:T(8,128)S(1)} %collective-permute-done.6.refs_1_, f32[4,16,256]{2,1,0:T(8,128)S(1)} %collective-permute-done.7.refs_2_, f32[4,16,256]{2,1,0:T(8,128)S(1)} %shade.7.refs_3_), custom_call_target="tpu_custom_call" | custom-call | tf_op jit(solution)/shard_map/compose/pallas_call | solution.py:313
  (2 shorter events, 0.0 us)
Async XLA Ops:
  0.0 5.7 %copy-start = (f32[8,64,256]{2,1,0:T(8,128)S(1)}, f32[8,64,256]{2,1,0:T(8,128)}, u32[]{:S(2)}) copy-start(f32[8,64,256]{2,1,0:T(8,128)} %density_ref.13) | copy-start | bytes 1572868
  0.0 8.7 %copy-start.3 = (s32[1,1,4]{2,1,0:T(1,128)S(1)}, s32[1,1,4]{2,1,0:T(1,128)}, u32[]{:S(2)}) copy-start(s32[1,1,4]{2,1,0:T(1,128)} %order_ref.1) | copy-start | bytes 52
  0.0 8.8 %copy-start.4 = (bf16[256]{0:T(256)(128)(2,1)S(1)}, bf16[256]{0:T(256)(128)(2,1)}, u32[]{:S(2)}) copy-start(bf16[256]{0:T(256)(128)(2,1)} %opacity_ref.1) | copy-start | bytes 1540
  0.0 8.8 %copy-start.2 = (bf16[3,256]{1,0:T(4,128)(2,1)S(1)}, bf16[3,256]{1,0:T(4,128)(2,1)}, u32[]{:S(2)}) copy-start(bf16[3,256]{1,0:T(4,128)(2,1)} %colour_ref.1) | copy-start | bytes 4612
  0.0 8.8 %copy-start.1 = (s32[8,64,256]{2,1,0:T(8,128)S(1)}, s32[8,64,256]{2,1,0:T(8,128)}, u32[]{:S(2)}) copy-start(s32[8,64,256]{2,1,0:T(8,128)} %bins_ref.1) | copy-start | bytes 1572868
  1.0 9.0 %collective-permute-start.1 = (f32[72,256]{1,0:T(8,128)S(1)}, f32[72,256]{1,0:T(8,128)S(1)}, u32[]{:S(2)}, u32[]{:S(2)}) collective-permute-start(f32[72,256]{1,0:T(8,128)S(1)} %get-tuple-element.17), channel_id=1, source_target_pairs={{0,8},{1,2},{2,1},{3,11},{4,12},{5,6},{6,5},{7,15},{8,0},{9,10},{1... | collective-permute-start | bytes 221192 | tf_op jit(solution)/shard_map/ppermute | solution.py:256
  1.5 8.4 %collective-permute-start = (f32[64,256]{1,0:T(8,128)S(1)}, f32[64,256]{1,0:T(8,128)S(1)}, u32[]{:S(2)}, u32[]{:S(2)}) collective-permute-start(f32[64,256]{1,0:T(8,128)S(1)} %get-tuple-element.16), channel_id=1, source_target_pairs={{0,1},{1,0},{2,3},{3,2},{4,5},{5,4},{6,7},{7,6},{8,9},{9,8},{10,11... | collective-permute-start | bytes 196616 | tf_op jit(solution)/shard_map/ppermute | solution.py:256
  5.8 4.1 %collective-permute-start.3 = (f32[16,256]{1,0:T(8,128)S(1)}, f32[16,256]{1,0:T(8,128)S(1)}, u32[]{:S(2)}, u32[]{:S(2)}) collective-permute-start(f32[16,256]{1,0:T(8,128)S(1)} %get-tuple-element.19), channel_id=1, source_target_pairs={{0,24},{1,25},{2,26},{3,27},{4,28},{5,29},{6,30},{7,31},{8,16},{9,... | collective-permute-start | bytes 49160 | tf_op jit(solution)/shard_map/ppermute | solution.py:256
  6.3 3.7 %collective-permute-start.4 = (f32[24,128]{1,0:T(8,128)S(1)}, f32[24,128]{1,0:T(8,128)S(1)}, u32[]{:S(2)}, u32[]{:S(2)}) collective-permute-start(f32[24,128]{1,0:T(8,128)S(1)} %get-tuple-element.20), channel_id=1, source_target_pairs={{0,4},{1,5},{2,6},{3,7},{4,0},{5,1},{6,2},{7,3},{8,12},{9,13},{10,... | collective-permute-start | bytes 36872 | tf_op jit(solution)/shard_map/ppermute | solution.py:256
  7.8 2.0 %collective-permute-start.2 = (f32[8,256]{1,0:T(8,128)S(1)}, f32[8,256]{1,0:T(8,128)S(1)}, u32[]{:S(2)}, u32[]{:S(2)}) collective-permute-start(f32[8,256]{1,0:T(8,128)S(1)} %get-tuple-element.18), channel_id=1, source_target_pairs={{0,8},{1,9},{2,10},{3,11},{4,12},{5,13},{6,14},{7,15},{8,0},{9,1},... | collective-permute-start | bytes 24584 | tf_op jit(solution)/shard_map/ppermute | solution.py:256
  10.3 6.8 %collective-permute-start.5 = (f32[4,16,256]{2,1,0:T(8,128)S(1)}, f32[4,16,256]{2,1,0:T(8,128)S(1)}, u32[]{:S(2)}, u32[]{:S(2)}) collective-permute-start(f32[4,16,256]{2,1,0:T(8,128)S(1)} %shade.4), channel_id=1, source_target_pairs={{0,3},{1,2},{2,1},{3,0},{4,7},{5,6},{6,5},{7,4},{8,11},{9,10},{10,... | collective-permute-start | bytes 196616 | tf_op jit(solution)/shard_map/ppermute | solution.py:307
  12.4 6.8 %collective-permute-start.6 = (f32[4,16,256]{2,1,0:T(8,128)S(1)}, f32[4,16,256]{2,1,0:T(8,128)S(1)}, u32[]{:S(2)}, u32[]{:S(2)}) collective-permute-start(f32[4,16,256]{2,1,0:T(8,128)S(1)} %shade.5), channel_id=1, source_target_pairs={{0,2},{1,3},{2,0},{3,1},{4,6},{5,7},{6,4},{7,5},{8,10},{9,11},{10,... | collective-permute-start | bytes 196616 | tf_op jit(solution)/shard_map/ppermute | solution.py:307
  13.0 6.3 %collective-permute-start.7 = (f32[4,16,256]{2,1,0:T(8,128)S(1)}, f32[4,16,256]{2,1,0:T(8,128)S(1)}, u32[]{:S(2)}, u32[]{:S(2)}) collective-permute-start(f32[4,16,256]{2,1,0:T(8,128)S(1)} %shade.6), channel_id=1, source_target_pairs={{0,1},{1,0},{2,3},{3,2},{4,5},{5,4},{6,7},{7,6},{8,9},{9,8},{10,11... | collective-permute-start | bytes 196616 | tf_op jit(solution)/shard_map/ppermute | solution.py:307

commit v5 on v4

--- a/solution.py
+++ b/solution.py
@@ -22,6 +22,20 @@
 
 def ends():
     return [(lax.axis_index(a) == 0, lax.axis_index(a) == lax.axis_size(a) - 1) for a in AXES]
+
+
+def by_core(shift):
+    even, odd = shift
+    return even if even == odd else jnp.where(lax.axis_index("gx") % 2 == 0, even, odd)
+
+
+def shifted(shift):
+    nx, ny, nz = (lax.axis_size(a) for a in AXES)
+    at = lambda x, y, z: (x * ny + y) * nz + z
+    return [
+        (at(x, y, z), at(x, y, (z + shift[x % 2]) % nz))
+        for x in range(nx) for y in range(ny) for z in range(nz)
+    ]
 
 
 def y_place(depth, tile):
@@ -86,17 +100,18 @@
 
 
 def weights_kernel(
-    step, relative, order_ref, density_ref, bins_ref, colour_ref, opacity_ref,
+    step, shifts, order_ref, density_ref, bins_ref, colour_ref, opacity_ref,
     weighted, depth_out, earlier,
 ):
     depth, columns, rows = density_ref.shape
     bricks = order_ref.shape[2]
     me = lax.axis_index("gz")
 
+    source = lambda i: i if shifts is None else (me + bricks - by_core(shifts[i])) % bricks
     order = order_ref[0]
     brick = lax.broadcasted_iota(jnp.int32, order.shape, 1)
     ranks = [
-        jnp.sum(jnp.where(brick == (i ^ me if relative else i), order, 0), axis=1, keepdims=True)
+        jnp.sum(jnp.where(brick == source(i), order, 0), axis=1, keepdims=True)
         for i in range(bricks)
     ]
     for i in range(bricks):
@@ -145,7 +160,9 @@
     even_x, even_y, even_z = evens()
     (first_x, last_x), (first_y, last_y), (first_z, last_z) = ends()
     tiles = out.shape[1] // SUBLANES
-    start = 0 if part is None else (lax.axis_index("gz") ^ part) * tiles
+    start = 0
+    if part is not None:
+        start = (lax.axis_index("gz") + by_core(part)) % lax.axis_size("gz") * tiles
     end = columns // SUBLANES - 1
     x_a, x_b = x_a[:depth, :], x_b[:depth, :]
     x_before[...] = jnp.where(first_x, 0.0, jnp.where(even_x, x_b, x_a))
@@ -218,7 +235,7 @@
 
 def compose_kernel(count, earlier, *refs):
     out = refs[-1]
-    bricks = refs[count - 1 :: -1] if len(refs) > 2 else [refs[0].at[i] for i in range(count)]
+    bricks = refs[:count] if len(refs) > 2 else [refs[0].at[i] for i in range(count)]
     depths = [b[3] for b in bricks]
     sums = [jnp.zeros_like(depths[0]) for _ in range(3)]
     total = jnp.zeros_like(depths[0])
@@ -287,10 +304,11 @@
     halos = swap(faces[:2], "gz") + swap(faces[2:4], "gx") + swap(faces[4:], "gy")
 
     tile_rows = columns // bricks
-    direct = tile_rows % SUBLANES == 0 and bricks & (bricks - 1) == 0
+    direct = tile_rows % SUBLANES == 0
+    shifts = [(k, k % (bricks - 1) + 1) for k in range(1, bricks)] + [(0, 0)] if direct else None
     step = 3.0 / (depth * bricks) * math.log2(math.e) / 1024.0
     weighted, depths, earlier = call(
-        functools.partial(weights_kernel, step, direct), "weights",
+        functools.partial(weights_kernel, step, shifts), "weights",
         [near(3, depth, columns, rows), near(columns, rows), near(bricks * bricks, rows)],
         [VMEM] * 5,
     )(order, density, bins, colour_table, opacity_table)
@@ -302,10 +320,11 @@
     )(density, weighted, depths, *here(*halos))
     if direct:
         received = []
-        for k in range(bricks - 1, 0, -1):
-            pairs = [(i, i ^ k) for i in range(bricks)]
-            received.append(lax.ppermute(shade(k, tile_rows), "gz", pairs))
-        received.append(shade(0, tile_rows))
+        for shift in shifts:
+            part = shade(shift, tile_rows)
+            if shift != (0, 0):
+                part = lax.ppermute(part, AXES, shifted(shift))
+            received.append(part)
     else:
         whole = shade(None, columns)
         cut = jnp.moveaxis(whole.reshape(4, bricks, tile_rows, rows), 1, 0)

time: 20.1 us -> 19.2 us (0.955)
  waiting for transfers between devices: 3.71 us -> 2.21 us
  starting transfers between devices: 12.2 us -> 12.7 us
    ppermute x3, waiting for transfers between devices: 3.57 us -> 2.1 us  [local(): part = lax.ppermute(part, AXES, shifted(shift))]
    ppermute x3, starting transfers between devices: 4.58 us -> 5.06 us  [local(): part = lax.ppermute(part, AXES, shifted(shift))]
  transfers between devices with their start and end apart: 8 -> 8, of which waited for: 4 -> 3; matrix products, arithmetic and copies ran while one was open for 0% -> 0% of each run, Pallas kernels for 10% -> 11%
where the time goes in v5:
time: 19.2 us; the launch traced here: 19 us
  starting transfers between devices  12.7 us (66%)
  Pallas kernels  4.03 us (21%)
  waiting for transfers between devices  2.21 us (12%)
    ppermute x5, starting transfers between devices, swap(): got.append(lax.ppermute(value, AXES, pairs))  7.59 us
    ppermute x3, starting transfers between devices, local(): part = lax.ppermute(part, AXES, shifted(shift))  5.06 us
    ppermute x3, waiting for transfers between devices, local(): part = lax.ppermute(part, AXES, shifted(shift))  2.1 us
    pallas_call x4, Pallas kernels, local(): call(functools.partial(shade_kernel, part), 'shade', near(4, tile, rows),...  1.13 us
    pallas_call x1, Pallas kernels, local(): call(functools.partial(weights_kernel, step, shifts), 'weights', [near(3,...  1.1 us
    pallas_call x1, Pallas kernels, local(): call(depth_faces_kernel, 'depth_faces', [near(columns, rows), near(column...  0.99 us
    pallas_call x1, Pallas kernels, local(): call(functools.partial(compose_kernel, bricks), 'compose', jax.ShapeDtype...  0.68 us
  transfers between devices with their start and end apart: 8, of which 3 were waited for; matrix products, arithmetic and copies ran while one was open for 0% of the time, Pallas kernels for 11%

profile of v5, /device:TPU:0, one launch (start us, length us, event | category | flops | bytes accessed | tf_op | source)
XLA Modules:
  0.0 19.0 jit_solution(7984612612735305258)
XLA Ops:
  0.0 0.0 copy-start
  0.0 0.0 copy-start.3
  0.0 0.0 copy-start.4
  0.0 1.0 %depth_faces.1 = (f32[64,256]{1,0:T(8,128)S(1)}, f32[72,256]{1,0:T(8,128)S(1)}) custom-call(f32[8,64,256]{2,1,0:T(8,128)} %density_ref.13), custom_call_target="tpu_custom_call" | custom-call | flops 2000000000 | bytes 2000000 | tf_op jit(solution)/shard_map/depth_faces/pallas_call | solution.py:290
  1.0 0.5 %collective-permute-start.1 = (f32[72,256]{1,0:T(8,128)S(1)}, f32[72,256]{1,0:T(8,128)S(1)}, u32[]{:S(2)}, u32[]{:S(2)}) collective-permute-start(f32[72,256]{1,0:T(8,128)S(1)} %get-tuple-element.17), channel_id=1, source_target_pairs={{0,8},{1,2},{2,1},{3,11},{4,12},{5,6},{6,5},{7,15},{8,0},{9,10},{1... | collective-permute-start | bytes 221192 | tf_op jit(solution)/shard_map/ppermute | solution.py:273
  1.5 4.1 %collective-permute-start = (f32[64,256]{1,0:T(8,128)S(1)}, f32[64,256]{1,0:T(8,128)S(1)}, u32[]{:S(2)}, u32[]{:S(2)}) collective-permute-start(f32[64,256]{1,0:T(8,128)S(1)} %get-tuple-element.16), channel_id=1, source_target_pairs={{0,1},{1,0},{2,3},{3,2},{4,5},{5,4},{6,7},{7,6},{8,9},{9,8},{10,11... | collective-permute-start | bytes 196616 | tf_op jit(solution)/shard_map/ppermute | solution.py:273
  5.7 0.0 copy-done
  5.7 0.1 side_faces.1
  5.8 0.4 %collective-permute-start.3 = (f32[16,256]{1,0:T(8,128)S(1)}, f32[16,256]{1,0:T(8,128)S(1)}, u32[]{:S(2)}, u32[]{:S(2)}) collective-permute-start(f32[16,256]{1,0:T(8,128)S(1)} %get-tuple-element.19), channel_id=1, source_target_pairs={{0,24},{1,25},{2,26},{3,27},{4,28},{5,29},{6,30},{7,31},{8,16},{9,... | collective-permute-start | bytes 49160 | tf_op jit(solution)/shard_map/ppermute | solution.py:273
  6.3 1.5 %collective-permute-start.4 = (f32[24,128]{1,0:T(8,128)S(1)}, f32[24,128]{1,0:T(8,128)S(1)}, u32[]{:S(2)}, u32[]{:S(2)}) collective-permute-start(f32[24,128]{1,0:T(8,128)S(1)} %get-tuple-element.20), channel_id=1, source_target_pairs={{0,4},{1,5},{2,6},{3,7},{4,0},{5,1},{6,2},{7,3},{8,12},{9,13},{10,... | collective-permute-start | bytes 36872 | tf_op jit(solution)/shard_map/ppermute | solution.py:273
  7.8 1.0 %collective-permute-start.2 = (f32[8,256]{1,0:T(8,128)S(1)}, f32[8,256]{1,0:T(8,128)S(1)}, u32[]{:S(2)}, u32[]{:S(2)}) collective-permute-start(f32[8,256]{1,0:T(8,128)S(1)} %get-tuple-element.18), channel_id=1, source_target_pairs={{0,8},{1,9},{2,10},{3,11},{4,12},{5,13},{6,14},{7,15},{8,0},{9,1},... | collective-permute-start | bytes 24584 | tf_op jit(solution)/shard_map/ppermute | solution.py:273
  8.8 0.0 copy-done.3
  8.8 0.0 copy-done.4
  8.8 0.0 copy-done.2
  8.8 0.0 copy-done.1
  8.8 1.1 %weights.1 = (f32[3,8,64,256]{3,2,1,0:T(8,128)S(1)}, f32[64,256]{1,0:T(8,128)S(1)}, f32[16,256]{1,0:T(8,128)S(1)}) custom-call(s32[1,1,4]{2,1,0:T(1,128)S(1)} %copy-done.3, f32[8,64,256]{2,1,0:T(8,128)S(1)} %copy-done, s32[8,64,256]{2,1,0:T(8,128)S(1)} %copy-done.1, bf16[3,256]{1,0:T(4,128)(2,1)S(1)} %copy-done.2, bf16[256]{0:T(256)(128)(2,1)S(1)} %copy-done.4), custom_call_target="tpu_custom_call" | custom-call | tf_op jit(solution)/shard_map/weights/pallas_call | solution.py:310
  9.9 0.0 collective-permute-done.2.refs_2_
  9.9 0.1 collective-permute-done.4.refs_4_
  10.0 0.0 collective-permute-done.3.refs_3_
  10.0 0.0 collective-permute-done.refs_0_
  10.0 0.0 collective-permute-done.1.refs_1_
  10.0 0.3 %shade.4 = f32[4,16,256]{2,1,0:T(8,128)S(1)} custom-call(f32[8,64,256]{2,1,0:T(8,128)S(1)} %copy-done, f32[3,8,64,256]{3,2,1,0:T(8,128)S(1)} %get-tuple-element.14.weighted, f32[64,256]{1,0:T(8,128)S(1)} %get-tuple-element.15.depth_in, f32[64,256]{1,0:T(8,128)S(1)} %collective-permute-done.refs_0_, f32[72,256]{1,0:T(8,128)S(1)} %collective-permute-done.1.refs_1_, ...), custom_call_target="tpu_custom_call" | custom-call | tf_op jit(solution)/shard_map/shade/pallas_call | solution.py:316
  10.3 0.5 %collective-permute-start.5 = (f32[4,16,256]{2,1,0:T(8,128)S(1)}, f32[4,16,256]{2,1,0:T(8,128)S(1)}, u32[]{:S(2)}, u32[]{:S(2)}) collective-permute-start(f32[4,16,256]{2,1,0:T(8,128)S(1)} %shade.4), channel_id=1, source_target_pairs={{0,1},{1,2},{2,3},{3,0},{4,5},{5,6},{6,7},{7,4},{8,10},{9,11},{10,... | collective-permute-start | bytes 196616 | tf_op jit(solution)/shard_map/ppermute | solution.py:326
  10.7 0.3 %shade.5 = f32[4,16,256]{2,1,0:T(8,128)S(1)} custom-call(f32[8,64,256]{2,1,0:T(8,128)S(1)} %copy-done, f32[3,8,64,256]{3,2,1,0:T(8,128)S(1)} %get-tuple-element.14.weighted, f32[64,256]{1,0:T(8,128)S(1)} %get-tuple-element.15.depth_in, f32[64,256]{1,0:T(8,128)S(1)} %collective-permute-done.refs_0_, f32[72,256]{1,0:T(8,128)S(1)} %collective-permute-done.1.refs_1_, ...), custom_call_target="tpu_custom_call" | custom-call | tf_op jit(solution)/shard_map/shade/pallas_call | solution.py:316
  11.0 2.0 %collective-permute-start.6 = (f32[4,16,256]{2,1,0:T(8,128)S(1)}, f32[4,16,256]{2,1,0:T(8,128)S(1)}, u32[]{:S(2)}, u32[]{:S(2)}) collective-permute-start(f32[4,16,256]{2,1,0:T(8,128)S(1)} %shade.5), channel_id=1, source_target_pairs={{0,2},{1,3},{2,0},{3,1},{4,6},{5,7},{6,4},{7,5},{8,11},{9,8},{10,9... | collective-permute-start | bytes 196616 | tf_op jit(solution)/shard_map/ppermute | solution.py:326
  13.0 0.3 %shade.6 = f32[4,16,256]{2,1,0:T(8,128)S(1)} custom-call(f32[8,64,256]{2,1,0:T(8,128)S(1)} %copy-done, f32[3,8,64,256]{3,2,1,0:T(8,128)S(1)} %get-tuple-element.14.weighted, f32[64,256]{1,0:T(8,128)S(1)} %get-tuple-element.15.depth_in, f32[64,256]{1,0:T(8,128)S(1)} %collective-permute-done.refs_0_, f32[72,256]{1,0:T(8,128)S(1)} %collective-permute-done.1.refs_1_, ...), custom_call_target="tpu_custom_call" | custom-call | tf_op jit(solution)/shard_map/shade/pallas_call | solution.py:316
  13.3 2.6 %collective-permute-start.7 = (f32[4,16,256]{2,1,0:T(8,128)S(1)}, f32[4,16,256]{2,1,0:T(8,128)S(1)}, u32[]{:S(2)}, u32[]{:S(2)}) collective-permute-start(f32[4,16,256]{2,1,0:T(8,128)S(1)} %shade.6), channel_id=1, source_target_pairs={{0,3},{1,0},{2,1},{3,2},{4,7},{5,4},{6,5},{7,6},{8,9},{9,10},{10,1... | collective-permute-start | bytes 196616 | tf_op jit(solution)/shard_map/ppermute | solution.py:326
  15.9 0.3 %shade.7.refs_3_ = f32[4,16,256]{2,1,0:T(8,128)S(1)} custom-call(f32[8,64,256]{2,1,0:T(8,128)S(1)} %copy-done, f32[3,8,64,256]{3,2,1,0:T(8,128)S(1)} %get-tuple-element.14.weighted, f32[64,256]{1,0:T(8,128)S(1)} %get-tuple-element.15.depth_in, f32[64,256]{1,0:T(8,128)S(1)} %collective-permute-done.refs_0_, f32[72,256]{1,0:T(8,128)S(1)} %collective-permute-done.1.refs_1_, ...), custom_call_target="tpu_custom_call" | custom-call | tf_op jit(solution)/shard_map/shade/pallas_call | solution.py:316
  16.2 0.8 %collective-permute-done.5.refs_0_ = f32[4,16,256]{2,1,0:T(8,128)S(1)} collective-permute-done((f32[4,16,256]{2,1,0:T(8,128)S(1)}, f32[4,16,256]{2,1,0:T(8,128)S(1)}, u32[]{:S(2)}, u32[]{:S(2)}) %collective-permute-start.5) | collective-permute-done | bytes 65568 | tf_op jit(solution)/shard_map/ppermute | solution.py:326
  17.0 1.3 %collective-permute-done.6.refs_1_ = f32[4,16,256]{2,1,0:T(8,128)S(1)} collective-permute-done((f32[4,16,256]{2,1,0:T(8,128)S(1)}, f32[4,16,256]{2,1,0:T(8,128)S(1)}, u32[]{:S(2)}, u32[]{:S(2)}) %collective-permute-start.6) | collective-permute-done | bytes 65568 | tf_op jit(solution)/shard_map/ppermute | solution.py:326
  18.3 0.0 collective-permute-done.7.refs_2_
  18.3 0.7 %compose.1 = f32[4,16,256]{2,1,0:T(8,128)} custom-call(f32[16,256]{1,0:T(8,128)S(1)} %get-tuple-element.13.earlier, f32[4,16,256]{2,1,0:T(8,128)S(1)} %collective-permute-done.5.refs_0_, f32[4,16,256]{2,1,0:T(8,128)S(1)} %collective-permute-done.6.refs_1_, f32[4,16,256]{2,1,0:T(8,128)S(1)} %collective-permute-done.7.refs_2_, f32[4,16,256]{2,1,0:T(8,128)S(1)} %shade.7.refs_3_), custom_call_target="tpu_custom_call" | custom-call | tf_op jit(solution)/shard_map/compose/pallas_call | solution.py:332
  (2 shorter events, 0.0 us)
Async XLA Ops:
  0.0 5.7 %copy-start = (f32[8,64,256]{2,1,0:T(8,128)S(1)}, f32[8,64,256]{2,1,0:T(8,128)}, u32[]{:S(2)}) copy-start(f32[8,64,256]{2,1,0:T(8,128)} %density_ref.13) | copy-start | bytes 1572868
  0.0 8.7 %copy-start.3 = (s32[1,1,4]{2,1,0:T(1,128)S(1)}, s32[1,1,4]{2,1,0:T(1,128)}, u32[]{:S(2)}) copy-start(s32[1,1,4]{2,1,0:T(1,128)} %order_ref.1) | copy-start | bytes 52
  0.0 8.8 %copy-start.4 = (bf16[256]{0:T(256)(128)(2,1)S(1)}, bf16[256]{0:T(256)(128)(2,1)}, u32[]{:S(2)}) copy-start(bf16[256]{0:T(256)(128)(2,1)} %opacity_ref.1) | copy-start | bytes 1540
  0.0 8.8 %copy-start.2 = (bf16[3,256]{1,0:T(4,128)(2,1)S(1)}, bf16[3,256]{1,0:T(4,128)(2,1)}, u32[]{:S(2)}) copy-start(bf16[3,256]{1,0:T(4,128)(2,1)} %colour_ref.1) | copy-start | bytes 4612
  0.0 8.8 %copy-start.1 = (s32[8,64,256]{2,1,0:T(8,128)S(1)}, s32[8,64,256]{2,1,0:T(8,128)}, u32[]{:S(2)}) copy-start(s32[8,64,256]{2,1,0:T(8,128)} %bins_ref.1) | copy-start | bytes 1572868
  1.0 9.0 %collective-permute-start.1 = (f32[72,256]{1,0:T(8,128)S(1)}, f32[72,256]{1,0:T(8,128)S(1)}, u32[]{:S(2)}, u32[]{:S(2)}) collective-permute-start(f32[72,256]{1,0:T(8,128)S(1)} %get-tuple-element.17), channel_id=1, source_target_pairs={{0,8},{1,2},{2,1},{3,11},{4,12},{5,6},{6,5},{7,15},{8,0},{9,10},{1... | collective-permute-start | bytes 221192 | tf_op jit(solution)/shard_map/ppermute | solution.py:273
  1.5 8.4 %collective-permute-start = (f32[64,256]{1,0:T(8,128)S(1)}, f32[64,256]{1,0:T(8,128)S(1)}, u32[]{:S(2)}, u32[]{:S(2)}) collective-permute-start(f32[64,256]{1,0:T(8,128)S(1)} %get-tuple-element.16), channel_id=1, source_target_pairs={{0,1},{1,0},{2,3},{3,2},{4,5},{5,4},{6,7},{7,6},{8,9},{9,8},{10,11... | collective-permute-start | bytes 196616 | tf_op jit(solution)/shard_map/ppermute | solution.py:273
  5.8 4.1 %collective-permute-start.3 = (f32[16,256]{1,0:T(8,128)S(1)}, f32[16,256]{1,0:T(8,128)S(1)}, u32[]{:S(2)}, u32[]{:S(2)}) collective-permute-start(f32[16,256]{1,0:T(8,128)S(1)} %get-tuple-element.19), channel_id=1, source_target_pairs={{0,24},{1,25},{2,26},{3,27},{4,28},{5,29},{6,30},{7,31},{8,16},{9,... | collective-permute-start | bytes 49160 | tf_op jit(solution)/shard_map/ppermute | solution.py:273
  6.3 3.7 %collective-permute-start.4 = (f32[24,128]{1,0:T(8,128)S(1)}, f32[24,128]{1,0:T(8,128)S(1)}, u32[]{:S(2)}, u32[]{:S(2)}) collective-permute-start(f32[24,128]{1,0:T(8,128)S(1)} %get-tuple-element.20), channel_id=1, source_target_pairs={{0,4},{1,5},{2,6},{3,7},{4,0},{5,1},{6,2},{7,3},{8,12},{9,13},{10,... | collective-permute-start | bytes 36872 | tf_op jit(solution)/shard_map/ppermute | solution.py:273
  7.8 2.1 %collective-permute-start.2 = (f32[8,256]{1,0:T(8,128)S(1)}, f32[8,256]{1,0:T(8,128)S(1)}, u32[]{:S(2)}, u32[]{:S(2)}) collective-permute-start(f32[8,256]{1,0:T(8,128)S(1)} %get-tuple-element.18), channel_id=1, source_target_pairs={{0,8},{1,9},{2,10},{3,11},{4,12},{5,13},{6,14},{7,15},{8,0},{9,1},... | collective-permute-start | bytes 24584 | tf_op jit(solution)/shard_map/ppermute | solution.py:273
  10.3 6.7 %collective-permute-start.5 = (f32[4,16,256]{2,1,0:T(8,128)S(1)}, f32[4,16,256]{2,1,0:T(8,128)S(1)}, u32[]{:S(2)}, u32[]{:S(2)}) collective-permute-start(f32[4,16,256]{2,1,0:T(8,128)S(1)} %shade.4), channel_id=1, source_target_pairs={{0,1},{1,2},{2,3},{3,0},{4,5},{5,6},{6,7},{7,4},{8,10},{9,11},{10,... | collective-permute-start | bytes 196616 | tf_op jit(solution)/shard_map/ppermute | solution.py:326
  11.0 7.3 %collective-permute-start.6 = (f32[4,16,256]{2,1,0:T(8,128)S(1)}, f32[4,16,256]{2,1,0:T(8,128)S(1)}, u32[]{:S(2)}, u32[]{:S(2)}) collective-permute-start(f32[4,16,256]{2,1,0:T(8,128)S(1)} %shade.5), channel_id=1, source_target_pairs={{0,2},{1,3},{2,0},{3,1},{4,6},{5,7},{6,4},{7,5},{8,11},{9,8},{10,9... | collective-permute-start | bytes 196616 | tf_op jit(solution)/shard_map/ppermute | solution.py:326
  13.3 5.0 %collective-permute-start.7 = (f32[4,16,256]{2,1,0:T(8,128)S(1)}, f32[4,16,256]{2,1,0:T(8,128)S(1)}, u32[]{:S(2)}, u32[]{:S(2)}) collective-permute-start(f32[4,16,256]{2,1,0:T(8,128)S(1)} %shade.6), channel_id=1, source_target_pairs={{0,3},{1,0},{2,1},{3,2},{4,7},{5,4},{6,5},{7,6},{8,9},{9,10},{10,1... | collective-permute-start | bytes 196616 | tf_op jit(solution)/shard_map/ppermute | solution.py:326

commit v6 on v5

--- a/solution.py
+++ b/solution.py
@@ -50,10 +50,14 @@
 def depth_faces_kernel(density_ref, z_a, z_b, sems):
     last = density_ref.shape[0] - 1
     even = lax.axis_index("gz") % 2 == 0
-    copies = [
-        pltpu.make_async_copy(density_ref.at[jnp.where(even, last, 0)], z_a, sems.at[0]),
-        pltpu.make_async_copy(density_ref.at[jnp.where(even, 0, last)], z_b.at[: z_a.shape[0]], sems.at[1]),
-    ]
+    half = density_ref.shape[1] // 2
+    copies = []
+    for out, plane in ((z_b, jnp.where(even, 0, last)), (z_a, jnp.where(even, last, 0))):
+        for i in range(2):
+            here = pl.ds(i * half, half)
+            copies.append(
+                pltpu.make_async_copy(density_ref.at[plane, here], out.at[here], sems.at[len(copies)])
+            )
     for copy in copies:
         copy.start()
     for copy in copies:
@@ -181,14 +185,9 @@
         )
         top, bottom = tile == 0, tile == end
         to, lane0 = y_place(depth, tile)
-        turn = (LANES - lane0 - jnp.where(even_y, 1, 0)) % LANES
         y_rows = pl.ds(pl.multiple_of(to, SUBLANES), SUBLANES)
-        y_before = y_after = pltpu.roll(y_a[y_rows, :], turn, 1)
-        if len(halos) == 6:
-            second = pltpu.roll(halos[5][y_rows, :], turn, 1)
-            y_before = jnp.where(even_y, second, y_before)
-            y_after = jnp.where(even_y, y_after, second)
-        y_before, y_after = jnp.where(first_y, 0.0, y_before), jnp.where(last_y, 0.0, y_after)
+        y_halos = [y[y_rows, :] for y in (y_a, *halos[5:])]
+        y_lane = jnp.full((SUBLANES, LANES), lane0 + jnp.where(even_y, 1, 0), jnp.int32)
         plane = [
             jnp.where(first_z, 0.0, jnp.where(even_z, z_b[here, at], z_a[here, at])) for at in cuts
         ]
@@ -199,11 +198,20 @@
         sums = [[jnp.zeros((SUBLANES, LANES), jnp.float32) for _ in range(3)] for _ in cuts]
         for z in range(depth):
             following = [density_ref[z + 1, here, at] for at in cuts] if z + 1 < depth else after
+            edges = [
+                jnp.take_along_axis(y, y_lane + z, axis=1, mode="promise_in_bounds")
+                for y in y_halos
+            ]
+            y_before = y_after = edges[0]
+            if len(edges) == 2:
+                y_before = jnp.where(even_y, edges[1], edges[0])
+                y_after = jnp.where(even_y, edges[0], edges[1])
+            y_before, y_after = jnp.where(first_y, 0.0, y_before), jnp.where(last_y, 0.0, y_after)
             right = [pltpu.roll(v, 1, 1) for v in current]
             left = [pltpu.roll(v, LANES - 1, 1) for v in current]
             for p, at in enumerate(cuts):
-                low = right[p - 1] if p > 0 else y_before[:, z : z + 1]
-                high = left[p + 1] if p + 1 < len(cuts) else y_after[:, z : z + 1]
+                low = right[p - 1] if p > 0 else y_before
+                high = left[p + 1] if p + 1 < len(cuts) else y_after
                 slope_row = jnp.where(lane == LANES - 1, high, left[p]) - jnp.where(
                     lane == 0, low, right[p]
                 )
@@ -289,7 +297,7 @@
     y_sides = 1 if lax.axis_size("gy") == 2 else 2
     z_faces = call(
         depth_faces_kernel, "depth_faces", [near(columns, rows), near(columns + SUBLANES, rows)], [HBM],
-        scratch_shapes=[pltpu.SemaphoreType.DMA((2,))],
+        scratch_shapes=[pltpu.SemaphoreType.DMA((4,))],
         cost_estimate=pl.CostEstimate(flops=2 * 10**9, bytes_accessed=2 * 10**6, transcendentals=0),
     )(*far(density))
     density, bins, order, colour_table, opacity_table = here(

time: 19.2 us -> 19.1 us (level)
  waiting for transfers between devices: 2.21 us -> 2.51 us
  Pallas kernels: 4.03 us -> 3.76 us
    ppermute x3, waiting for transfers between devices: 2.1 us -> 2.4 us  [local(): part = lax.ppermute(part, AXES, shifted(shift))]
    pallas_call x4, Pallas kernels: 1.13 us -> 0.91 us  [local(): call(functools.partial(shade_kernel, part), 'shade', near(4, tile, rows),...]
  transfers between devices with their start and end apart: 8 -> 8, of which waited for: 3 -> 3; matrix products, arithmetic and copies ran while one was open for 0% -> 0% of each run, Pallas kernels for 11% -> 10%
where the time goes in v6:
time: 19.1 us; the launch traced here: 19 us
  starting transfers between devices  12.7 us (66%)
  Pallas kernels  3.76 us (20%)
  waiting for transfers between devices  2.51 us (13%)
    ppermute x5, starting transfers between devices, swap(): got.append(lax.ppermute(value, AXES, pairs))  7.59 us
    ppermute x3, starting transfers between devices, local(): part = lax.ppermute(part, AXES, shifted(shift))  5.06 us
    ppermute x3, waiting for transfers between devices, local(): part = lax.ppermute(part, AXES, shifted(shift))  2.4 us
    pallas_call x1, Pallas kernels, local(): call(functools.partial(weights_kernel, step, shifts), 'weights', [near(3,...  1.1 us
    pallas_call x1, Pallas kernels, local(): call(depth_faces_kernel, 'depth_faces', [near(columns, rows), near(column...  0.94 us
    pallas_call x4, Pallas kernels, local(): call(functools.partial(shade_kernel, part), 'shade', near(4, tile, rows),...  0.91 us
    pallas_call x1, Pallas kernels, local(): call(functools.partial(compose_kernel, bricks), 'compose', jax.ShapeDtype...  0.68 us
  transfers between devices with their start and end apart: 8, of which 3 were waited for; matrix products, arithmetic and copies ran while one was open for 0% of the time, Pallas kernels for 10%

profile of v6, /device:TPU:0, one launch (start us, length us, event | category | flops | bytes accessed | tf_op | source)
XLA Modules:
  0.0 19.0 jit_solution(7461205811017955001)
XLA Ops:
  0.0 0.0 copy-start
  0.0 0.0 copy-start.3
  0.0 0.0 copy-start.4
  0.0 0.9 %depth_faces.1 = (f32[64,256]{1,0:T(8,128)S(1)}, f32[72,256]{1,0:T(8,128)S(1)}) custom-call(f32[8,64,256]{2,1,0:T(8,128)} %density_ref.13), custom_call_target="tpu_custom_call" | custom-call | flops 2000000000 | bytes 2000000 | tf_op jit(solution)/shard_map/depth_faces/pallas_call | solution.py:298
  1.0 0.5 %collective-permute-start.1 = (f32[72,256]{1,0:T(8,128)S(1)}, f32[72,256]{1,0:T(8,128)S(1)}, u32[]{:S(2)}, u32[]{:S(2)}) collective-permute-start(f32[72,256]{1,0:T(8,128)S(1)} %get-tuple-element.17), channel_id=1, source_target_pairs={{0,8},{1,2},{2,1},{3,11},{4,12},{5,6},{6,5},{7,15},{8,0},{9,10},{1... | collective-permute-start | bytes 221192 | tf_op jit(solution)/shard_map/ppermute | solution.py:281
  1.5 4.1 %collective-permute-start = (f32[64,256]{1,0:T(8,128)S(1)}, f32[64,256]{1,0:T(8,128)S(1)}, u32[]{:S(2)}, u32[]{:S(2)}) collective-permute-start(f32[64,256]{1,0:T(8,128)S(1)} %get-tuple-element.16), channel_id=1, source_target_pairs={{0,1},{1,0},{2,3},{3,2},{4,5},{5,4},{6,7},{7,6},{8,9},{9,8},{10,11... | collective-permute-start | bytes 196616 | tf_op jit(solution)/shard_map/ppermute | solution.py:281
  5.6 0.0 copy-done
  5.6 0.1 side_faces.1
  5.8 0.4 %collective-permute-start.3 = (f32[16,256]{1,0:T(8,128)S(1)}, f32[16,256]{1,0:T(8,128)S(1)}, u32[]{:S(2)}, u32[]{:S(2)}) collective-permute-start(f32[16,256]{1,0:T(8,128)S(1)} %get-tuple-element.19), channel_id=1, source_target_pairs={{0,24},{1,25},{2,26},{3,27},{4,28},{5,29},{6,30},{7,31},{8,16},{9,... | collective-permute-start | bytes 49160 | tf_op jit(solution)/shard_map/ppermute | solution.py:281
  6.2 1.5 %collective-permute-start.4 = (f32[24,128]{1,0:T(8,128)S(1)}, f32[24,128]{1,0:T(8,128)S(1)}, u32[]{:S(2)}, u32[]{:S(2)}) collective-permute-start(f32[24,128]{1,0:T(8,128)S(1)} %get-tuple-element.20), channel_id=1, source_target_pairs={{0,4},{1,5},{2,6},{3,7},{4,0},{5,1},{6,2},{7,3},{8,12},{9,13},{10,... | collective-permute-start | bytes 36872 | tf_op jit(solution)/shard_map/ppermute | solution.py:281
  7.7 1.0 %collective-permute-start.2 = (f32[8,256]{1,0:T(8,128)S(1)}, f32[8,256]{1,0:T(8,128)S(1)}, u32[]{:S(2)}, u32[]{:S(2)}) collective-permute-start(f32[8,256]{1,0:T(8,128)S(1)} %get-tuple-element.18), channel_id=1, source_target_pairs={{0,8},{1,9},{2,10},{3,11},{4,12},{5,13},{6,14},{7,15},{8,0},{9,1},... | collective-permute-start | bytes 24584 | tf_op jit(solution)/shard_map/ppermute | solution.py:281
  8.7 0.0 copy-done.3
  8.7 0.0 copy-done.4
  8.7 0.0 copy-done.2
  8.7 0.0 copy-done.1
  8.7 1.1 %weights.1 = (f32[3,8,64,256]{3,2,1,0:T(8,128)S(1)}, f32[64,256]{1,0:T(8,128)S(1)}, f32[16,256]{1,0:T(8,128)S(1)}) custom-call(s32[1,1,4]{2,1,0:T(1,128)S(1)} %copy-done.3, f32[8,64,256]{2,1,0:T(8,128)S(1)} %copy-done, s32[8,64,256]{2,1,0:T(8,128)S(1)} %copy-done.1, bf16[3,256]{1,0:T(4,128)(2,1)S(1)} %copy-done.2, bf16[256]{0:T(256)(128)(2,1)S(1)} %copy-done.4), custom_call_target="tpu_custom_call" | custom-call | tf_op jit(solution)/shard_map/weights/pallas_call | solution.py:318
  9.8 0.0 collective-permute-done.2.refs_2_
  9.8 0.1 collective-permute-done.4.refs_4_
  9.9 0.0 collective-permute-done.3.refs_3_
  9.9 0.0 collective-permute-done.refs_0_
  9.9 0.0 collective-permute-done.1.refs_1_
  9.9 0.2 %shade.4 = f32[4,16,256]{2,1,0:T(8,128)S(1)} custom-call(f32[8,64,256]{2,1,0:T(8,128)S(1)} %copy-done, f32[3,8,64,256]{3,2,1,0:T(8,128)S(1)} %get-tuple-element.14.weighted, f32[64,256]{1,0:T(8,128)S(1)} %get-tuple-element.15.depth_in, f32[64,256]{1,0:T(8,128)S(1)} %collective-permute-done.refs_0_, f32[72,256]{1,0:T(8,128)S(1)} %collective-permute-done.1.refs_1_, ...), custom_call_target="tpu_custom_call" | custom-call | tf_op jit(solution)/shard_map/shade/pallas_call | solution.py:324
  10.2 0.5 %collective-permute-start.5 = (f32[4,16,256]{2,1,0:T(8,128)S(1)}, f32[4,16,256]{2,1,0:T(8,128)S(1)}, u32[]{:S(2)}, u32[]{:S(2)}) collective-permute-start(f32[4,16,256]{2,1,0:T(8,128)S(1)} %shade.4), channel_id=1, source_target_pairs={{0,1},{1,2},{2,3},{3,0},{4,5},{5,6},{6,7},{7,4},{8,10},{9,11},{10,... | collective-permute-start | bytes 196616 | tf_op jit(solution)/shard_map/ppermute | solution.py:334
  10.6 0.2 %shade.5 = f32[4,16,256]{2,1,0:T(8,128)S(1)} custom-call(f32[8,64,256]{2,1,0:T(8,128)S(1)} %copy-done, f32[3,8,64,256]{3,2,1,0:T(8,128)S(1)} %get-tuple-element.14.weighted, f32[64,256]{1,0:T(8,128)S(1)} %get-tuple-element.15.depth_in, f32[64,256]{1,0:T(8,128)S(1)} %collective-permute-done.refs_0_, f32[72,256]{1,0:T(8,128)S(1)} %collective-permute-done.1.refs_1_, ...), custom_call_target="tpu_custom_call" | custom-call | tf_op jit(solution)/shard_map/shade/pallas_call | solution.py:324
  10.9 2.0 %collective-permute-start.6 = (f32[4,16,256]{2,1,0:T(8,128)S(1)}, f32[4,16,256]{2,1,0:T(8,128)S(1)}, u32[]{:S(2)}, u32[]{:S(2)}) collective-permute-start(f32[4,16,256]{2,1,0:T(8,128)S(1)} %shade.5), channel_id=1, source_target_pairs={{0,2},{1,3},{2,0},{3,1},{4,6},{5,7},{6,4},{7,5},{8,11},{9,8},{10,9... | collective-permute-start | bytes 196616 | tf_op jit(solution)/shard_map/ppermute | solution.py:334
  12.8 0.2 %shade.6 = f32[4,16,256]{2,1,0:T(8,128)S(1)} custom-call(f32[8,64,256]{2,1,0:T(8,128)S(1)} %copy-done, f32[3,8,64,256]{3,2,1,0:T(8,128)S(1)} %get-tuple-element.14.weighted, f32[64,256]{1,0:T(8,128)S(1)} %get-tuple-element.15.depth_in, f32[64,256]{1,0:T(8,128)S(1)} %collective-permute-done.refs_0_, f32[72,256]{1,0:T(8,128)S(1)} %collective-permute-done.1.refs_1_, ...), custom_call_target="tpu_custom_call" | custom-call | tf_op jit(solution)/shard_map/shade/pallas_call | solution.py:324
  13.1 2.7 %collective-permute-start.7 = (f32[4,16,256]{2,1,0:T(8,128)S(1)}, f32[4,16,256]{2,1,0:T(8,128)S(1)}, u32[]{:S(2)}, u32[]{:S(2)}) collective-permute-start(f32[4,16,256]{2,1,0:T(8,128)S(1)} %shade.6), channel_id=1, source_target_pairs={{0,3},{1,0},{2,1},{3,2},{4,7},{5,4},{6,5},{7,6},{8,9},{9,10},{10,1... | collective-permute-start | bytes 196616 | tf_op jit(solution)/shard_map/ppermute | solution.py:334
  15.7 0.2 %shade.7.refs_3_ = f32[4,16,256]{2,1,0:T(8,128)S(1)} custom-call(f32[8,64,256]{2,1,0:T(8,128)S(1)} %copy-done, f32[3,8,64,256]{3,2,1,0:T(8,128)S(1)} %get-tuple-element.14.weighted, f32[64,256]{1,0:T(8,128)S(1)} %get-tuple-element.15.depth_in, f32[64,256]{1,0:T(8,128)S(1)} %collective-permute-done.refs_0_, f32[72,256]{1,0:T(8,128)S(1)} %collective-permute-done.1.refs_1_, ...), custom_call_target="tpu_custom_call" | custom-call | tf_op jit(solution)/shard_map/shade/pallas_call | solution.py:324
  15.9 0.9 %collective-permute-done.5.refs_0_ = f32[4,16,256]{2,1,0:T(8,128)S(1)} collective-permute-done((f32[4,16,256]{2,1,0:T(8,128)S(1)}, f32[4,16,256]{2,1,0:T(8,128)S(1)}, u32[]{:S(2)}, u32[]{:S(2)}) %collective-permute-start.5) | collective-permute-done | bytes 65568 | tf_op jit(solution)/shard_map/ppermute | solution.py:334
  16.8 1.5 %collective-permute-done.6.refs_1_ = f32[4,16,256]{2,1,0:T(8,128)S(1)} collective-permute-done((f32[4,16,256]{2,1,0:T(8,128)S(1)}, f32[4,16,256]{2,1,0:T(8,128)S(1)}, u32[]{:S(2)}, u32[]{:S(2)}) %collective-permute-start.6) | collective-permute-done | bytes 65568 | tf_op jit(solution)/shard_map/ppermute | solution.py:334
  18.3 0.0 collective-permute-done.7.refs_2_
  18.3 0.7 %compose.1 = f32[4,16,256]{2,1,0:T(8,128)} custom-call(f32[16,256]{1,0:T(8,128)S(1)} %get-tuple-element.13.earlier, f32[4,16,256]{2,1,0:T(8,128)S(1)} %collective-permute-done.5.refs_0_, f32[4,16,256]{2,1,0:T(8,128)S(1)} %collective-permute-done.6.refs_1_, f32[4,16,256]{2,1,0:T(8,128)S(1)} %collective-permute-done.7.refs_2_, f32[4,16,256]{2,1,0:T(8,128)S(1)} %shade.7.refs_3_), custom_call_target="tpu_custom_call" | custom-call | tf_op jit(solution)/shard_map/compose/pallas_call | solution.py:340
  (2 shorter events, 0.0 us)
Async XLA Ops:
  0.0 5.6 %copy-start = (f32[8,64,256]{2,1,0:T(8,128)S(1)}, f32[8,64,256]{2,1,0:T(8,128)}, u32[]{:S(2)}) copy-start(f32[8,64,256]{2,1,0:T(8,128)} %density_ref.13) | copy-start | bytes 1572868
  0.0 8.7 %copy-start.3 = (s32[1,1,4]{2,1,0:T(1,128)S(1)}, s32[1,1,4]{2,1,0:T(1,128)}, u32[]{:S(2)}) copy-start(s32[1,1,4]{2,1,0:T(1,128)} %order_ref.1) | copy-start | bytes 52
  0.0 8.7 %copy-start.4 = (bf16[256]{0:T(256)(128)(2,1)S(1)}, bf16[256]{0:T(256)(128)(2,1)}, u32[]{:S(2)}) copy-start(bf16[256]{0:T(256)(128)(2,1)} %opacity_ref.1) | copy-start | bytes 1540
  0.0 8.7 %copy-start.2 = (bf16[3,256]{1,0:T(4,128)(2,1)S(1)}, bf16[3,256]{1,0:T(4,128)(2,1)}, u32[]{:S(2)}) copy-start(bf16[3,256]{1,0:T(4,128)(2,1)} %colour_ref.1) | copy-start | bytes 4612
  0.0 8.7 %copy-start.1 = (s32[8,64,256]{2,1,0:T(8,128)S(1)}, s32[8,64,256]{2,1,0:T(8,128)}, u32[]{:S(2)}) copy-start(s32[8,64,256]{2,1,0:T(8,128)} %bins_ref.1) | copy-start | bytes 1572868
  1.0 9.0 %collective-permute-start.1 = (f32[72,256]{1,0:T(8,128)S(1)}, f32[72,256]{1,0:T(8,128)S(1)}, u32[]{:S(2)}, u32[]{:S(2)}) collective-permute-start(f32[72,256]{1,0:T(8,128)S(1)} %get-tuple-element.17), channel_id=1, source_target_pairs={{0,8},{1,2},{2,1},{3,11},{4,12},{5,6},{6,5},{7,15},{8,0},{9,10},{1... | collective-permute-start | bytes 221192 | tf_op jit(solution)/shard_map/ppermute | solution.py:281
  1.5 8.4 %collective-permute-start = (f32[64,256]{1,0:T(8,128)S(1)}, f32[64,256]{1,0:T(8,128)S(1)}, u32[]{:S(2)}, u32[]{:S(2)}) collective-permute-start(f32[64,256]{1,0:T(8,128)S(1)} %get-tuple-element.16), channel_id=1, source_target_pairs={{0,1},{1,0},{2,3},{3,2},{4,5},{5,4},{6,7},{7,6},{8,9},{9,8},{10,11... | collective-permute-start | bytes 196616 | tf_op jit(solution)/shard_map/ppermute | solution.py:281
  5.8 4.1 %collective-permute-start.3 = (f32[16,256]{1,0:T(8,128)S(1)}, f32[16,256]{1,0:T(8,128)S(1)}, u32[]{:S(2)}, u32[]{:S(2)}) collective-permute-start(f32[16,256]{1,0:T(8,128)S(1)} %get-tuple-element.19), channel_id=1, source_target_pairs={{0,24},{1,25},{2,26},{3,27},{4,28},{5,29},{6,30},{7,31},{8,16},{9,... | collective-permute-start | bytes 49160 | tf_op jit(solution)/shard_map/ppermute | solution.py:281
  6.2 3.7 %collective-permute-start.4 = (f32[24,128]{1,0:T(8,128)S(1)}, f32[24,128]{1,0:T(8,128)S(1)}, u32[]{:S(2)}, u32[]{:S(2)}) collective-permute-start(f32[24,128]{1,0:T(8,128)S(1)} %get-tuple-element.20), channel_id=1, source_target_pairs={{0,4},{1,5},{2,6},{3,7},{4,0},{5,1},{6,2},{7,3},{8,12},{9,13},{10,... | collective-permute-start | bytes 36872 | tf_op jit(solution)/shard_map/ppermute | solution.py:281
  7.7 2.1 %collective-permute-start.2 = (f32[8,256]{1,0:T(8,128)S(1)}, f32[8,256]{1,0:T(8,128)S(1)}, u32[]{:S(2)}, u32[]{:S(2)}) collective-permute-start(f32[8,256]{1,0:T(8,128)S(1)} %get-tuple-element.18), channel_id=1, source_target_pairs={{0,8},{1,9},{2,10},{3,11},{4,12},{5,13},{6,14},{7,15},{8,0},{9,1},... | collective-permute-start | bytes 24584 | tf_op jit(solution)/shard_map/ppermute | solution.py:281
  10.2 6.6 %collective-permute-start.5 = (f32[4,16,256]{2,1,0:T(8,128)S(1)}, f32[4,16,256]{2,1,0:T(8,128)S(1)}, u32[]{:S(2)}, u32[]{:S(2)}) collective-permute-start(f32[4,16,256]{2,1,0:T(8,128)S(1)} %shade.4), channel_id=1, source_target_pairs={{0,1},{1,2},{2,3},{3,0},{4,5},{5,6},{6,7},{7,4},{8,10},{9,11},{10,... | collective-permute-start | bytes 196616 | tf_op jit(solution)/shard_map/ppermute | solution.py:334
  10.9 7.5 %collective-permute-start.6 = (f32[4,16,256]{2,1,0:T(8,128)S(1)}, f32[4,16,256]{2,1,0:T(8,128)S(1)}, u32[]{:S(2)}, u32[]{:S(2)}) collective-permute-start(f32[4,16,256]{2,1,0:T(8,128)S(1)} %shade.5), channel_id=1, source_target_pairs={{0,2},{1,3},{2,0},{3,1},{4,6},{5,7},{6,4},{7,5},{8,11},{9,8},{10,9... | collective-permute-start | bytes 196616 | tf_op jit(solution)/shard_map/ppermute | solution.py:334
  13.1 5.3 %collective-permute-start.7 = (f32[4,16,256]{2,1,0:T(8,128)S(1)}, f32[4,16,256]{2,1,0:T(8,128)S(1)}, u32[]{:S(2)}, u32[]{:S(2)}) collective-permute-start(f32[4,16,256]{2,1,0:T(8,128)S(1)} %shade.6), channel_id=1, source_target_pairs={{0,3},{1,0},{2,1},{3,2},{4,7},{5,4},{6,5},{7,6},{8,9},{9,10},{10,1... | collective-permute-start | bytes 196616 | tf_op jit(solution)/shard_map/ppermute | solution.py:334

commit v7 on v6

--- a/solution.py
+++ b/solution.py
@@ -159,7 +159,7 @@
 
 def shade_kernel(part, density_ref, weighted, depth_in, *refs):
     halos, out, x_before, x_after = refs[:-3], refs[-3], refs[-2], refs[-1]
-    z_a, z_b, x_a, x_b, y_a = halos[:5]
+    z_a, z_b, *y_refs, x_a, x_b = halos
     depth, columns, rows = density_ref.shape
     even_x, even_y, even_z = evens()
     (first_x, last_x), (first_y, last_y), (first_z, last_z) = ends()
@@ -186,7 +186,7 @@
         top, bottom = tile == 0, tile == end
         to, lane0 = y_place(depth, tile)
         y_rows = pl.ds(pl.multiple_of(to, SUBLANES), SUBLANES)
-        y_halos = [y[y_rows, :] for y in (y_a, *halos[5:])]
+        y_halos = [y[y_rows, :] for y in y_refs]
         y_lane = jnp.full((SUBLANES, LANES), lane0 + jnp.where(even_y, 1, 0), jnp.int32)
         plane = [
             jnp.where(first_z, 0.0, jnp.where(even_z, z_b[here, at], z_a[here, at])) for at in cuts
@@ -296,7 +296,7 @@
     y_height, _ = y_shape(depth, columns)
     y_sides = 1 if lax.axis_size("gy") == 2 else 2
     z_faces = call(
-        depth_faces_kernel, "depth_faces", [near(columns, rows), near(columns + SUBLANES, rows)], [HBM],
+        depth_faces_kernel, "depth_faces", [near(columns + SUBLANES, rows), near(columns, rows)], [HBM],
         scratch_shapes=[pltpu.SemaphoreType.DMA((4,))],
         cost_estimate=pl.CostEstimate(flops=2 * 10**9, bytes_accessed=2 * 10**6, transcendentals=0),
     )(*far(density))
@@ -306,10 +306,12 @@
     side_faces = call(
         side_faces_kernel, "side_faces",
         [near(depth, rows), near(2 * depth, rows)]
-        + [near(y_height + 2 * SUBLANES, LANES)] * y_sides, [VMEM],
+        + [near(y_height + SUBLANES, LANES)] * y_sides, [VMEM],
+        cost_estimate=pl.CostEstimate(flops=7 * 10**8, bytes_accessed=2 * 10**6, transcendentals=0),
+
     )(density)
     faces = here(*z_faces, *side_faces)
-    halos = swap(faces[:2], "gz") + swap(faces[2:4], "gx") + swap(faces[4:], "gy")
+    halos = swap(faces[:2], "gz") + swap(faces[4:], "gy") + swap(faces[2:4], "gx")
 
     tile_rows = columns // bricks
     direct = tile_rows % SUBLANES == 0

time: 19.1 us -> 19.1 us (level)
  no operation moved by 1% of the time
where the time goes in v7:
time: 19.1 us; the launch traced here: 18.9 us
  starting transfers between devices  12.6 us (66%)
  Pallas kernels  3.71 us (19%)
  waiting for transfers between devices  2.44 us (13%)
    ppermute x5, starting transfers between devices, swap(): got.append(lax.ppermute(value, AXES, pairs))  7.58 us
    ppermute x3, starting transfers between devices, local(): part = lax.ppermute(part, AXES, shifted(shift))  5.06 us
    ppermute x3, waiting for transfers between devices, local(): part = lax.ppermute(part, AXES, shifted(shift))  2.36 us
    pallas_call x1, Pallas kernels, local(): call(functools.partial(weights_kernel, step, shifts), 'weights', [near(3,...  1.1 us
    pallas_call x4, Pallas kernels, local(): call(functools.partial(shade_kernel, part), 'shade', near(4, tile, rows),...  0.91 us
    pallas_call x1, Pallas kernels, local(): call(depth_faces_kernel, 'depth_faces', [near(columns + SUBLANES, rows),...  0.9 us
    pallas_call x1, Pallas kernels, local(): call(functools.partial(compose_kernel, bricks), 'compose', jax.ShapeDtype...  0.67 us
  transfers between devices with their start and end apart: 8, of which 3 were waited for; matrix products, arithmetic and copies ran while one was open for 0% of the time, Pallas kernels for 10%

profile of v7, /device:TPU:0, one launch (start us, length us, event | category | flops | bytes accessed | tf_op | source)
XLA Modules:
  0.0 18.9 jit_solution(14184459344047867815)
XLA Ops:
  0.0 0.9 %depth_faces.1 = (f32[72,256]{1,0:T(8,128)S(1)}, f32[64,256]{1,0:T(8,128)S(1)}) custom-call(f32[8,64,256]{2,1,0:T(8,128)} %density_ref.13), custom_call_target="tpu_custom_call" | custom-call | flops 2000000000 | bytes 2000000 | tf_op jit(solution)/shard_map/depth_faces/pallas_call | solution.py:298
  0.9 0.0 copy-start.1
  0.9 0.0 copy-start.2
  0.9 0.0 copy-start.3
  0.9 0.0 copy-start.4
  1.0 0.5 %collective-permute-start.1 = (f32[64,256]{1,0:T(8,128)S(1)}, f32[64,256]{1,0:T(8,128)S(1)}, u32[]{:S(2)}, u32[]{:S(2)}) collective-permute-start(f32[64,256]{1,0:T(8,128)S(1)} %get-tuple-element.17), channel_id=1, source_target_pairs={{0,8},{1,2},{2,1},{3,11},{4,12},{5,6},{6,5},{7,15},{8,0},{9,10},{1... | collective-permute-start | bytes 196616 | tf_op jit(solution)/shard_map/ppermute | solution.py:281
  1.5 4.1 %collective-permute-start = (f32[72,256]{1,0:T(8,128)S(1)}, f32[72,256]{1,0:T(8,128)S(1)}, u32[]{:S(2)}, u32[]{:S(2)}) collective-permute-start(f32[72,256]{1,0:T(8,128)S(1)} %get-tuple-element.16), channel_id=1, source_target_pairs={{0,1},{1,0},{2,3},{3,2},{4,5},{5,4},{6,7},{7,6},{8,9},{9,8},{10,11... | collective-permute-start | bytes 221192 | tf_op jit(solution)/shard_map/ppermute | solution.py:281
  5.6 0.0 copy-done
  5.6 0.1 side_faces.1
  5.8 0.4 %collective-permute-start.4 = (f32[16,256]{1,0:T(8,128)S(1)}, f32[16,256]{1,0:T(8,128)S(1)}, u32[]{:S(2)}, u32[]{:S(2)}) collective-permute-start(f32[16,256]{1,0:T(8,128)S(1)} %get-tuple-element.20), channel_id=1, source_target_pairs={{0,24},{1,25},{2,26},{3,27},{4,28},{5,29},{6,30},{7,31},{8,16},{9,... | collective-permute-start | bytes 49160 | tf_op jit(solution)/shard_map/ppermute | solution.py:281
  6.2 1.5 %collective-permute-start.2 = (f32[16,128]{1,0:T(8,128)S(1)}, f32[16,128]{1,0:T(8,128)S(1)}, u32[]{:S(2)}, u32[]{:S(2)}) collective-permute-start(f32[16,128]{1,0:T(8,128)S(1)} %get-tuple-element.18), channel_id=1, source_target_pairs={{0,4},{1,5},{2,6},{3,7},{4,0},{5,1},{6,2},{7,3},{8,12},{9,13},{10,... | collective-permute-start | bytes 24584 | tf_op jit(solution)/shard_map/ppermute | solution.py:281
  7.7 1.0 %collective-permute-start.3 = (f32[8,256]{1,0:T(8,128)S(1)}, f32[8,256]{1,0:T(8,128)S(1)}, u32[]{:S(2)}, u32[]{:S(2)}) collective-permute-start(f32[8,256]{1,0:T(8,128)S(1)} %get-tuple-element.19), channel_id=1, source_target_pairs={{0,8},{1,9},{2,10},{3,11},{4,12},{5,13},{6,14},{7,15},{8,0},{9,1},... | collective-permute-start | bytes 24584 | tf_op jit(solution)/shard_map/ppermute | solution.py:281
  8.7 0.0 copy-done.1
  8.7 0.0 copy-done.2
  8.7 0.0 copy-done.3
  8.7 1.1 %weights.1 = (f32[3,8,64,256]{3,2,1,0:T(8,128)S(1)}, f32[64,256]{1,0:T(8,128)S(1)}, f32[16,256]{1,0:T(8,128)S(1)}) custom-call(s32[1,1,4]{2,1,0:T(1,128)S(1)} %copy-done.3, f32[8,64,256]{2,1,0:T(8,128)S(1)} %copy-done, s32[8,64,256]{2,1,0:T(8,128)S(1)} %copy-done.1, bf16[3,256]{1,0:T(4,128)(2,1)S(1)} %copy-done.2, bf16[256]{0:T(256)(128)(2,1)S(1)} %copy-done.4), custom_call_target="tpu_custom_call" | custom-call | tf_op jit(solution)/shard_map/weights/pallas_call | solution.py:320
  9.8 0.1 collective-permute-done.2.refs_2_
  9.9 0.0 collective-permute-done.3.refs_3_
  9.9 0.0 collective-permute-done.4.refs_4_
  9.9 0.0 collective-permute-done.1.refs_1_
  9.9 0.0 collective-permute-done.refs_0_
  9.9 0.2 %shade.4 = f32[4,16,256]{2,1,0:T(8,128)S(1)} custom-call(f32[8,64,256]{2,1,0:T(8,128)S(1)} %copy-done, f32[3,8,64,256]{3,2,1,0:T(8,128)S(1)} %get-tuple-element.14.weighted, f32[64,256]{1,0:T(8,128)S(1)} %get-tuple-element.15.depth_in, f32[72,256]{1,0:T(8,128)S(1)} %collective-permute-done.refs_0_, f32[64,256]{1,0:T(8,128)S(1)} %collective-permute-done.1.refs_1_, ...), custom_call_target="tpu_custom_call" | custom-call | tf_op jit(solution)/shard_map/shade/pallas_call | solution.py:326
  10.1 0.4 %collective-permute-start.5 = (f32[4,16,256]{2,1,0:T(8,128)S(1)}, f32[4,16,256]{2,1,0:T(8,128)S(1)}, u32[]{:S(2)}, u32[]{:S(2)}) collective-permute-start(f32[4,16,256]{2,1,0:T(8,128)S(1)} %shade.4), channel_id=1, source_target_pairs={{0,1},{1,2},{2,3},{3,0},{4,5},{5,6},{6,7},{7,4},{8,10},{9,11},{10,... | collective-permute-start | bytes 196616 | tf_op jit(solution)/shard_map/ppermute | solution.py:336
  10.5 0.2 %shade.5 = f32[4,16,256]{2,1,0:T(8,128)S(1)} custom-call(f32[8,64,256]{2,1,0:T(8,128)S(1)} %copy-done, f32[3,8,64,256]{3,2,1,0:T(8,128)S(1)} %get-tuple-element.14.weighted, f32[64,256]{1,0:T(8,128)S(1)} %get-tuple-element.15.depth_in, f32[72,256]{1,0:T(8,128)S(1)} %collective-permute-done.refs_0_, f32[64,256]{1,0:T(8,128)S(1)} %collective-permute-done.1.refs_1_, ...), custom_call_target="tpu_custom_call" | custom-call | tf_op jit(solution)/shard_map/shade/pallas_call | solution.py:326
  10.8 2.0 %collective-permute-start.6 = (f32[4,16,256]{2,1,0:T(8,128)S(1)}, f32[4,16,256]{2,1,0:T(8,128)S(1)}, u32[]{:S(2)}, u32[]{:S(2)}) collective-permute-start(f32[4,16,256]{2,1,0:T(8,128)S(1)} %shade.5), channel_id=1, source_target_pairs={{0,2},{1,3},{2,0},{3,1},{4,6},{5,7},{6,4},{7,5},{8,11},{9,8},{10,9... | collective-permute-start | bytes 196616 | tf_op jit(solution)/shard_map/ppermute | solution.py:336
  12.7 0.2 %shade.6 = f32[4,16,256]{2,1,0:T(8,128)S(1)} custom-call(f32[8,64,256]{2,1,0:T(8,128)S(1)} %copy-done, f32[3,8,64,256]{3,2,1,0:T(8,128)S(1)} %get-tuple-element.14.weighted, f32[64,256]{1,0:T(8,128)S(1)} %get-tuple-element.15.depth_in, f32[72,256]{1,0:T(8,128)S(1)} %collective-permute-done.refs_0_, f32[64,256]{1,0:T(8,128)S(1)} %collective-permute-done.1.refs_1_, ...), custom_call_target="tpu_custom_call" | custom-call | tf_op jit(solution)/shard_map/shade/pallas_call | solution.py:326
  13.0 2.7 %collective-permute-start.7 = (f32[4,16,256]{2,1,0:T(8,128)S(1)}, f32[4,16,256]{2,1,0:T(8,128)S(1)}, u32[]{:S(2)}, u32[]{:S(2)}) collective-permute-start(f32[4,16,256]{2,1,0:T(8,128)S(1)} %shade.6), channel_id=1, source_target_pairs={{0,3},{1,0},{2,1},{3,2},{4,7},{5,4},{6,5},{7,6},{8,9},{9,10},{10,1... | collective-permute-start | bytes 196616 | tf_op jit(solution)/shard_map/ppermute | solution.py:336
  15.7 0.2 %shade.7.refs_3_ = f32[4,16,256]{2,1,0:T(8,128)S(1)} custom-call(f32[8,64,256]{2,1,0:T(8,128)S(1)} %copy-done, f32[3,8,64,256]{3,2,1,0:T(8,128)S(1)} %get-tuple-element.14.weighted, f32[64,256]{1,0:T(8,128)S(1)} %get-tuple-element.15.depth_in, f32[72,256]{1,0:T(8,128)S(1)} %collective-permute-done.refs_0_, f32[64,256]{1,0:T(8,128)S(1)} %collective-permute-done.1.refs_1_, ...), custom_call_target="tpu_custom_call" | custom-call | tf_op jit(solution)/shard_map/shade/pallas_call | solution.py:326
  15.9 0.9 %collective-permute-done.5.refs_0_ = f32[4,16,256]{2,1,0:T(8,128)S(1)} collective-permute-done((f32[4,16,256]{2,1,0:T(8,128)S(1)}, f32[4,16,256]{2,1,0:T(8,128)S(1)}, u32[]{:S(2)}, u32[]{:S(2)}) %collective-permute-start.5) | collective-permute-done | bytes 65568 | tf_op jit(solution)/shard_map/ppermute | solution.py:336
  16.8 1.5 %collective-permute-done.6.refs_1_ = f32[4,16,256]{2,1,0:T(8,128)S(1)} collective-permute-done((f32[4,16,256]{2,1,0:T(8,128)S(1)}, f32[4,16,256]{2,1,0:T(8,128)S(1)}, u32[]{:S(2)}, u32[]{:S(2)}) %collective-permute-start.6) | collective-permute-done | bytes 65568 | tf_op jit(solution)/shard_map/ppermute | solution.py:336
  18.2 0.0 collective-permute-done.7.refs_2_
  18.2 0.7 %compose.1 = f32[4,16,256]{2,1,0:T(8,128)} custom-call(f32[16,256]{1,0:T(8,128)S(1)} %get-tuple-element.13.earlier, f32[4,16,256]{2,1,0:T(8,128)S(1)} %collective-permute-done.5.refs_0_, f32[4,16,256]{2,1,0:T(8,128)S(1)} %collective-permute-done.6.refs_1_, f32[4,16,256]{2,1,0:T(8,128)S(1)} %collective-permute-done.7.refs_2_, f32[4,16,256]{2,1,0:T(8,128)S(1)} %shade.7.refs_3_), custom_call_target="tpu_custom_call" | custom-call | tf_op jit(solution)/shard_map/compose/pallas_call | solution.py:342
  (2 shorter events, 0.0 us)
Async XLA Ops:
  0.0 5.6 %copy-start = (f32[8,64,256]{2,1,0:T(8,128)S(1)}, f32[8,64,256]{2,1,0:T(8,128)}, u32[]{:S(2)}) copy-start(f32[8,64,256]{2,1,0:T(8,128)} %density_ref.13) | copy-start | bytes 1572868
  0.9 7.8 %copy-start.1 = (s32[8,64,256]{2,1,0:T(8,128)S(1)}, s32[8,64,256]{2,1,0:T(8,128)}, u32[]{:S(2)}) copy-start(s32[8,64,256]{2,1,0:T(8,128)} %bins_ref.1) | copy-start | bytes 1572868
  0.9 7.8 %copy-start.2 = (bf16[3,256]{1,0:T(4,128)(2,1)S(1)}, bf16[3,256]{1,0:T(4,128)(2,1)}, u32[]{:S(2)}) copy-start(bf16[3,256]{1,0:T(4,128)(2,1)} %colour_ref.1) | copy-start | bytes 4612
  0.9 7.8 %copy-start.3 = (s32[1,1,4]{2,1,0:T(1,128)S(1)}, s32[1,1,4]{2,1,0:T(1,128)}, u32[]{:S(2)}) copy-start(s32[1,1,4]{2,1,0:T(1,128)} %order_ref.1) | copy-start | bytes 52
  0.9 7.8 %copy-start.4 = (bf16[256]{0:T(256)(128)(2,1)S(1)}, bf16[256]{0:T(256)(128)(2,1)}, u32[]{:S(2)}) copy-start(bf16[256]{0:T(256)(128)(2,1)} %opacity_ref.1) | copy-start | bytes 1540
  1.0 8.9 %collective-permute-start.1 = (f32[64,256]{1,0:T(8,128)S(1)}, f32[64,256]{1,0:T(8,128)S(1)}, u32[]{:S(2)}, u32[]{:S(2)}) collective-permute-start(f32[64,256]{1,0:T(8,128)S(1)} %get-tuple-element.17), channel_id=1, source_target_pairs={{0,8},{1,2},{2,1},{3,11},{4,12},{5,6},{6,5},{7,15},{8,0},{9,10},{1... | collective-permute-start | bytes 196616 | tf_op jit(solution)/shard_map/ppermute | solution.py:281
  1.5 8.4 %collective-permute-start = (f32[72,256]{1,0:T(8,128)S(1)}, f32[72,256]{1,0:T(8,128)S(1)}, u32[]{:S(2)}, u32[]{:S(2)}) collective-permute-start(f32[72,256]{1,0:T(8,128)S(1)} %get-tuple-element.16), channel_id=1, source_target_pairs={{0,1},{1,0},{2,3},{3,2},{4,5},{5,4},{6,7},{7,6},{8,9},{9,8},{10,11... | collective-permute-start | bytes 221192 | tf_op jit(solution)/shard_map/ppermute | solution.py:281
  5.8 4.1 %collective-permute-start.4 = (f32[16,256]{1,0:T(8,128)S(1)}, f32[16,256]{1,0:T(8,128)S(1)}, u32[]{:S(2)}, u32[]{:S(2)}) collective-permute-start(f32[16,256]{1,0:T(8,128)S(1)} %get-tuple-element.20), channel_id=1, source_target_pairs={{0,24},{1,25},{2,26},{3,27},{4,28},{5,29},{6,30},{7,31},{8,16},{9,... | collective-permute-start | bytes 49160 | tf_op jit(solution)/shard_map/ppermute | solution.py:281
  6.2 3.7 %collective-permute-start.2 = (f32[16,128]{1,0:T(8,128)S(1)}, f32[16,128]{1,0:T(8,128)S(1)}, u32[]{:S(2)}, u32[]{:S(2)}) collective-permute-start(f32[16,128]{1,0:T(8,128)S(1)} %get-tuple-element.18), channel_id=1, source_target_pairs={{0,4},{1,5},{2,6},{3,7},{4,0},{5,1},{6,2},{7,3},{8,12},{9,13},{10,... | collective-permute-start | bytes 24584 | tf_op jit(solution)/shard_map/ppermute | solution.py:281
  7.7 2.1 %collective-permute-start.3 = (f32[8,256]{1,0:T(8,128)S(1)}, f32[8,256]{1,0:T(8,128)S(1)}, u32[]{:S(2)}, u32[]{:S(2)}) collective-permute-start(f32[8,256]{1,0:T(8,128)S(1)} %get-tuple-element.19), channel_id=1, source_target_pairs={{0,8},{1,9},{2,10},{3,11},{4,12},{5,13},{6,14},{7,15},{8,0},{9,1},... | collective-permute-start | bytes 24584 | tf_op jit(solution)/shard_map/ppermute | solution.py:281
  10.1 6.6 %collective-permute-start.5 = (f32[4,16,256]{2,1,0:T(8,128)S(1)}, f32[4,16,256]{2,1,0:T(8,128)S(1)}, u32[]{:S(2)}, u32[]{:S(2)}) collective-permute-start(f32[4,16,256]{2,1,0:T(8,128)S(1)} %shade.4), channel_id=1, source_target_pairs={{0,1},{1,2},{2,3},{3,0},{4,5},{5,6},{6,7},{7,4},{8,10},{9,11},{10,... | collective-permute-start | bytes 196616 | tf_op jit(solution)/shard_map/ppermute | solution.py:336
  10.8 7.5 %collective-permute-start.6 = (f32[4,16,256]{2,1,0:T(8,128)S(1)}, f32[4,16,256]{2,1,0:T(8,128)S(1)}, u32[]{:S(2)}, u32[]{:S(2)}) collective-permute-start(f32[4,16,256]{2,1,0:T(8,128)S(1)} %shade.5), channel_id=1, source_target_pairs={{0,2},{1,3},{2,0},{3,1},{4,6},{5,7},{6,4},{7,5},{8,11},{9,8},{10,9... | collective-permute-start | bytes 196616 | tf_op jit(solution)/shard_map/ppermute | solution.py:336
  13.0 5.3 %collective-permute-start.7 = (f32[4,16,256]{2,1,0:T(8,128)S(1)}, f32[4,16,256]{2,1,0:T(8,128)S(1)}, u32[]{:S(2)}, u32[]{:S(2)}) collective-permute-start(f32[4,16,256]{2,1,0:T(8,128)S(1)} %shade.6), channel_id=1, source_target_pairs={{0,3},{1,0},{2,1},{3,2},{4,7},{5,4},{6,5},{7,6},{8,9},{9,10},{10,1... | collective-permute-start | bytes 196616 | tf_op jit(solution)/shard_map/ppermute | solution.py:336

commit v8 on v7

--- a/solution.py
+++ b/solution.py
@@ -124,16 +124,13 @@
             earlier[i * bricks + j : i * bricks + j + 1, :] = jnp.broadcast_to(before, (1, rows))
 
     colours = (colour_ref[...].astype(jnp.float32) * 4096.0).astype(jnp.int32)
+    powers = sum((colours >= 256 << i).astype(jnp.int32) for i in range(5))
+    codes = powers * 128 + (jnp.right_shift(colours, powers) - 128)
     opacity = (opacity_ref[...].reshape(1, -1).astype(jnp.float32) * 1024.0).astype(jnp.int32)
-    red_green = colours[0:1] * 8192 + colours[1:2]
-    blue_opacity = colours[2:3] * 8192 + opacity
-
-    def halves(word):
-        return [
-            jnp.broadcast_to(word[:, i : i + LANES], (SUBLANES, LANES)) for i in (0, LANES)
-        ]
-
-    red_green, blue_opacity = halves(red_green), halves(blue_opacity)
+    every = lambda word: jnp.broadcast_to(word, (SUBLANES, LANES))
+    colour_word = codes[0:1] * 1048576 + codes[1:2] * 1024 + codes[2:3]
+    colour_word = [every(colour_word[:, i : i + LANES]) for i in (0, LANES)]
+    opacity_word = every(opacity[:, LANES:] * 4096 + opacity[:, :LANES])
 
     def one_tile(tile, carry):
         here = pl.ds(pl.multiple_of(tile * SUBLANES, SUBLANES), SUBLANES)
@@ -143,13 +140,16 @@
             for z in range(depth):
                 b = bins_ref[z, here, at]
                 index, upper = b & (LANES - 1), b >= LANES
-                rg, bo = look(red_green, index, upper), look(blue_opacity, index, upper)
-                opacity = (bo & 8191).astype(jnp.float32)
+                colour = look(colour_word, index, upper)
+                both = jnp.take_along_axis(opacity_word, index, axis=1, mode="promise_in_bounds")
+                opacity = jnp.where(upper, both >> 12, both & 4095).astype(jnp.float32)
                 total = total + opacity * (density_ref[z, here, at] * step)
                 left = jnp.exp2(-total) * (1.0 / 4096.0)
                 weight = seen - left
                 seen = left
-                for c, entry in enumerate((rg >> 13, rg & 8191, bo >> 13)):
+                for c in range(3):
+                    code = (colour >> (20 - 10 * c)) & 1023
+                    entry = jnp.left_shift((code & 127) + 128, code >> 7)
                     weighted[c, z, here, at] = weight * entry.astype(jnp.float32)
             depth_out[here, at] = total
         return carry

time: 19.1 us -> 19.1 us (level)
  transfers between devices with their start and end apart: 8 -> 8, of which waited for: 3 -> 3; matrix products, arithmetic and copies ran while one was open for 0% -> 0% of each run, Pallas kernels for 10% -> 9%
where the time goes in v8:
time: 19.1 us; the launch traced here: 18.9 us
  starting transfers between devices  12.6 us (66%)
  Pallas kernels  3.58 us (19%)
  waiting for transfers between devices  2.56 us (13%)
    ppermute x5, starting transfers between devices, swap(): got.append(lax.ppermute(value, AXES, pairs))  7.58 us
    ppermute x3, starting transfers between devices, local(): part = lax.ppermute(part, AXES, shifted(shift))  5.06 us
    ppermute x3, waiting for transfers between devices, local(): part = lax.ppermute(part, AXES, shifted(shift))  2.36 us
    pallas_call x1, Pallas kernels, local(): call(functools.partial(weights_kernel, step, shifts), 'weights', [near(3,...  0.96 us
    pallas_call x4, Pallas kernels, local(): call(functools.partial(shade_kernel, part), 'shade', near(4, tile, rows),...  0.91 us
    pallas_call x1, Pallas kernels, local(): call(depth_faces_kernel, 'depth_faces', [near(columns + SUBLANES, rows),...  0.9 us
    pallas_call x1, Pallas kernels, local(): call(functools.partial(compose_kernel, bricks), 'compose', jax.ShapeDtype...  0.67 us
  transfers between devices with their start and end apart: 8, of which 3 were waited for; matrix products, arithmetic and copies ran while one was open for 0% of the time, Pallas kernels for 9%

profile of v8, /device:TPU:0, one launch (start us, length us, event | category | flops | bytes accessed | tf_op | source)
XLA Modules:
  0.0 18.9 jit_solution(13046675840992223908)
XLA Ops:
  0.0 0.9 %depth_faces.1 = (f32[72,256]{1,0:T(8,128)S(1)}, f32[64,256]{1,0:T(8,128)S(1)}) custom-call(f32[8,64,256]{2,1,0:T(8,128)} %density_ref.13), custom_call_target="tpu_custom_call" | custom-call | flops 2000000000 | bytes 2000000 | tf_op jit(solution)/shard_map/depth_faces/pallas_call | solution.py:298
  0.9 0.0 copy-start.1
  0.9 0.0 copy-start.2
  0.9 0.0 copy-start.3
  0.9 0.0 copy-start.4
  1.0 0.5 %collective-permute-start.1 = (f32[64,256]{1,0:T(8,128)S(1)}, f32[64,256]{1,0:T(8,128)S(1)}, u32[]{:S(2)}, u32[]{:S(2)}) collective-permute-start(f32[64,256]{1,0:T(8,128)S(1)} %get-tuple-element.17), channel_id=1, source_target_pairs={{0,8},{1,2},{2,1},{3,11},{4,12},{5,6},{6,5},{7,15},{8,0},{9,10},{1... | collective-permute-start | bytes 196616 | tf_op jit(solution)/shard_map/ppermute | solution.py:281
  1.5 4.1 %collective-permute-start = (f32[72,256]{1,0:T(8,128)S(1)}, f32[72,256]{1,0:T(8,128)S(1)}, u32[]{:S(2)}, u32[]{:S(2)}) collective-permute-start(f32[72,256]{1,0:T(8,128)S(1)} %get-tuple-element.16), channel_id=1, source_target_pairs={{0,1},{1,0},{2,3},{3,2},{4,5},{5,4},{6,7},{7,6},{8,9},{9,8},{10,11... | collective-permute-start | bytes 221192 | tf_op jit(solution)/shard_map/ppermute | solution.py:281
  5.6 0.0 copy-done
  5.6 0.1 side_faces.1
  5.8 0.4 %collective-permute-start.4 = (f32[16,256]{1,0:T(8,128)S(1)}, f32[16,256]{1,0:T(8,128)S(1)}, u32[]{:S(2)}, u32[]{:S(2)}) collective-permute-start(f32[16,256]{1,0:T(8,128)S(1)} %get-tuple-element.20), channel_id=1, source_target_pairs={{0,24},{1,25},{2,26},{3,27},{4,28},{5,29},{6,30},{7,31},{8,16},{9,... | collective-permute-start | bytes 49160 | tf_op jit(solution)/shard_map/ppermute | solution.py:281
  6.2 1.5 %collective-permute-start.2 = (f32[16,128]{1,0:T(8,128)S(1)}, f32[16,128]{1,0:T(8,128)S(1)}, u32[]{:S(2)}, u32[]{:S(2)}) collective-permute-start(f32[16,128]{1,0:T(8,128)S(1)} %get-tuple-element.18), channel_id=1, source_target_pairs={{0,4},{1,5},{2,6},{3,7},{4,0},{5,1},{6,2},{7,3},{8,12},{9,13},{10,... | collective-permute-start | bytes 24584 | tf_op jit(solution)/shard_map/ppermute | solution.py:281
  7.7 1.0 %collective-permute-start.3 = (f32[8,256]{1,0:T(8,128)S(1)}, f32[8,256]{1,0:T(8,128)S(1)}, u32[]{:S(2)}, u32[]{:S(2)}) collective-permute-start(f32[8,256]{1,0:T(8,128)S(1)} %get-tuple-element.19), channel_id=1, source_target_pairs={{0,8},{1,9},{2,10},{3,11},{4,12},{5,13},{6,14},{7,15},{8,0},{9,1},... | collective-permute-start | bytes 24584 | tf_op jit(solution)/shard_map/ppermute | solution.py:281
  8.7 0.0 copy-done.1
  8.7 0.0 copy-done.2
  8.7 0.0 copy-done.3
  8.7 1.0 %weights.1 = (f32[3,8,64,256]{3,2,1,0:T(8,128)S(1)}, f32[64,256]{1,0:T(8,128)S(1)}, f32[16,256]{1,0:T(8,128)S(1)}) custom-call(s32[1,1,4]{2,1,0:T(1,128)S(1)} %copy-done.3, f32[8,64,256]{2,1,0:T(8,128)S(1)} %copy-done, s32[8,64,256]{2,1,0:T(8,128)S(1)} %copy-done.1, bf16[3,256]{1,0:T(4,128)(2,1)S(1)} %copy-done.2, bf16[256]{0:T(256)(128)(2,1)S(1)} %copy-done.4), custom_call_target="tpu_custom_call" | custom-call | tf_op jit(solution)/shard_map/weights/pallas_call | solution.py:320
  9.7 0.2 %collective-permute-done.2.refs_2_ = f32[16,128]{1,0:T(8,128)S(1)} collective-permute-done((f32[16,128]{1,0:T(8,128)S(1)}, f32[16,128]{1,0:T(8,128)S(1)}, u32[]{:S(2)}, u32[]{:S(2)}) %collective-permute-start.2) | collective-permute-done | bytes 8224 | tf_op jit(solution)/shard_map/ppermute | solution.py:281
  9.9 0.0 collective-permute-done.3.refs_3_
  9.9 0.0 collective-permute-done.4.refs_4_
  9.9 0.0 collective-permute-done.1.refs_1_
  9.9 0.0 collective-permute-done.refs_0_
  9.9 0.2 %shade.4 = f32[4,16,256]{2,1,0:T(8,128)S(1)} custom-call(f32[8,64,256]{2,1,0:T(8,128)S(1)} %copy-done, f32[3,8,64,256]{3,2,1,0:T(8,128)S(1)} %get-tuple-element.14.weighted, f32[64,256]{1,0:T(8,128)S(1)} %get-tuple-element.15.depth_in, f32[72,256]{1,0:T(8,128)S(1)} %collective-permute-done.refs_0_, f32[64,256]{1,0:T(8,128)S(1)} %collective-permute-done.1.refs_1_, ...), custom_call_target="tpu_custom_call" | custom-call | tf_op jit(solution)/shard_map/shade/pallas_call | solution.py:326
  10.1 0.4 %collective-permute-start.5 = (f32[4,16,256]{2,1,0:T(8,128)S(1)}, f32[4,16,256]{2,1,0:T(8,128)S(1)}, u32[]{:S(2)}, u32[]{:S(2)}) collective-permute-start(f32[4,16,256]{2,1,0:T(8,128)S(1)} %shade.4), channel_id=1, source_target_pairs={{0,1},{1,2},{2,3},{3,0},{4,5},{5,6},{6,7},{7,4},{8,10},{9,11},{10,... | collective-permute-start | bytes 196616 | tf_op jit(solution)/shard_map/ppermute | solution.py:336
  10.5 0.2 %shade.5 = f32[4,16,256]{2,1,0:T(8,128)S(1)} custom-call(f32[8,64,256]{2,1,0:T(8,128)S(1)} %copy-done, f32[3,8,64,256]{3,2,1,0:T(8,128)S(1)} %get-tuple-element.14.weighted, f32[64,256]{1,0:T(8,128)S(1)} %get-tuple-element.15.depth_in, f32[72,256]{1,0:T(8,128)S(1)} %collective-permute-done.refs_0_, f32[64,256]{1,0:T(8,128)S(1)} %collective-permute-done.1.refs_1_, ...), custom_call_target="tpu_custom_call" | custom-call | tf_op jit(solution)/shard_map/shade/pallas_call | solution.py:326
  10.8 2.0 %collective-permute-start.6 = (f32[4,16,256]{2,1,0:T(8,128)S(1)}, f32[4,16,256]{2,1,0:T(8,128)S(1)}, u32[]{:S(2)}, u32[]{:S(2)}) collective-permute-start(f32[4,16,256]{2,1,0:T(8,128)S(1)} %shade.5), channel_id=1, source_target_pairs={{0,2},{1,3},{2,0},{3,1},{4,6},{5,7},{6,4},{7,5},{8,11},{9,8},{10,9... | collective-permute-start | bytes 196616 | tf_op jit(solution)/shard_map/ppermute | solution.py:336
  12.7 0.2 %shade.6 = f32[4,16,256]{2,1,0:T(8,128)S(1)} custom-call(f32[8,64,256]{2,1,0:T(8,128)S(1)} %copy-done, f32[3,8,64,256]{3,2,1,0:T(8,128)S(1)} %get-tuple-element.14.weighted, f32[64,256]{1,0:T(8,128)S(1)} %get-tuple-element.15.depth_in, f32[72,256]{1,0:T(8,128)S(1)} %collective-permute-done.refs_0_, f32[64,256]{1,0:T(8,128)S(1)} %collective-permute-done.1.refs_1_, ...), custom_call_target="tpu_custom_call" | custom-call | tf_op jit(solution)/shard_map/shade/pallas_call | solution.py:326
  13.0 2.7 %collective-permute-start.7 = (f32[4,16,256]{2,1,0:T(8,128)S(1)}, f32[4,16,256]{2,1,0:T(8,128)S(1)}, u32[]{:S(2)}, u32[]{:S(2)}) collective-permute-start(f32[4,16,256]{2,1,0:T(8,128)S(1)} %shade.6), channel_id=1, source_target_pairs={{0,3},{1,0},{2,1},{3,2},{4,7},{5,4},{6,5},{7,6},{8,9},{9,10},{10,1... | collective-permute-start | bytes 196616 | tf_op jit(solution)/shard_map/ppermute | solution.py:336
  15.7 0.2 %shade.7.refs_3_ = f32[4,16,256]{2,1,0:T(8,128)S(1)} custom-call(f32[8,64,256]{2,1,0:T(8,128)S(1)} %copy-done, f32[3,8,64,256]{3,2,1,0:T(8,128)S(1)} %get-tuple-element.14.weighted, f32[64,256]{1,0:T(8,128)S(1)} %get-tuple-element.15.depth_in, f32[72,256]{1,0:T(8,128)S(1)} %collective-permute-done.refs_0_, f32[64,256]{1,0:T(8,128)S(1)} %collective-permute-done.1.refs_1_, ...), custom_call_target="tpu_custom_call" | custom-call | tf_op jit(solution)/shard_map/shade/pallas_call | solution.py:326
  15.9 0.9 %collective-permute-done.5.refs_0_ = f32[4,16,256]{2,1,0:T(8,128)S(1)} collective-permute-done((f32[4,16,256]{2,1,0:T(8,128)S(1)}, f32[4,16,256]{2,1,0:T(8,128)S(1)}, u32[]{:S(2)}, u32[]{:S(2)}) %collective-permute-start.5) | collective-permute-done | bytes 65568 | tf_op jit(solution)/shard_map/ppermute | solution.py:336
  16.8 1.5 %collective-permute-done.6.refs_1_ = f32[4,16,256]{2,1,0:T(8,128)S(1)} collective-permute-done((f32[4,16,256]{2,1,0:T(8,128)S(1)}, f32[4,16,256]{2,1,0:T(8,128)S(1)}, u32[]{:S(2)}, u32[]{:S(2)}) %collective-permute-start.6) | collective-permute-done | bytes 65568 | tf_op jit(solution)/shard_map/ppermute | solution.py:336
  18.2 0.0 collective-permute-done.7.refs_2_
  18.2 0.7 %compose.1 = f32[4,16,256]{2,1,0:T(8,128)} custom-call(f32[16,256]{1,0:T(8,128)S(1)} %get-tuple-element.13.earlier, f32[4,16,256]{2,1,0:T(8,128)S(1)} %collective-permute-done.5.refs_0_, f32[4,16,256]{2,1,0:T(8,128)S(1)} %collective-permute-done.6.refs_1_, f32[4,16,256]{2,1,0:T(8,128)S(1)} %collective-permute-done.7.refs_2_, f32[4,16,256]{2,1,0:T(8,128)S(1)} %shade.7.refs_3_), custom_call_target="tpu_custom_call" | custom-call | tf_op jit(solution)/shard_map/compose/pallas_call | solution.py:342
  (2 shorter events, 0.0 us)
Async XLA Ops:
  0.0 5.6 %copy-start = (f32[8,64,256]{2,1,0:T(8,128)S(1)}, f32[8,64,256]{2,1,0:T(8,128)}, u32[]{:S(2)}) copy-start(f32[8,64,256]{2,1,0:T(8,128)} %density_ref.13) | copy-start | bytes 1572868
  0.9 7.8 %copy-start.1 = (s32[8,64,256]{2,1,0:T(8,128)S(1)}, s32[8,64,256]{2,1,0:T(8,128)}, u32[]{:S(2)}) copy-start(s32[8,64,256]{2,1,0:T(8,128)} %bins_ref.1) | copy-start | bytes 1572868
  0.9 7.8 %copy-start.2 = (bf16[3,256]{1,0:T(4,128)(2,1)S(1)}, bf16[3,256]{1,0:T(4,128)(2,1)}, u32[]{:S(2)}) copy-start(bf16[3,256]{1,0:T(4,128)(2,1)} %colour_ref.1) | copy-start | bytes 4612
  0.9 7.8 %copy-start.3 = (s32[1,1,4]{2,1,0:T(1,128)S(1)}, s32[1,1,4]{2,1,0:T(1,128)}, u32[]{:S(2)}) copy-start(s32[1,1,4]{2,1,0:T(1,128)} %order_ref.1) | copy-start | bytes 52
  0.9 7.8 %copy-start.4 = (bf16[256]{0:T(256)(128)(2,1)S(1)}, bf16[256]{0:T(256)(128)(2,1)}, u32[]{:S(2)}) copy-start(bf16[256]{0:T(256)(128)(2,1)} %opacity_ref.1) | copy-start | bytes 1540
  1.0 8.9 %collective-permute-start.1 = (f32[64,256]{1,0:T(8,128)S(1)}, f32[64,256]{1,0:T(8,128)S(1)}, u32[]{:S(2)}, u32[]{:S(2)}) collective-permute-start(f32[64,256]{1,0:T(8,128)S(1)} %get-tuple-element.17), channel_id=1, source_target_pairs={{0,8},{1,2},{2,1},{3,11},{4,12},{5,6},{6,5},{7,15},{8,0},{9,10},{1... | collective-permute-start | bytes 196616 | tf_op jit(solution)/shard_map/ppermute | solution.py:281
  1.5 8.4 %collective-permute-start = (f32[72,256]{1,0:T(8,128)S(1)}, f32[72,256]{1,0:T(8,128)S(1)}, u32[]{:S(2)}, u32[]{:S(2)}) collective-permute-start(f32[72,256]{1,0:T(8,128)S(1)} %get-tuple-element.16), channel_id=1, source_target_pairs={{0,1},{1,0},{2,3},{3,2},{4,5},{5,4},{6,7},{7,6},{8,9},{9,8},{10,11... | collective-permute-start | bytes 221192 | tf_op jit(solution)/shard_map/ppermute | solution.py:281
  5.8 4.1 %collective-permute-start.4 = (f32[16,256]{1,0:T(8,128)S(1)}, f32[16,256]{1,0:T(8,128)S(1)}, u32[]{:S(2)}, u32[]{:S(2)}) collective-permute-start(f32[16,256]{1,0:T(8,128)S(1)} %get-tuple-element.20), channel_id=1, source_target_pairs={{0,24},{1,25},{2,26},{3,27},{4,28},{5,29},{6,30},{7,31},{8,16},{9,... | collective-permute-start | bytes 49160 | tf_op jit(solution)/shard_map/ppermute | solution.py:281
  6.2 3.7 %collective-permute-start.2 = (f32[16,128]{1,0:T(8,128)S(1)}, f32[16,128]{1,0:T(8,128)S(1)}, u32[]{:S(2)}, u32[]{:S(2)}) collective-permute-start(f32[16,128]{1,0:T(8,128)S(1)} %get-tuple-element.18), channel_id=1, source_target_pairs={{0,4},{1,5},{2,6},{3,7},{4,0},{5,1},{6,2},{7,3},{8,12},{9,13},{10,... | collective-permute-start | bytes 24584 | tf_op jit(solution)/shard_map/ppermute | solution.py:281
  7.7 2.1 %collective-permute-start.3 = (f32[8,256]{1,0:T(8,128)S(1)}, f32[8,256]{1,0:T(8,128)S(1)}, u32[]{:S(2)}, u32[]{:S(2)}) collective-permute-start(f32[8,256]{1,0:T(8,128)S(1)} %get-tuple-element.19), channel_id=1, source_target_pairs={{0,8},{1,9},{2,10},{3,11},{4,12},{5,13},{6,14},{7,15},{8,0},{9,1},... | collective-permute-start | bytes 24584 | tf_op jit(solution)/shard_map/ppermute | solution.py:281
  10.1 6.6 %collective-permute-start.5 = (f32[4,16,256]{2,1,0:T(8,128)S(1)}, f32[4,16,256]{2,1,0:T(8,128)S(1)}, u32[]{:S(2)}, u32[]{:S(2)}) collective-permute-start(f32[4,16,256]{2,1,0:T(8,128)S(1)} %shade.4), channel_id=1, source_target_pairs={{0,1},{1,2},{2,3},{3,0},{4,5},{5,6},{6,7},{7,4},{8,10},{9,11},{10,... | collective-permute-start | bytes 196616 | tf_op jit(solution)/shard_map/ppermute | solution.py:336
  10.8 7.5 %collective-permute-start.6 = (f32[4,16,256]{2,1,0:T(8,128)S(1)}, f32[4,16,256]{2,1,0:T(8,128)S(1)}, u32[]{:S(2)}, u32[]{:S(2)}) collective-permute-start(f32[4,16,256]{2,1,0:T(8,128)S(1)} %shade.5), channel_id=1, source_target_pairs={{0,2},{1,3},{2,0},{3,1},{4,6},{5,7},{6,4},{7,5},{8,11},{9,8},{10,9... | collective-permute-start | bytes 196616 | tf_op jit(solution)/shard_map/ppermute | solution.py:336
  13.0 5.3 %collective-permute-start.7 = (f32[4,16,256]{2,1,0:T(8,128)S(1)}, f32[4,16,256]{2,1,0:T(8,128)S(1)}, u32[]{:S(2)}, u32[]{:S(2)}) collective-permute-start(f32[4,16,256]{2,1,0:T(8,128)S(1)} %shade.6), channel_id=1, source_target_pairs={{0,3},{1,0},{2,1},{3,2},{4,7},{5,4},{6,5},{7,6},{8,9},{9,10},{10,1... | collective-permute-start | bytes 196616 | tf_op jit(solution)/shard_map/ppermute | solution.py:336

commit v9 on v8

--- a/solution.py
+++ b/solution.py
@@ -71,6 +71,7 @@
     for out in (x_a, x_b, y_a, *y_b):
         out[...] = jnp.zeros_like(out)
     lane = lax.broadcasted_iota(jnp.int32, (SUBLANES, LANES), 1) - odd_y
+    starts = [jnp.where(even_y, rows - LANES, 0), jnp.where(even_y, 0, rows - LANES)]
     faces = {}
     for z in range(depth):
         first, last = density_ref[z, 0:1, :], density_ref[z, columns - 1 : columns, :]
@@ -78,10 +79,9 @@
         x_b[z : z + 1, :] = jnp.where(even_x, first, last)
         for tile in range(columns // SUBLANES):
             here = slice(tile * SUBLANES, (tile + 1) * SUBLANES)
-            first, last = density_ref[z, here, :LANES], density_ref[z, here, rows - LANES :]
             to, at = y_place(depth, tile)
-            for out, near_, far_ in ((y_a, last, first), *((y, first, last) for y in y_b)):
-                edge = jnp.where(even_y, near_, far_)
+            for out, start in zip((y_a, *y_b), starts):
+                edge = density_ref[z, here, pl.ds(pl.multiple_of(start, LANES), LANES)]
                 if out is not y_a:
                     edge = pltpu.roll(edge, jnp.where(even_y, LANES - 1, 1), 1)
                 key = (to, out is y_a)

time: 19.1 us -> 19 us (level)
  no operation moved by 1% of the time
where the time goes in v9:
time: 19 us; the launch traced here: 18.9 us
  starting transfers between devices  12.6 us (66%)
  Pallas kernels  3.57 us (19%)
  waiting for transfers between devices  2.56 us (13%)
    ppermute x5, starting transfers between devices, swap(): got.append(lax.ppermute(value, AXES, pairs))  7.58 us
    ppermute x3, starting transfers between devices, local(): part = lax.ppermute(part, AXES, shifted(shift))  5.06 us
    ppermute x3, waiting for transfers between devices, local(): part = lax.ppermute(part, AXES, shifted(shift))  2.36 us
    pallas_call x1, Pallas kernels, local(): call(functools.partial(weights_kernel, step, shifts), 'weights', [near(3,...  0.96 us
    pallas_call x4, Pallas kernels, local(): call(functools.partial(shade_kernel, part), 'shade', near(4, tile, rows),...  0.91 us
    pallas_call x1, Pallas kernels, local(): call(depth_faces_kernel, 'depth_faces', [near(columns + SUBLANES, rows),...  0.9 us
    pallas_call x1, Pallas kernels, local(): call(functools.partial(compose_kernel, bricks), 'compose', jax.ShapeDtype...  0.67 us
  transfers between devices with their start and end apart: 8, of which 3 were waited for; matrix products, arithmetic and copies ran while one was open for 0% of the time, Pallas kernels for 9%

profile of v9, /device:TPU:0, one launch (start us, length us, event | category | flops | bytes accessed | tf_op | source)
XLA Modules:
  0.0 18.9 jit_solution(571319946368895364)
XLA Ops:
  0.0 0.9 %depth_faces.1 = (f32[72,256]{1,0:T(8,128)S(1)}, f32[64,256]{1,0:T(8,128)S(1)}) custom-call(f32[8,64,256]{2,1,0:T(8,128)} %density_ref.13), custom_call_target="tpu_custom_call" | custom-call | flops 2000000000 | bytes 2000000 | tf_op jit(solution)/shard_map/depth_faces/pallas_call | solution.py:298
  0.9 0.0 copy-start.1
  0.9 0.0 copy-start.2
  0.9 0.0 copy-start.3
  0.9 0.0 copy-start.4
  1.0 0.5 %collective-permute-start.1 = (f32[64,256]{1,0:T(8,128)S(1)}, f32[64,256]{1,0:T(8,128)S(1)}, u32[]{:S(2)}, u32[]{:S(2)}) collective-permute-start(f32[64,256]{1,0:T(8,128)S(1)} %get-tuple-element.17), channel_id=1, source_target_pairs={{0,8},{1,2},{2,1},{3,11},{4,12},{5,6},{6,5},{7,15},{8,0},{9,10},{1... | collective-permute-start | bytes 196616 | tf_op jit(solution)/shard_map/ppermute | solution.py:281
  1.5 4.1 %collective-permute-start = (f32[72,256]{1,0:T(8,128)S(1)}, f32[72,256]{1,0:T(8,128)S(1)}, u32[]{:S(2)}, u32[]{:S(2)}) collective-permute-start(f32[72,256]{1,0:T(8,128)S(1)} %get-tuple-element.16), channel_id=1, source_target_pairs={{0,1},{1,0},{2,3},{3,2},{4,5},{5,4},{6,7},{7,6},{8,9},{9,8},{10,11... | collective-permute-start | bytes 221192 | tf_op jit(solution)/shard_map/ppermute | solution.py:281
  5.6 0.0 copy-done
  5.6 0.1 side_faces.1
  5.8 0.4 %collective-permute-start.4 = (f32[16,256]{1,0:T(8,128)S(1)}, f32[16,256]{1,0:T(8,128)S(1)}, u32[]{:S(2)}, u32[]{:S(2)}) collective-permute-start(f32[16,256]{1,0:T(8,128)S(1)} %get-tuple-element.20), channel_id=1, source_target_pairs={{0,24},{1,25},{2,26},{3,27},{4,28},{5,29},{6,30},{7,31},{8,16},{9,... | collective-permute-start | bytes 49160 | tf_op jit(solution)/shard_map/ppermute | solution.py:281
  6.2 1.5 %collective-permute-start.2 = (f32[16,128]{1,0:T(8,128)S(1)}, f32[16,128]{1,0:T(8,128)S(1)}, u32[]{:S(2)}, u32[]{:S(2)}) collective-permute-start(f32[16,128]{1,0:T(8,128)S(1)} %get-tuple-element.18), channel_id=1, source_target_pairs={{0,4},{1,5},{2,6},{3,7},{4,0},{5,1},{6,2},{7,3},{8,12},{9,13},{10,... | collective-permute-start | bytes 24584 | tf_op jit(solution)/shard_map/ppermute | solution.py:281
  7.7 1.0 %collective-permute-start.3 = (f32[8,256]{1,0:T(8,128)S(1)}, f32[8,256]{1,0:T(8,128)S(1)}, u32[]{:S(2)}, u32[]{:S(2)}) collective-permute-start(f32[8,256]{1,0:T(8,128)S(1)} %get-tuple-element.19), channel_id=1, source_target_pairs={{0,8},{1,9},{2,10},{3,11},{4,12},{5,13},{6,14},{7,15},{8,0},{9,1},... | collective-permute-start | bytes 24584 | tf_op jit(solution)/shard_map/ppermute | solution.py:281
  8.7 0.0 copy-done.1
  8.7 0.0 copy-done.2
  8.7 0.0 copy-done.3
  8.7 1.0 %weights.1 = (f32[3,8,64,256]{3,2,1,0:T(8,128)S(1)}, f32[64,256]{1,0:T(8,128)S(1)}, f32[16,256]{1,0:T(8,128)S(1)}) custom-call(s32[1,1,4]{2,1,0:T(1,128)S(1)} %copy-done.3, f32[8,64,256]{2,1,0:T(8,128)S(1)} %copy-done, s32[8,64,256]{2,1,0:T(8,128)S(1)} %copy-done.1, bf16[3,256]{1,0:T(4,128)(2,1)S(1)} %copy-done.2, bf16[256]{0:T(256)(128)(2,1)S(1)} %copy-done.4), custom_call_target="tpu_custom_call" | custom-call | tf_op jit(solution)/shard_map/weights/pallas_call | solution.py:320
  9.7 0.2 %collective-permute-done.2.refs_2_ = f32[16,128]{1,0:T(8,128)S(1)} collective-permute-done((f32[16,128]{1,0:T(8,128)S(1)}, f32[16,128]{1,0:T(8,128)S(1)}, u32[]{:S(2)}, u32[]{:S(2)}) %collective-permute-start.2) | collective-permute-done | bytes 8224 | tf_op jit(solution)/shard_map/ppermute | solution.py:281
  9.9 0.0 collective-permute-done.3.refs_3_
  9.9 0.0 collective-permute-done.4.refs_4_
  9.9 0.0 collective-permute-done.1.refs_1_
  9.9 0.0 collective-permute-done.refs_0_
  9.9 0.2 %shade.4 = f32[4,16,256]{2,1,0:T(8,128)S(1)} custom-call(f32[8,64,256]{2,1,0:T(8,128)S(1)} %copy-done, f32[3,8,64,256]{3,2,1,0:T(8,128)S(1)} %get-tuple-element.14.weighted, f32[64,256]{1,0:T(8,128)S(1)} %get-tuple-element.15.depth_in, f32[72,256]{1,0:T(8,128)S(1)} %collective-permute-done.refs_0_, f32[64,256]{1,0:T(8,128)S(1)} %collective-permute-done.1.refs_1_, ...), custom_call_target="tpu_custom_call" | custom-call | tf_op jit(solution)/shard_map/shade/pallas_call | solution.py:326
  10.1 0.4 %collective-permute-start.5 = (f32[4,16,256]{2,1,0:T(8,128)S(1)}, f32[4,16,256]{2,1,0:T(8,128)S(1)}, u32[]{:S(2)}, u32[]{:S(2)}) collective-permute-start(f32[4,16,256]{2,1,0:T(8,128)S(1)} %shade.4), channel_id=1, source_target_pairs={{0,1},{1,2},{2,3},{3,0},{4,5},{5,6},{6,7},{7,4},{8,10},{9,11},{10,... | collective-permute-start | bytes 196616 | tf_op jit(solution)/shard_map/ppermute | solution.py:336
  10.5 0.2 %shade.5 = f32[4,16,256]{2,1,0:T(8,128)S(1)} custom-call(f32[8,64,256]{2,1,0:T(8,128)S(1)} %copy-done, f32[3,8,64,256]{3,2,1,0:T(8,128)S(1)} %get-tuple-element.14.weighted, f32[64,256]{1,0:T(8,128)S(1)} %get-tuple-element.15.depth_in, f32[72,256]{1,0:T(8,128)S(1)} %collective-permute-done.refs_0_, f32[64,256]{1,0:T(8,128)S(1)} %collective-permute-done.1.refs_1_, ...), custom_call_target="tpu_custom_call" | custom-call | tf_op jit(solution)/shard_map/shade/pallas_call | solution.py:326
  10.8 2.0 %collective-permute-start.6 = (f32[4,16,256]{2,1,0:T(8,128)S(1)}, f32[4,16,256]{2,1,0:T(8,128)S(1)}, u32[]{:S(2)}, u32[]{:S(2)}) collective-permute-start(f32[4,16,256]{2,1,0:T(8,128)S(1)} %shade.5), channel_id=1, source_target_pairs={{0,2},{1,3},{2,0},{3,1},{4,6},{5,7},{6,4},{7,5},{8,11},{9,8},{10,9... | collective-permute-start | bytes 196616 | tf_op jit(solution)/shard_map/ppermute | solution.py:336
  12.7 0.2 %shade.6 = f32[4,16,256]{2,1,0:T(8,128)S(1)} custom-call(f32[8,64,256]{2,1,0:T(8,128)S(1)} %copy-done, f32[3,8,64,256]{3,2,1,0:T(8,128)S(1)} %get-tuple-element.14.weighted, f32[64,256]{1,0:T(8,128)S(1)} %get-tuple-element.15.depth_in, f32[72,256]{1,0:T(8,128)S(1)} %collective-permute-done.refs_0_, f32[64,256]{1,0:T(8,128)S(1)} %collective-permute-done.1.refs_1_, ...), custom_call_target="tpu_custom_call" | custom-call | tf_op jit(solution)/shard_map/shade/pallas_call | solution.py:326
  12.9 2.7 %collective-permute-start.7 = (f32[4,16,256]{2,1,0:T(8,128)S(1)}, f32[4,16,256]{2,1,0:T(8,128)S(1)}, u32[]{:S(2)}, u32[]{:S(2)}) collective-permute-start(f32[4,16,256]{2,1,0:T(8,128)S(1)} %shade.6), channel_id=1, source_target_pairs={{0,3},{1,0},{2,1},{3,2},{4,7},{5,4},{6,5},{7,6},{8,9},{9,10},{10,1... | collective-permute-start | bytes 196616 | tf_op jit(solution)/shard_map/ppermute | solution.py:336
  15.6 0.2 %shade.7.refs_3_ = f32[4,16,256]{2,1,0:T(8,128)S(1)} custom-call(f32[8,64,256]{2,1,0:T(8,128)S(1)} %copy-done, f32[3,8,64,256]{3,2,1,0:T(8,128)S(1)} %get-tuple-element.14.weighted, f32[64,256]{1,0:T(8,128)S(1)} %get-tuple-element.15.depth_in, f32[72,256]{1,0:T(8,128)S(1)} %collective-permute-done.refs_0_, f32[64,256]{1,0:T(8,128)S(1)} %collective-permute-done.1.refs_1_, ...), custom_call_target="tpu_custom_call" | custom-call | tf_op jit(solution)/shard_map/shade/pallas_call | solution.py:326
  15.9 0.9 %collective-permute-done.5.refs_0_ = f32[4,16,256]{2,1,0:T(8,128)S(1)} collective-permute-done((f32[4,16,256]{2,1,0:T(8,128)S(1)}, f32[4,16,256]{2,1,0:T(8,128)S(1)}, u32[]{:S(2)}, u32[]{:S(2)}) %collective-permute-start.5) | collective-permute-done | bytes 65568 | tf_op jit(solution)/shard_map/ppermute | solution.py:336
  16.8 1.5 %collective-permute-done.6.refs_1_ = f32[4,16,256]{2,1,0:T(8,128)S(1)} collective-permute-done((f32[4,16,256]{2,1,0:T(8,128)S(1)}, f32[4,16,256]{2,1,0:T(8,128)S(1)}, u32[]{:S(2)}, u32[]{:S(2)}) %collective-permute-start.6) | collective-permute-done | bytes 65568 | tf_op jit(solution)/shard_map/ppermute | solution.py:336
  18.2 0.0 collective-permute-done.7.refs_2_
  18.2 0.7 %compose.1 = f32[4,16,256]{2,1,0:T(8,128)} custom-call(f32[16,256]{1,0:T(8,128)S(1)} %get-tuple-element.13.earlier, f32[4,16,256]{2,1,0:T(8,128)S(1)} %collective-permute-done.5.refs_0_, f32[4,16,256]{2,1,0:T(8,128)S(1)} %collective-permute-done.6.refs_1_, f32[4,16,256]{2,1,0:T(8,128)S(1)} %collective-permute-done.7.refs_2_, f32[4,16,256]{2,1,0:T(8,128)S(1)} %shade.7.refs_3_), custom_call_target="tpu_custom_call" | custom-call | tf_op jit(solution)/shard_map/compose/pallas_call | solution.py:342
  (2 shorter events, 0.0 us)
Async XLA Ops:
  0.0 5.6 %copy-start = (f32[8,64,256]{2,1,0:T(8,128)S(1)}, f32[8,64,256]{2,1,0:T(8,128)}, u32[]{:S(2)}) copy-start(f32[8,64,256]{2,1,0:T(8,128)} %density_ref.13) | copy-start | bytes 1572868
  0.9 7.8 %copy-start.1 = (s32[8,64,256]{2,1,0:T(8,128)S(1)}, s32[8,64,256]{2,1,0:T(8,128)}, u32[]{:S(2)}) copy-start(s32[8,64,256]{2,1,0:T(8,128)} %bins_ref.1) | copy-start | bytes 1572868
  0.9 7.8 %copy-start.2 = (bf16[3,256]{1,0:T(4,128)(2,1)S(1)}, bf16[3,256]{1,0:T(4,128)(2,1)}, u32[]{:S(2)}) copy-start(bf16[3,256]{1,0:T(4,128)(2,1)} %colour_ref.1) | copy-start | bytes 4612
  0.9 7.8 %copy-start.3 = (s32[1,1,4]{2,1,0:T(1,128)S(1)}, s32[1,1,4]{2,1,0:T(1,128)}, u32[]{:S(2)}) copy-start(s32[1,1,4]{2,1,0:T(1,128)} %order_ref.1) | copy-start | bytes 52
  0.9 7.7 %copy-start.4 = (bf16[256]{0:T(256)(128)(2,1)S(1)}, bf16[256]{0:T(256)(128)(2,1)}, u32[]{:S(2)}) copy-start(bf16[256]{0:T(256)(128)(2,1)} %opacity_ref.1) | copy-start | bytes 1540
  1.0 8.9 %collective-permute-start.1 = (f32[64,256]{1,0:T(8,128)S(1)}, f32[64,256]{1,0:T(8,128)S(1)}, u32[]{:S(2)}, u32[]{:S(2)}) collective-permute-start(f32[64,256]{1,0:T(8,128)S(1)} %get-tuple-element.17), channel_id=1, source_target_pairs={{0,8},{1,2},{2,1},{3,11},{4,12},{5,6},{6,5},{7,15},{8,0},{9,10},{1... | collective-permute-start | bytes 196616 | tf_op jit(solution)/shard_map/ppermute | solution.py:281
  1.5 8.4 %collective-permute-start = (f32[72,256]{1,0:T(8,128)S(1)}, f32[72,256]{1,0:T(8,128)S(1)}, u32[]{:S(2)}, u32[]{:S(2)}) collective-permute-start(f32[72,256]{1,0:T(8,128)S(1)} %get-tuple-element.16), channel_id=1, source_target_pairs={{0,1},{1,0},{2,3},{3,2},{4,5},{5,4},{6,7},{7,6},{8,9},{9,8},{10,11... | collective-permute-start | bytes 221192 | tf_op jit(solution)/shard_map/ppermute | solution.py:281
  5.8 4.1 %collective-permute-start.4 = (f32[16,256]{1,0:T(8,128)S(1)}, f32[16,256]{1,0:T(8,128)S(1)}, u32[]{:S(2)}, u32[]{:S(2)}) collective-permute-start(f32[16,256]{1,0:T(8,128)S(1)} %get-tuple-element.20), channel_id=1, source_target_pairs={{0,24},{1,25},{2,26},{3,27},{4,28},{5,29},{6,30},{7,31},{8,16},{9,... | collective-permute-start | bytes 49160 | tf_op jit(solution)/shard_map/ppermute | solution.py:281
  6.2 3.7 %collective-permute-start.2 = (f32[16,128]{1,0:T(8,128)S(1)}, f32[16,128]{1,0:T(8,128)S(1)}, u32[]{:S(2)}, u32[]{:S(2)}) collective-permute-start(f32[16,128]{1,0:T(8,128)S(1)} %get-tuple-element.18), channel_id=1, source_target_pairs={{0,4},{1,5},{2,6},{3,7},{4,0},{5,1},{6,2},{7,3},{8,12},{9,13},{10,... | collective-permute-start | bytes 24584 | tf_op jit(solution)/shard_map/ppermute | solution.py:281
  7.7 2.1 %collective-permute-start.3 = (f32[8,256]{1,0:T(8,128)S(1)}, f32[8,256]{1,0:T(8,128)S(1)}, u32[]{:S(2)}, u32[]{:S(2)}) collective-permute-start(f32[8,256]{1,0:T(8,128)S(1)} %get-tuple-element.19), channel_id=1, source_target_pairs={{0,8},{1,9},{2,10},{3,11},{4,12},{5,13},{6,14},{7,15},{8,0},{9,1},... | collective-permute-start | bytes 24584 | tf_op jit(solution)/shard_map/ppermute | solution.py:281
  10.1 6.6 %collective-permute-start.5 = (f32[4,16,256]{2,1,0:T(8,128)S(1)}, f32[4,16,256]{2,1,0:T(8,128)S(1)}, u32[]{:S(2)}, u32[]{:S(2)}) collective-permute-start(f32[4,16,256]{2,1,0:T(8,128)S(1)} %shade.4), channel_id=1, source_target_pairs={{0,1},{1,2},{2,3},{3,0},{4,5},{5,6},{6,7},{7,4},{8,10},{9,11},{10,... | collective-permute-start | bytes 196616 | tf_op jit(solution)/shard_map/ppermute | solution.py:336
  10.8 7.5 %collective-permute-start.6 = (f32[4,16,256]{2,1,0:T(8,128)S(1)}, f32[4,16,256]{2,1,0:T(8,128)S(1)}, u32[]{:S(2)}, u32[]{:S(2)}) collective-permute-start(f32[4,16,256]{2,1,0:T(8,128)S(1)} %shade.5), channel_id=1, source_target_pairs={{0,2},{1,3},{2,0},{3,1},{4,6},{5,7},{6,4},{7,5},{8,11},{9,8},{10,9... | collective-permute-start | bytes 196616 | tf_op jit(solution)/shard_map/ppermute | solution.py:336
  12.9 5.3 %collective-permute-start.7 = (f32[4,16,256]{2,1,0:T(8,128)S(1)}, f32[4,16,256]{2,1,0:T(8,128)S(1)}, u32[]{:S(2)}, u32[]{:S(2)}) collective-permute-start(f32[4,16,256]{2,1,0:T(8,128)S(1)} %shade.6), channel_id=1, source_target_pairs={{0,3},{1,0},{2,1},{3,2},{4,7},{5,4},{6,5},{7,6},{8,9},{9,10},{10,1... | collective-permute-start | bytes 196616 | tf_op jit(solution)/shard_map/ppermute | solution.py:336
